TPU v7x, 1024 devices: a whole 8x8x8 slice. The times are simulated.
1024 devices in a mesh: expert: 32 (over x, y_hi), mp: 8 (over z), dp: 4 (over y_lo, core).
Axes of the slice: x: 8, y: 8 (y_hi: 4, y_lo: 2; y = y_hi * 2 + y_lo), z: 8, core: 2. Of those that a mesh axis runs over, the one named last changes fastest.
Arguments:
- grad_out: bfloat16 [32768, 2048], P(('expert', 'dp')), may hold values from -1.5 to 1.5
- tokens: bfloat16 [32768, 2048], P(('expert', 'dp')), may hold values from -6 to 6
- gate: bfloat16 [32768], P(('expert', 'dp')), may hold values from 0.19921875 to 1
- expert_index: int32 [32768], P(('expert', 'dp')), may hold values from 0 to 31, as said below
- slot: int32 [32768], P(('expert', 'dp')), may hold values from 0 to 7, as said below
- kept: int32 [32768], P(('expert', 'dp')), may hold values from 0 to 1, as said below
- w_in: bfloat16 [32, 2048, 5120], P('expert', None, 'mp'), may hold values from -0.125 to 0.125
- w_out: bfloat16 [32, 5120, 2048], P('expert', 'mp'), may hold values from -0.078125 to 0.078125
Outputs:
- grad_tokens: bfloat16 [32768, 2048], P(('expert', 'dp'))
- grad_gate: bfloat16 [32768], P(('expert', 'dp'))
- grad_w_in: bfloat16 [32, 2048, 5120], P('expert', 'dp', 'mp')
- grad_w_out: bfloat16 [32, 5120, 2048], P('expert', 'mp', 'dp')
Inputs may be any that keep to these rules, and one draw needn't show every extreme that they name: `expert_index`: in each group of 256 consecutive tokens, kept tokens of one expert have distinct slots, and some expert has exactly 8 kept tokens; which experts are busy is drawn from the seed. slot is 0 where kept is 0. A token of one group is kept exactly when fewer than 8 tokens of that group with the same expert come before it in a priority order drawn from the seed.
All inputs are finite; a program needn't handle non-finite values.
Results may differ from a plain program's by a relative error of at most 0.022.
Values may be sent and summed in bfloat16 or wider, within the bound.
No kernel may reach another device: no remote copies, remote signals or barrier semaphores. Data moves between devices by JAX's collectives and lax.ppermute only.
A program may use at most 64 MiB of HBM per device.

v0:
```python
import math

import jax
import jax.numpy as jnp
from jax import lax
from jax.sharding import PartitionSpec as P

D = 2048
CAP = 8


root_two_pi = math.sqrt(2.0 / math.pi)


def gelu_value(pre):
    inner = root_two_pi * (pre + 0.044715 * pre * pre * pre)
    return 0.5 * pre * (1.0 + jnp.tanh(inner))


def gelu_slope(pre):
    inner = root_two_pi * (pre + 0.044715 * pre * pre * pre)
    tangent = jnp.tanh(inner)
    return 0.5 * (1.0 + tangent) + 0.5 * pre * (1.0 - tangent * tangent) * root_two_pi * (
        1.0 + 3.0 * 0.044715 * pre * pre
    )


def contract_rows(left, right):
    return lax.dot_general(
        left, right, (((0,), (0,)), ((), ())), preferred_element_type=jnp.float32
    )


def contract_cols(left, right):
    return lax.dot_general(
        left, right, (((1,), (1,)), ((), ())), preferred_element_type=jnp.float32
    )


def local(grad_out, tokens, gate, expert_index, slot, kept, w_in, w_out):
    experts = lax.axis_size("expert")
    slots = experts * CAP
    count = grad_out.shape[0]
    zero_half = jnp.zeros((), jnp.bfloat16)
    position = expert_index * CAP + slot
    live = kept == 1
    table = (position[:, None] == jnp.arange(slots, dtype=jnp.int32)[None, :]) & live[:, None]
    table_float = table.astype(jnp.float32)
    filled = jnp.sum(table_float, axis=0) > 0.5
    source_row = jnp.dot(
        jnp.arange(count, dtype=jnp.float32), table_float, precision=lax.Precision.HIGHEST
    ).astype(jnp.int32)
    send_x = jnp.where(filled[:, None], tokens[source_row], zero_half).reshape(experts, CAP, D)
    send_dy = jnp.where(filled[:, None], grad_out[source_row], zero_half).reshape(experts, CAP, D)
    send_gate = jnp.where(filled, gate[source_row], zero_half).reshape(experts, CAP)
    arrived = (
        lax.all_to_all(send_x, "expert", split_axis=0, concat_axis=0, tiled=True),
        lax.all_to_all(send_dy, "expert", split_axis=0, concat_axis=0, tiled=True),
        lax.all_to_all(send_gate, "expert", split_axis=0, concat_axis=0, tiled=True),
    )
    rows = experts * CAP
    x_rows = arrived[0].reshape(rows, D)
    dy_rows = arrived[1].reshape(rows, D)
    gate_rows = arrived[2].reshape(rows).astype(jnp.float32)[:, None]
    weight_in = w_in[0]
    weight_out = w_out[0]
    pre = jnp.dot(x_rows, weight_in, preferred_element_type=jnp.float32)
    hidden = gelu_value(pre).astype(jnp.bfloat16)
    back = contract_cols(dy_rows, weight_out)
    gate_part = jnp.sum(hidden.astype(jnp.float32) * back, axis=1)
    grad_pre = (gate_rows * back * gelu_slope(pre)).astype(jnp.bfloat16)
    scaled = (gate_rows * dy_rows.astype(jnp.float32)).astype(jnp.bfloat16)
    part_in = contract_rows(x_rows, grad_pre)
    part_out = contract_rows(scaled, hidden)
    weight_total = (
        lax.psum_scatter(
            part_in.astype(jnp.bfloat16), "dp", scatter_dimension=0, tiled=True
        ).astype(jnp.float32),
        lax.psum_scatter(
            part_out.astype(jnp.bfloat16), "dp", scatter_dimension=0, tiled=True
        ).astype(jnp.float32),
    )
    total_in = weight_total[0]
    total_out = weight_total[1]
    grad_w_in = total_in.astype(jnp.bfloat16)[None]
    grad_w_out = total_out.astype(jnp.bfloat16).T[None]
    token_part = contract_cols(grad_pre, weight_in)
    token_total, gate_total = (
        lax.psum(token_part.astype(jnp.bfloat16), "mp").astype(jnp.float32),
        lax.psum(gate_part.astype(jnp.bfloat16), "mp").astype(jnp.float32),
    )
    returned = (
        lax.all_to_all(
            token_total.astype(jnp.bfloat16).reshape(experts, CAP, D),
            "expert",
            split_axis=0,
            concat_axis=0,
            tiled=True,
        ),
        lax.all_to_all(
            gate_total.astype(jnp.bfloat16).reshape(experts, CAP),
            "expert",
            split_axis=0,
            concat_axis=0,
            tiled=True,
        ),
    )
    token_rows = returned[0].reshape(slots, D)[position]
    grad_tokens = jnp.where(live[:, None], token_rows, zero_half)
    gate_back = returned[1].reshape(slots)[position]
    grad_gate = jnp.where(live, gate_back, zero_half)
    return (grad_tokens, grad_gate, grad_w_in, grad_w_out)


def solution(mesh):
    placed = (
        P(("expert", "dp"), None),
        P(("expert", "dp"), None),
        P(("expert", "dp")),
        P(("expert", "dp")),
        P(("expert", "dp")),
        P(("expert", "dp")),
        P("expert", None, "mp"),
        P("expert", "mp", None),
    )
    return jax.shard_map(
        local,
        mesh=mesh,
        in_specs=placed,
        out_specs=(
            P(("expert", "dp"), None),
            P(("expert", "dp")),
            P("expert", "dp", "mp"),
            P("expert", "mp", "dp"),
        ),
        check_vma=False,
    )
```

profile of v0, /device:TPU:2, one launch (start us, length us, event | category | flops | bytes accessed | tf_op | source)
XLA Modules:
  0.0 270.0 jit_solution(4707917052954241092)
XLA Ops:
  8.0 0.0 copy-start
  8.0 0.8 broadcast_compare_fusion.1
  8.8 0.7 compare_select_fusion
  9.5 0.2 fusion.25
  9.8 0.2 convert_reduce_fusion
  10.0 1.9 gather_fusion
  11.9 0.7 select_n.47
  12.7 16.7 %all-to-all-start = ((bf16[32,1,8]{2,1,0:T(2,128)(2,1)}), bf16[32,1,8]{2,1,0:T(2,128)(2,1)S(1)}, u32[]{:S(2)}, u32[]{:S(2)}) async-start(bf16[32,1,8]{2,1,0:T(2,128)(2,1)} %select_n.47), calls=%async_computation | async-start | bytes 32768 | tf_op jit(solution)/shard_map/all_to_all | solution.py:59
  29.3 0.1 gt.24
  29.4 4.7 %gather_fusion.2 = bf16[256,2048]{1,0:T(8,128)(2,1)} fusion(bf16[256,2048]{1,0:T(8,128)(2,1)} %param.9, s32[1024]{0:T(1024)S(1)} %pad_clamp_fusion.1), kind=kCustom, calls=%fused_computation.2 | custom fusion | bytes 2098176 | tf_op jit(solution)/shard_map/gather | solution.py:53
  34.1 4.7 %gather_fusion.1 = bf16[256,2048]{1,0:T(8,128)(2,1)} fusion(bf16[256,2048]{1,0:T(8,128)(2,1)} %param.8, s32[1024]{0:T(1024)S(1)} %pad_clamp_fusion.1), kind=kCustom, calls=%fused_computation.1 | custom fusion | bytes 2098176 | tf_op jit(solution)/shard_map/gather | solution.py:54
  38.8 3.1 %bitcast_select_fusion.1 = (bf16[32,8,2048]{2,1,0:T(8,128)(2,1)}, bf16[32,8,2048]{2,1,0:T(8,128)(2,1)}) fusion(bf16[256,2048]{1,0:T(8,128)(2,1)} %gather_fusion.1, pred[32,8]{1,0:T(8,128)(4,1)S(1)} %gt.24, bf16[256,2048]{1,0:T(8,128)(2,1)} %gather_fusion.2), kind=kLoop, calls=%fused_computation.21 | loop fusion | flops 1048576 | bytes 4194560 | tf_op jit(solution)/shard_map/jit(_where)/select_n | solution.py:54
  41.9 0.0 all-to-all-done
  41.9 38.0 %all_to_all.30 = bf16[32,8,2048]{2,1,0:T(8,128)(2,1)} all-to-all(bf16[32,8,2048]{2,1,0:T(8,128)(2,1)} %get-tuple-element.27), channel_id=1, replica_groups=mesh['expert'=32,'mp'=8,'dp'=4] {'expert'}, dimensions={0} | all-to-all | bytes 2097152 | tf_op jit(solution)/shard_map/all_to_all | solution.py:57
  79.9 6.2 %all-to-all-start.1 = ((bf16[32,8,2048]{2,1,0:T(8,128)(2,1)}), bf16[32,8,2048]{2,1,0:T(8,128)(2,1)}, u32[]{:S(2)}, u32[]{:S(2)}) async-start(bf16[32,8,2048]{2,1,0:T(8,128)(2,1)} %get-tuple-element.26), calls=%async_computation.1 | async-start | bytes 2097152 | tf_op jit(solution)/shard_map/all_to_all | solution.py:58
  86.1 0.0 all-reduce.2.cloned.1.call-start
  86.2 0.1 convert_reduce_fusion.1
  86.3 0.1 reshape.93
  86.3 0.0 copy-done
  86.3 3.0 %fusion.2 = f32[256,640]{1,0:T(8,128)} fusion(bf16[1,2048,640]{2,1,0:T(8,128)(2,1)S(1)} %copy-done, bf16[32,8,2048]{2,1,0:T(8,128)(2,1)} %all_to_all.30), kind=kOutput, calls=%fused_computation.9 | convolution fusion | flops 671088640 | bytes 4325376 | tf_op jit(solution)/shard_map/dot_general | solution.py:67
  89.4 23.0 %all-to-all-done.1 = bf16[32,8,2048]{2,1,0:T(8,128)(2,1)} async-done(((bf16[32,8,2048]{2,1,0:T(8,128)(2,1)}), bf16[32,8,2048]{2,1,0:T(8,128)(2,1)}, u32[]{:S(2)}, u32[]{:S(2)}) %all-to-all-start.1) | async-done | bytes 1048608 | tf_op jit(solution)/shard_map/all_to_all | solution.py:58
  112.4 3.6 %multiply_reduce_fusion = (bf16[256]{0:T(256)(128)(2,1)S(1)}, bf16[256,640]{1,0:T(8,128)(2,1)S(1)}) fusion(f32[256,640]{1,0:T(8,128)} %fusion.2, f32[256]{0:T(256)S(1)} %reshape.93, bf16[1,640,2048]{2,1,0:T(8,128)(2,1)} %param.15, bf16[32,8,2048]{2,1,0:T(8,128)(2,1)} %all-to-all-done.1), kind=kOutput, calls=%fused_computation.33 | convolution fusion | flops 675184384 | bytes 4654592 | tf_op jit(solution)/shard_map/dot_general | solution.py:35
  115.9 2.0 fusion.9
  117.9 0.0 all-reduce.2.cloned.1.call-update
  118.0 0.0 reduce-scatter.5.cloned.1.call-start
  118.0 4.1 %convolution_convert_fusion = bf16[2048,640]{1,0:T(8,128)(2,1)} fusion(bf16[32,8,2048]{2,1,0:T(8,128)(2,1)} %all-to-all-done.1, f32[256]{0:T(256)S(1)} %reshape.93, f32[256,640]{1,0:T(8,128)} %fusion.2), kind=kOutput, calls=%fused_computation.5 | convolution fusion | flops 675446784 | bytes 4326400 | tf_op jit(solution)/shard_map/dot_general | solution.py:29
  122.1 0.0 reduce-scatter.5.cloned.1.call-update
  122.1 0.0 reduce-scatter.3.cloned.1.call-start
  122.1 3.8 %convolution_convert_fusion.1 = bf16[2048,640]{1,0:T(8,128)(2,1)} fusion(bf16[256,640]{1,0:T(8,128)(2,1)S(1)} %get-tuple-element.25, bf16[32,8,2048]{2,1,0:T(8,128)(2,1)} %all_to_all.30), kind=kOutput, calls=%fused_computation.6 | convolution fusion | flops 672399360 | bytes 3997696 | tf_op jit(solution)/shard_map/dot_general | solution.py:29
  125.9 0.0 copy-start.1
  125.9 0.0 reduce-scatter.3.cloned.1.call-update
  126.0 0.1 all_to_all.23
  126.0 32.8 %psum.15 = bf16[32,1,8]{2,0,1:T(8,128)(2,1)S(1)} all-reduce(bf16[32,1,8]{2,0,1:T(8,128)(2,1)S(1)} %all_to_all.23), channel_id=1, replica_groups=mesh['expert'=32,'mp'=8,'dp'=4] {'mp'}, use_global_device_ids=true, to_apply=%region_3.4 | all-reduce | flops 256 | bytes 1024 | tf_op jit(solution)/shard_map/psum | solution.py:90
  158.9 17.4 %all_to_all.31 = bf16[32,1,8]{2,1,0:T(2,128)(2,1)S(1)} all-to-all(bf16[32,1,8]{2,1,0:T(2,128)(2,1)S(1)} %copy.18), channel_id=1, replica_groups=mesh['expert'=32,'mp'=8,'dp'=4] {'expert'}, dimensions={0} | all-to-all | bytes 1024 | tf_op jit(solution)/shard_map/all_to_all | solution.py:100
  176.3 38.6 %all-reduce.2.cloned.1.call-done = bf16[32,8,2048]{2,1,0:T(8,128)(2,1)} async-done(((bf16[32,8,2048]{2,1,0:T(8,128)(2,1)}), bf16[32,8,2048]{2,1,0:T(8,128)(2,1)}) %all-reduce.2.cloned.1.call-update) | async-done | bytes 1048592 | tf_op jit(solution)/shard_map/psum | solution.py:89
  214.9 12.5 %all-to-all-start.3 = ((bf16[32,8,2048]{2,1,0:T(8,128)(2,1)}), bf16[32,8,2048]{2,1,0:T(8,128)(2,1)}, u32[]{:S(2)}, u32[]{:S(2)}) async-start(bf16[32,8,2048]{2,1,0:T(8,128)(2,1)} %all-reduce.2.cloned.1.call-done), calls=%async_computation.3 | async-start | bytes 2097152 | tf_op jit(solution)/shard_map/all_to_all | solution.py:93
  227.5 0.1 reduce.1
  227.5 0.1 reshape.92
  227.6 1.9 gather_fusion.4
  229.5 0.0 copy-done.1
  229.5 0.5 broadcast_select_fusion.1
  230.0 23.4 %all-to-all-done.3 = bf16[32,8,2048]{2,1,0:T(8,128)(2,1)} async-done(((bf16[32,8,2048]{2,1,0:T(8,128)(2,1)}), bf16[32,8,2048]{2,1,0:T(8,128)(2,1)}, u32[]{:S(2)}, u32[]{:S(2)}) %all-to-all-start.3) | async-done | bytes 1048608 | tf_op jit(solution)/shard_map/all_to_all | solution.py:93
  253.4 4.7 %gather_fusion.3 = bf16[256,2048]{1,0:T(8,128)(2,1)} fusion(bf16[256,2048]{1,0:T(8,128)(2,1)} %bitcast.8, s32[1024]{0:T(1024)S(1)} %pad_clamp_fusion), kind=kCustom, calls=%fused_computation.3 | custom fusion | bytes 2098176 | tf_op jit(solution)/shard_map/gather | solution.py:108
  258.1 2.3 broadcast_select_fusion
  260.4 0.0 reduce-scatter.5.cloned.1.call-done
  260.4 2.2 copy.19
  262.6 0.0 reduce-scatter.3.cloned.1.call-done
  (5 shorter events, 0.0 us)
Async XLA Ops:
  8.0 78.3 %copy-start = (bf16[1,2048,640]{2,1,0:T(8,128)(2,1)S(1)}, bf16[1,2048,640]{2,1,0:T(8,128)(2,1)}, u32[]{:S(2)}) copy-start(bf16[1,2048,640]{2,1,0:T(8,128)(2,1)} %param.14) | copy-start | bytes 7864324
  12.7 29.3 %all-to-all-start = ((bf16[32,1,8]{2,1,0:T(2,128)(2,1)}), bf16[32,1,8]{2,1,0:T(2,128)(2,1)S(1)}, u32[]{:S(2)}, u32[]{:S(2)}) async-start(bf16[32,1,8]{2,1,0:T(2,128)(2,1)} %select_n.47), calls=%async_computation | async-start | bytes 32768 | tf_op jit(solution)/shard_map/all_to_all | solution.py:59
  79.9 32.4 %all-to-all-start.1 = ((bf16[32,8,2048]{2,1,0:T(8,128)(2,1)}), bf16[32,8,2048]{2,1,0:T(8,128)(2,1)}, u32[]{:S(2)}, u32[]{:S(2)}) async-start(bf16[32,8,2048]{2,1,0:T(8,128)(2,1)} %get-tuple-element.26), calls=%async_computation.1 | async-start | bytes 2097152 | tf_op jit(solution)/shard_map/all_to_all | solution.py:58
  86.1 128.8 %all-reduce.2.cloned.1.call-start = ((), (), s32[]{:S(2)}) async-start(), calls=%async_computation.7 | async-start | bytes 2097152 | tf_op jit(solution)/shard_map/psum | solution.py:89
  118.0 142.5 %reduce-scatter.5.cloned.1.call-start = ((), (), s32[]{:S(2)}) async-start(), calls=%async_computation.9 | async-start | bytes 3276800 | tf_op jit(solution)/shard_map/reduce_scatter | solution.py:79
  122.1 140.5 %reduce-scatter.3.cloned.1.call-start = ((), (), s32[]{:S(2)}) async-start(), calls=%async_computation.8 | async-start | bytes 3276800 | tf_op jit(solution)/shard_map/reduce_scatter | solution.py:76
  125.9 103.6 %copy-start.1 = (s32[256]{0:T(256)S(1)}, s32[256]{0:T(256)}, u32[]{:S(2)}) copy-start(s32[256]{0:T(256)} %param.13) | copy-start | bytes 3076
  214.9 38.4 %all-to-all-start.3 = ((bf16[32,8,2048]{2,1,0:T(8,128)(2,1)}), bf16[32,8,2048]{2,1,0:T(8,128)(2,1)}, u32[]{:S(2)}, u32[]{:S(2)}) async-start(bf16[32,8,2048]{2,1,0:T(8,128)(2,1)} %all-reduce.2.cloned.1.call-done), calls=%async_computation.3 | async-start | bytes 2097152 | tf_op jit(solution)/shard_map/all_to_all | solution.py:93
Sparse Core Ops, SparseCore 0:
  118.1 96.8 all-reduce.1
Sparse Core Ops, SparseCore 1:
  122.2 48.0 reduce-scatter.4
  174.1 41.4 reduce-scatter.2
where the time goes:
time: 271 us; the launch traced here: 270 us
  blocking collectives  88.3 us (33%)
  waiting for transfers between devices  85 us (31%)
  starting transfers between devices  35.5 us (13%)
  local copies, waits for them, and re-layouts  21.2 us (8%)
  matrix products  16.7 us (6%)
  between operations  15.6 us (6%)
  other arithmetic  7.82 us (3%)
    psum x1, waiting for transfers between devices, local(): lax.psum(token_part.astype(jnp.bfloat16), 'mp').astype(jnp.float32)  38.6 us
    all_to_all x1, blocking collectives, local(): lax.all_to_all(send_x, 'expert', split_axis=0, concat_axis=0, tiled=True)  38 us
    psum x1, blocking collectives, local(): lax.psum(gate_part.astype(jnp.bfloat16), 'mp').astype(jnp.float32)  32.8 us
    all_to_all x1, waiting for transfers between devices, local(): lax.all_to_all(token_total.astype(jnp.bfloat16).reshape(experts, CAP, D),...  23.4 us
    all_to_all x1, waiting for transfers between devices, local(): lax.all_to_all(send_dy, 'expert', split_axis=0, concat_axis=0, tiled=True)  23 us
    all_to_all x1, blocking collectives, local(): lax.all_to_all(gate_total.astype(jnp.bfloat16).reshape(experts, CAP), 'ex...  17.4 us
    all_to_all x1, starting transfers between devices, local(): lax.all_to_all(send_gate, 'expert', split_axis=0, concat_axis=0, tiled=True)  16.7 us
    all_to_all x1, starting transfers between devices, local(): lax.all_to_all(token_total.astype(jnp.bfloat16).reshape(experts, CAP, D),...  12.5 us
  transfers between devices with their start and end apart: 6, of which 3 were waited for; matrix products, arithmetic and copies ran while one was open for 13% of the time, Pallas kernels for 0%

commit v1 on v0

v1 whole, which is shorter than its diff:
```python
import math

import jax
import jax.numpy as jnp
from jax import lax
from jax.sharding import PartitionSpec as P

D = 2048
CAP = 8
LANES = 128

root_two_pi = math.sqrt(2.0 / math.pi)


def gelu_pair(pre):
    inner = root_two_pi * (pre + 0.044715 * pre * pre * pre)
    tangent = jnp.tanh(inner)
    half = 0.5 * (1.0 + tangent)
    slope = half + 0.5 * pre * (1.0 - tangent * tangent) * root_two_pi * (
        1.0 + 3.0 * 0.044715 * pre * pre
    )
    return pre * half, slope


def dot(left, right, dims):
    return lax.dot_general(left, right, (dims, ((), ())), preferred_element_type=jnp.float32)


def shift(value, step):
    return lax.ppermute(value, "mp", [(i, (i + step) % 8) for i in range(8)])


def swap(value, bit):
    return lax.ppermute(value, "dp", [(i, i ^ bit) for i in range(4)])


def gather_pieces(piece):
    right, left, right2, left2 = (shift(piece, step) for step in (1, -1, 2, -2))
    half = piece.shape[0] // 2
    far = jnp.concatenate([shift(right2[:half], 2), shift(left2[half:], -2)])
    return [piece, right, left, right2, left2, shift(right2, 1), shift(left2, -1), far]


OFFSETS = (0, -1, 1, -2, 2, -3, 3, 4)


def local(grad_out, tokens, gate, expert_index, slot, kept, w_in, w_out):
    experts = lax.axis_size("expert")
    me = lax.axis_index("mp")
    data = lax.axis_index("dp")
    count = grad_out.shape[0]
    weight_in = w_in[0]
    weight_out = w_out[0]
    live = kept == 1
    gate_float = gate.astype(jnp.float32)

    position = expert_index * CAP + slot
    slots = experts * CAP
    pick = (
        (lax.broadcasted_iota(jnp.int32, (slots, count), 0) == position[None, :]) & live[None, :]
    ).astype(jnp.bfloat16)
    send = jnp.concatenate(
        [
            dot(pick, tokens, ((1,), (0,))).astype(jnp.bfloat16),
            dot(pick * gate[None, :], grad_out, ((1,), (0,))).astype(jnp.bfloat16),
        ],
        axis=1,
    )
    came = lax.all_to_all(
        send.reshape(experts, CAP, 2 * D), "expert", split_axis=0, concat_axis=0, tiled=True
    ).reshape(slots, 2 * D)
    x_rows = came[:, :D]
    s_rows = came[:, D:]

    pre = dot(x_rows, weight_in, ((1,), (0,)))
    value, slope = gelu_pair(pre)
    hidden = value.astype(jnp.bfloat16)
    back = dot(s_rows, weight_out, ((1,), (1,)))
    grad_pre = (back * slope).astype(jnp.bfloat16)
    gate_part = jnp.sum(hidden.astype(jnp.float32) * back, axis=1).astype(jnp.bfloat16)
    order = lax.broadcasted_iota(jnp.int32, (slots, slots), 0)
    order = order % experts * CAP + order // experts
    order = (order == lax.broadcasted_iota(jnp.int32, (slots, slots), 1)).astype(jnp.bfloat16)
    sorted_grad = dot(order, grad_pre, ((1,), (0,))).astype(jnp.bfloat16)
    sorted_gate = dot(
        order, jnp.broadcast_to(gate_part[:, None], (slots, LANES)), ((1,), (0,))
    ).astype(jnp.bfloat16)
    token_part = dot(sorted_grad, weight_in, ((1,), (1,))).astype(jnp.bfloat16)
    rows = jnp.concatenate([token_part, sorted_gate], axis=1)

    terms = lax.all_to_all(
        rows.reshape(CAP, experts, D + LANES), "mp", split_axis=0, concat_axis=0, tiled=True
    )
    total = jnp.sum(terms.astype(jnp.float32), axis=0)
    total = total.astype(jnp.bfloat16)
    home = lax.all_to_all(
        jnp.pad(total, ((0, 0), (0, LANES))).reshape(experts, 2, D // 2 + LANES),
        "expert", split_axis=0, concat_axis=0, tiled=True,
    ).reshape(experts, D + 2 * LANES)[:, : D + LANES]
    table = jnp.concatenate(gather_pieces(home))
    row_block = lax.broadcasted_iota(jnp.int32, (count, CAP * experts), 1) // experts
    row_expert = lax.broadcasted_iota(jnp.int32, (count, CAP * experts), 1) % experts
    ahead = (slot - me) & 7
    block = jnp.zeros_like(slot)
    for k, offset in enumerate(OFFSETS):
        block = jnp.where(ahead == offset % 8, k, block)
    choose = (
        (row_block == block[:, None]) & (row_expert == expert_index[:, None]) & live[:, None]
    ).astype(jnp.bfloat16)
    result = dot(choose, table, ((1,), (0,)))
    grad_tokens = result[:, :D].astype(jnp.bfloat16)
    grad_gate = (result[:, D] / gate_float).astype(jnp.bfloat16)

    def column(value, index):
        return lax.dynamic_slice_in_dim(value, index * (D // 4), D // 4, 1)

    def halves(value, mask):
        return column(value, data ^ mask), column(value, data ^ (mask ^ 2))

    x_keep, x_pass = halves(x_rows, 0)
    s_keep, s_pass = halves(s_rows, 0)
    other = swap(jnp.concatenate(halves(x_rows, 1) + halves(s_rows, 1), axis=1), 1)
    acts = jnp.concatenate([grad_pre, hidden], axis=1)
    other_acts = swap(acts, 1)
    width = grad_pre.shape[1]
    q = D // 4
    grads = jnp.concatenate([grad_pre, other_acts[:, :width]])
    hiddens = jnp.concatenate([hidden, other_acts[:, width:]])
    x_keep = jnp.concatenate([x_keep, other[:, :q]])
    x_pass = jnp.concatenate([x_pass, other[:, q : 2 * q]])
    s_keep = jnp.concatenate([s_keep, other[:, 2 * q : 3 * q]])
    s_pass = jnp.concatenate([s_pass, other[:, 3 * q :]])
    rows_first = ((0,), (0,))
    in_term = swap(dot(x_pass, grads, rows_first).astype(jnp.bfloat16), 2)
    out_term = swap(dot(hiddens, s_pass, rows_first).astype(jnp.bfloat16), 2)
    grad_w_in = (dot(x_keep, grads, rows_first) + in_term.astype(jnp.float32)).astype(jnp.bfloat16)[None]
    grad_w_out = (dot(hiddens, s_keep, rows_first) + out_term.astype(jnp.float32)).astype(jnp.bfloat16)[None]
    return (grad_tokens, grad_gate, grad_w_in, grad_w_out)


def solution(mesh):
    placed = (
        P(("expert", "dp"), None),
        P(("expert", "dp"), None),
        P(("expert", "dp")),
        P(("expert", "dp")),
        P(("expert", "dp")),
        P(("expert", "dp")),
        P("expert", None, "mp"),
        P("expert", "mp", None),
    )
    return jax.shard_map(
        local,
        mesh=mesh,
        in_specs=placed,
        out_specs=(
            P(("expert", "dp"), None),
            P(("expert", "dp")),
            P("expert", "dp", "mp"),
            P("expert", "mp", "dp"),
        ),
        check_vma=False,
    )
```

time: 271 us -> 199 us (0.73)
  blocking collectives: 88.3 us -> 0 us
  starting transfers between devices: 35.5 us -> 86.1 us
  between operations: 15.6 us -> 1.11 us
  local copies, waits for them, and re-layouts: 21.2 us -> 9.45 us
  waiting for transfers between devices: 85 us -> 73.9 us
  matrix products: 16.7 us -> 20.2 us
    all_to_all x2 -> x0, blocking collectives: 55.4 us -> none  [the longest x1 38 us: local(): lax.all_to_all(send_x, 'expert', split_axis=0, concat_axis=0, tiled=True)]
    psum x1 -> x0, waiting for transfers between devices: 38.6 us -> none  [local(): lax.psum(token_part.astype(jnp.bfloat16), 'mp').astype(jnp.float32)]
    ppermute x0 -> x12, starting transfers between devices: none -> 34.6 us  [the longest x8 26.5 us: shift(): return lax.ppermute(value, 'mp', [(i, (i + step) % 8) for i in range(8)])]
    psum x1 -> x0, blocking collectives: 32.8 us -> none  [local(): lax.psum(gate_part.astype(jnp.bfloat16), 'mp').astype(jnp.float32)]
    all_to_all x3, waiting for transfers between devices: 46.4 us -> 66.9 us  [the longest x1 46.7 us: local(): lax.all_to_all(send.reshape(experts, CAP, 2 * D), 'expert', split_axis=0,...]
    gather x5 -> x0, local copies, waits for them, and re-layouts: 17.9 us -> none  [the longest x1 4.71 us: local(): tokens[source_row]]
    all_to_all x3, starting transfers between devices: 35.4 us -> 51.4 us  [the longest x1 21.2 us: local(): lax.all_to_all(rows.reshape(CAP, experts, D + LANES), 'mp', split_axis=0,...]
    ppermute x0 -> x12, waiting for transfers between devices: none -> 7.07 us  [the longest x8 5.36 us: shift(): return lax.ppermute(value, 'mp', [(i, (i + step) % 8) for i in range(8)])]
  transfers between devices with their start and end apart: 6 -> 15, of which waited for: 3 -> 5; matrix products, arithmetic and copies ran while one was open for 13% -> 8% of each run, Pallas kernels for 0% -> 0%
where the time goes in v1:
time: 199 us; the launch traced here: 198 us
  starting transfers between devices  86.1 us (43%)
  waiting for transfers between devices  73.9 us (37%)
  matrix products  20.2 us (10%)
  local copies, waits for them, and re-layouts  9.45 us (5%)
  other arithmetic  7.58 us (4%)
    all_to_all x1, waiting for transfers between devices, local(): lax.all_to_all(send.reshape(experts, CAP, 2 * D), 'expert', split_axis=0,...  46.7 us
    ppermute x8, starting transfers between devices, shift(): return lax.ppermute(value, 'mp', [(i, (i + step) % 8) for i in range(8)])  26.5 us
    all_to_all x1, starting transfers between devices, local(): lax.all_to_all(rows.reshape(CAP, experts, D + LANES), 'mp', split_axis=0,...  21.2 us
    dot_general x11, matrix products, dot(): lax.dot_general(left, right, (dims, ((), ())), preferred_element_type=jnp...  20.2 us
    all_to_all x1, starting transfers between devices, local(): lax.all_to_all(send.reshape(experts, CAP, 2 * D), 'expert', split_axis=0,...  17.5 us
    all_to_all x1, waiting for transfers between devices, local(): lax.all_to_all(rows.reshape(CAP, experts, D + LANES), 'mp', split_axis=0,...  14.6 us
    all_to_all x1, starting transfers between devices, local(): lax.all_to_all(jnp.pad(total, ((0, 0), (0, LANES))).reshape(experts, 2, D...  12.7 us
    ppermute x4, starting transfers between devices, swap(): return lax.ppermute(value, 'dp', [(i, i ^ bit) for i in range(4)])  8.15 us
  transfers between devices with their start and end apart: 15, of which 5 were waited for; matrix products, arithmetic and copies ran while one was open for 8% of the time, Pallas kernels for 0%

profile of v1, /device:TPU:2, one launch (start us, length us, event | category | flops | bytes accessed | tf_op | source)
XLA Modules:
  0.0 198.3 jit_solution(18102618981540010144)
XLA Ops:
  0.6 0.0 copy-start
  0.7 0.8 broadcast_compare_fusion
  1.5 0.8 compare_select_fusion.6
  2.3 1.7 convolution_convert_fusion.1
  4.0 0.4 convolution_convert_fusion
  4.4 1.5 maximum_bitcast_fusion
  5.9 17.5 %all-to-all-start = ((bf16[32,8,4096]{2,1,0:T(8,128)(2,1)}), bf16[32,8,4096]{2,1,0:T(8,128)(2,1)}, u32[]{:S(2)}, u32[]{:S(2)}) async-start(bf16[32,8,4096]{2,1,0:T(8,128)(2,1)} %maximum_bitcast_fusion), calls=%async_computation | async-start | bytes 4194304 | tf_op jit(solution)/shard_map/all_to_all | solution.py:69
  23.6 46.7 %all-to-all-done = bf16[32,8,4096]{2,1,0:T(8,128)(2,1)} async-done(((bf16[32,8,4096]{2,1,0:T(8,128)(2,1)}), bf16[32,8,4096]{2,1,0:T(8,128)(2,1)}, u32[]{:S(2)}, u32[]{:S(2)}) %all-to-all-start) | async-done | bytes 2097184 | tf_op jit(solution)/shard_map/all_to_all | solution.py:69
  70.2 3.1 %fusion.66 = (bf16[256,2048]{1,0:T(8,128)(2,1)}, bf16[256,2048]{1,0:T(8,128)(2,1)}) fusion(bf16[256,4096]{1,0:T(8,128)(2,1)} %bitcast.1), kind=kLoop, calls=%fused_computation.119 | loop fusion | bytes 4194304 | tf_op jit(solution)/shard_map/slice | solution.py:72
  73.4 2.4 %fusion.2 = f32[256,640]{1,0:T(8,128)S(1)} fusion(bf16[1,2048,640]{2,1,0:T(8,128)(2,1)S(1)} %copy-done, bf16[256,4096]{1,0:T(8,128)(2,1)} %bitcast.1), kind=kOutput, calls=%fused_computation.2 | convolution fusion | flops 671088640 | bytes 4325376 | tf_op jit(solution)/shard_map/dot_general | solution.py:26
  75.7 3.3 %multiply_reduce_fusion = (bf16[256]{0:T(256)(128)(2,1)S(1)}, bf16[256,640]{1,0:T(8,128)(2,1)}, bf16[256,640]{1,0:T(8,128)(2,1)S(1)}) fusion(f32[256,640]{1,0:T(8,128)S(1)} %fusion.2, bf16[1,640,2048]{2,1,0:T(8,128)(2,1)S(1)} %copy-done.10, bf16[256,4096]{1,0:T(8,128)(2,1)} %bitcast.1), kind=kOutput, calls=%fused_computation.35 | convolution fusion | flops 675020544 | bytes 4981248 | tf_op jit(solution)/shard_map/dot_general | solution.py:26
  79.0 0.4 convolution_convert_fusion.5
  79.4 2.3 %fusion.6 = bf16[256,2048]{1,0:T(8,128)(2,1)} fusion(bf16[1,2048,640]{2,1,0:T(8,128)(2,1)S(1)} %copy-done, bf16[256,640]{1,0:T(8,128)(2,1)S(1)} %get-tuple-element.8, s32[256]{0:T(256)S(1)} %get-tuple-element.29, s32[256]{0:T(256)S(1)} %get-tuple-element.32, s32[256]{0:T(256)S(1)} %get-tuple-element.30, s32[256]{0:T(256)S(1)} %get-tuple-element.31, ...), kind=kOutput, calls=%fused_computation.6 | convolution fusion | flops 755990528 | bytes 4002304 | tf_op jit(solution)/shard_map/dot_general | solution.py:26
  81.7 2.3 %pad_maximum_fusion = bf16[256,2176]{1,0:T(8,128)(2,1)} fusion(bf16[256,128]{1,0:T(8,128)(2,1)S(1)} %convolution_convert_fusion.5, bf16[256,2048]{1,0:T(8,128)(2,1)} %fusion.6), kind=kLoop, calls=%fused_computation.21 | loop fusion | flops 2228224 | bytes 2228224 | tf_op jit(solution)/shard_map/concatenate | solution.py:89
  84.0 21.2 %all-to-all-start.1 = ((bf16[8,32,2176]{2,1,0:T(8,128)(2,1)}), bf16[8,32,2176]{2,1,0:T(8,128)(2,1)}, u32[]{:S(2)}, u32[]{:S(2)}) async-start(bf16[8,32,2176]{2,1,0:T(8,128)(2,1)} %bitcast.26), calls=%async_computation.1 | async-start | bytes 2228224 | tf_op jit(solution)/shard_map/all_to_all | solution.py:91
  105.2 2.4 %constant_dynamic-slice_fusion.1 = (bf16[256,512]{1,0:T(8,128)(2,1)}, bf16[256,512]{1,0:T(8,128)(2,1)S(1)}, bf16[256,512]{1,0:T(8,128)(2,1)S(1)}, bf16[256,512]{...) fusion(bf16[256,2048]{1,0:T(8,128)(2,1)} %get-tuple-element.7, ...), kind=kLoop, calls=%fused_computation.86 | loop fusion | bytes 4194320 | tf_op jit(solution)/shard_map/dynamic_slice | solution.py:115
  107.6 0.1 pad_maximum_fusion.1
  107.8 1.9 collective-permute-start.8
  109.7 0.1 pad_maximum_fusion.2
  109.8 2.4 %collective-permute-start.9 = (bf16[256,1280]{1,0:T(8,128)(2,1)S(1)}, bf16[256,1280]{1,0:T(8,128)(2,1)S(1)}, u32[]{:S(2)}, u32[]{:S(2)}) collective-permute-start(bf16[256,1280]{1,0:T(8,128)(2,1)S(1)} %pad_maximum_fusion.2), channel_id=1, source_target_pairs={{0,1},{1,0},{2,3},{3,2},{4,5},{5,4},{6,7},{7,6},{8,9},{9,8},{10,11... | collective-permute-start | bytes 1966088 | tf_op jit(solution)/shard_map/ppermute | solution.py:34
  112.2 1.7 collective-permute-done.9
  113.9 0.8 fusion.68
  114.7 0.9 fusion.67
  115.6 1.4 convolution_convert_fusion.2
  116.9 1.9 collective-permute-start.11
  118.9 14.6 %all-to-all-done.1 = bf16[8,32,2176]{2,1,0:T(8,128)(2,1)} async-done(((bf16[8,32,2176]{2,1,0:T(8,128)(2,1)}), bf16[8,32,2176]{2,1,0:T(8,128)(2,1)}, u32[]{:S(2)}, u32[]{:S(2)}) %all-to-all-start.1) | async-done | bytes 1114144 | tf_op jit(solution)/shard_map/all_to_all | solution.py:91
  133.5 1.4 reduce_sum.22
  134.9 0.7 reshape.35
  135.6 12.7 %all-to-all-start.2 = ((bf16[32,2,1152]{2,1,0:T(2,128)(2,1)}), bf16[32,2,1152]{2,1,0:T(2,128)(2,1)S(1)}, u32[]{:S(2)}, u32[]{:S(2)}) async-start(bf16[32,2,1152]{2,1,0:T(2,128)(2,1)} %reshape.35), calls=%async_computation.2 | async-start | bytes 294912 | tf_op jit(solution)/shard_map/all_to_all | solution.py:96
  148.4 2.7 %convolution_convert_fusion.3 = bf16[512,640]{1,0:T(8,128)(2,1)} fusion(bf16[256,512]{1,0:T(8,128)(2,1)} %get-tuple-element.15, bf16[256,512]{1,0:T(8,128)(2,1)} %get-tuple-element.33, bf16[256,640]{1,0:T(8,128)(2,1)} %get-tuple-element.22, bf16[256,640]{1,0:T(8,128)(2,1)S(1)} %get-tuple-element.8), kind=kOutput, calls=%fused_computation.16 | convolution fusion | flops 338231296 | bytes 1835008 | tf_op jit(solution)/shard_map/dot_general | solution.py:26
  151.0 1.9 collective-permute-start.10
  152.9 0.0 collective-permute-done.11
  153.0 2.5 %fusion.11 = bf16[1,640,512]{2,1,0:T(8,128)(2,1)} fusion(bf16[640,512]{1,0:T(8,128)(2,1)} %collective-permute-done.11, bf16[256,512]{1,0:T(8,128)(2,1)S(1)} %copy-done.6, bf16[256,512]{1,0:T(8,128)(2,1)S(1)} %copy-done.7, bf16[256,640]{1,0:T(8,128)(2,1)S(1)} %copy-done.5, bf16[256,640]{1,0:T(8,128)(2,1)S(1)} %copy-done.3), kind=kOutput, calls=%fused_computation.17 | convolution fusion | flops 338886656 | bytes 2490368 | tf_op jit(solution)/shard_map/dot_general | solution.py:26
  155.5 5.6 %all-to-all-done.2 = bf16[32,2,1152]{2,1,0:T(2,128)(2,1)S(1)} async-done(((bf16[32,2,1152]{2,1,0:T(2,128)(2,1)}), bf16[32,2,1152]{2,1,0:T(2,128)(2,1)S(1)}, u32[]{:S(2)}, u32[]{:S(2)}) %all-to-all-start.2) | async-done | bytes 147488 | tf_op jit(solution)/shard_map/all_to_all | solution.py:96
  161.1 2.1 %collective-permute-start.3 = (bf16[32,2176]{1,0:T(8,128)(2,1)S(1)}, bf16[32,2176]{1,0:T(8,128)(2,1)S(1)}, u32[]{:S(2)}, u32[]{:S(2)}) collective-permute-start(bf16[32,2176]{1,0:T(8,128)(2,1)S(1)} %get-tuple-element.23), channel_id=1, source_target_pairs={{0,24},{4,28},{8,0},{12,4},{16,8},{20,12},{24,16},{28,20},{1,25},{... | collective-permute-start | bytes 417800 | tf_op jit(solution)/shard_map/ppermute | solution.py:30
  163.2 4.6 %collective-permute-start.2 = (bf16[32,2176]{1,0:T(8,128)(2,1)S(1)}, bf16[32,2176]{1,0:T(8,128)(2,1)S(1)}, u32[]{:S(2)}, u32[]{:S(2)}) collective-permute-start(bf16[32,2176]{1,0:T(8,128)(2,1)S(1)} %get-tuple-element.23), channel_id=1, source_target_pairs={{0,8},{4,12},{8,16},{12,20},{16,24},{20,28},{24,0},{28,4},{1,9},{5... | collective-permute-start | bytes 417800 | tf_op jit(solution)/shard_map/ppermute | solution.py:30
  167.8 2.1 %collective-permute-start = (bf16[32,2176]{1,0:T(8,128)(2,1)S(1)}, bf16[32,2176]{1,0:T(8,128)(2,1)S(1)}, u32[]{:S(2)}, u32[]{:S(2)}) collective-permute-start(bf16[32,2176]{1,0:T(8,128)(2,1)S(1)} %get-tuple-element.23), channel_id=1, source_target_pairs={{0,4},{4,8},{8,12},{12,16},{16,20},{20,24},{24,28},{28,0},{1,5},{5... | collective-permute-start | bytes 417800 | tf_op jit(solution)/shard_map/ppermute | solution.py:30
  170.0 2.7 %fusion.12 = bf16[1,512,640]{2,1,0:T(8,128)(2,1)} fusion(bf16[512,640]{1,0:T(8,128)(2,1)} %collective-permute-done.10, bf16[256,512]{1,0:T(8,128)(2,1)S(1)} %get-tuple-element.16, bf16[256,512]{1,0:T(8,128)(2,1)} %get-tuple-element.36, bf16[256,640]{1,0:T(8,128)(2,1)} %get-tuple-element.22, bf16[256,640]{1,0:T(8,128)(2,1)S(1)} %get-tuple-element.8), kind=kOutput, calls=%fused_computation.18 | convolution fusion | flops 338886656 | bytes 2490368 | tf_op jit(solution)/shard_map/dot_general | solution.py:26
  172.7 5.0 %collective-permute-start.1 = (bf16[32,2176]{1,0:T(8,128)(2,1)S(1)}, bf16[32,2176]{1,0:T(8,128)(2,1)S(1)}, u32[]{:S(2)}, u32[]{:S(2)}) collective-permute-start(bf16[32,2176]{1,0:T(8,128)(2,1)S(1)} %get-tuple-element.23), channel_id=1, source_target_pairs={{0,28},{4,0},{8,4},{12,8},{16,12},{20,16},{24,20},{28,24},{1,29},{... | collective-permute-start | bytes 417800 | tf_op jit(solution)/shard_map/ppermute | solution.py:30
  177.8 2.1 %collective-permute-start.7 = (bf16[16,2176]{1,0:T(8,128)(2,1)S(1)}, bf16[16,2176]{1,0:T(8,128)(2,1)S(1)}, u32[]{:S(2)}, u32[]{:S(2)}) collective-permute-start(bf16[16,2176]{1,0:T(8,128)(2,1)S(1)} %slice.57), channel_id=1, source_target_pairs={{0,24},{4,28},{8,0},{12,4},{16,8},{20,12},{24,16},{28,20},{1,25},{... | collective-permute-start | bytes 208904 | tf_op jit(solution)/shard_map/ppermute | solution.py:30
  179.9 4.6 %collective-permute-start.6 = (bf16[16,2176]{1,0:T(8,128)(2,1)S(1)}, bf16[16,2176]{1,0:T(8,128)(2,1)S(1)}, u32[]{:S(2)}, u32[]{:S(2)}) collective-permute-start(bf16[16,2176]{1,0:T(8,128)(2,1)S(1)} %slice.56), channel_id=1, source_target_pairs={{0,8},{4,12},{8,16},{12,20},{16,24},{20,28},{24,0},{28,4},{1,9},{5... | collective-permute-start | bytes 208904 | tf_op jit(solution)/shard_map/ppermute | solution.py:30
  184.5 3.1 %collective-permute-start.5 = (bf16[32,2176]{1,0:T(8,128)(2,1)S(1)}, bf16[32,2176]{1,0:T(8,128)(2,1)S(1)}, u32[]{:S(2)}, u32[]{:S(2)}) collective-permute-start(bf16[32,2176]{1,0:T(8,128)(2,1)S(1)} %collective-permute-done.3), channel_id=1, source_target_pairs={{0,28},{4,0},{8,4},{12,8},{16,12},{20,16},{24,20},{28,24},{1,29},{... | collective-permute-start | bytes 417800 | tf_op jit(solution)/shard_map/ppermute | solution.py:30
  187.7 2.7 %collective-permute-start.4 = (bf16[32,2176]{1,0:T(8,128)(2,1)S(1)}, bf16[32,2176]{1,0:T(8,128)(2,1)S(1)}, u32[]{:S(2)}, u32[]{:S(2)}) collective-permute-start(bf16[32,2176]{1,0:T(8,128)(2,1)S(1)} %collective-permute-done.2), channel_id=1, source_target_pairs={{0,4},{4,8},{8,12},{12,16},{16,20},{20,24},{24,28},{28,0},{1,5},{5... | collective-permute-start | bytes 417800 | tf_op jit(solution)/shard_map/ppermute | solution.py:30
  190.5 5.3 %collective-permute-done.4 = bf16[32,2176]{1,0:T(8,128)(2,1)S(1)} collective-permute-done((bf16[32,2176]{1,0:T(8,128)(2,1)S(1)}, bf16[32,2176]{1,0:T(8,128)(2,1)S(1)}, u32[]{:S(2)}, u32[]{:S(2)}) %collective-permute-start.4) | collective-permute-done | bytes 139296 | tf_op jit(solution)/shard_map/ppermute | solution.py:30
  196.0 0.6 fusion.34
  196.5 0.1 slice_reduce_fusion
  196.6 1.1 slice.73
  197.8 0.5 fusion.56
  (46 shorter events, 0.3 us)
Async XLA Ops:
  0.6 72.7 %copy-start = (bf16[1,2048,640]{2,1,0:T(8,128)(2,1)S(1)}, bf16[1,2048,640]{2,1,0:T(8,128)(2,1)}, u32[]{:S(2)}) copy-start(bf16[1,2048,640]{2,1,0:T(8,128)(2,1)} %param.14) | copy-start | bytes 7864324
  0.6 3.3 %copy-start.9 = (bf16[256]{0:T(256)(128)(2,1)S(1)}, bf16[256]{0:T(256)(128)(2,1)}, u32[]{:S(2)}) copy-start(bf16[256]{0:T(256)(128)(2,1)} %param.10) | copy-start | bytes 1540
  0.7 3.3 %copy-start.1 = (bf16[256,2048]{1,0:T(8,128)(2,1)S(1)}, bf16[256,2048]{1,0:T(8,128)(2,1)}, u32[]{:S(2)}) copy-start(bf16[256,2048]{1,0:T(8,128)(2,1)} %param.8) | copy-start | bytes 3145732
  5.9 64.3 %all-to-all-start = ((bf16[32,8,4096]{2,1,0:T(8,128)(2,1)}), bf16[32,8,4096]{2,1,0:T(8,128)(2,1)}, u32[]{:S(2)}, u32[]{:S(2)}) async-start(bf16[32,8,4096]{2,1,0:T(8,128)(2,1)} %maximum_bitcast_fusion), calls=%async_computation | async-start | bytes 4194304 | tf_op jit(solution)/shard_map/all_to_all | solution.py:69
  73.4 2.4 %copy-start.10 = (bf16[1,640,2048]{2,1,0:T(8,128)(2,1)S(1)}, bf16[1,640,2048]{2,1,0:T(8,128)(2,1)}, u32[]{:S(2)}) copy-start(bf16[1,640,2048]{2,1,0:T(8,128)(2,1)} %param.15) | copy-start | bytes 7864324
  84.0 49.5 %all-to-all-start.1 = ((bf16[8,32,2176]{2,1,0:T(8,128)(2,1)}), bf16[8,32,2176]{2,1,0:T(8,128)(2,1)}, u32[]{:S(2)}, u32[]{:S(2)}) async-start(bf16[8,32,2176]{2,1,0:T(8,128)(2,1)} %bitcast.26), calls=%async_computation.1 | async-start | bytes 2228224 | tf_op jit(solution)/shard_map/all_to_all | solution.py:91
  107.6 2.1 %copy-start.2 = (bf16[256,640]{1,0:T(8,128)(2,1)S(1)}, bf16[256,640]{1,0:T(8,128)(2,1)}, u32[]{:S(2)}) copy-start(bf16[256,640]{1,0:T(8,128)(2,1)} %get-tuple-element.5) | copy-start | bytes 983044
  107.8 6.9 %collective-permute-start.8 = (bf16[256,2048]{1,0:T(8,128)(2,1)S(1)}, bf16[256,2048]{1,0:T(8,128)(2,1)S(1)}, u32[]{:S(2)}, u32[]{:S(2)}) collective-permute-start(bf16[256,2048]{1,0:T(8,128)(2,1)S(1)} %pad_maximum_fusion.1), channel_id=1, source_target_pairs={{0,1},{1,0},{2,3},{3,2},{4,5},{5,4},{6,7},{7,6},{8,9},{9,8},{10,11... | collective-permute-start | bytes 3145736 | tf_op jit(solution)/shard_map/ppermute | solution.py:34
  109.8 4.1 %collective-permute-start.9 = (bf16[256,1280]{1,0:T(8,128)(2,1)S(1)}, bf16[256,1280]{1,0:T(8,128)(2,1)S(1)}, u32[]{:S(2)}, u32[]{:S(2)}) collective-permute-start(bf16[256,1280]{1,0:T(8,128)(2,1)S(1)} %pad_maximum_fusion.2), channel_id=1, source_target_pairs={{0,1},{1,0},{2,3},{3,2},{4,5},{5,4},{6,7},{7,6},{8,9},{9,8},{10,11... | collective-permute-start | bytes 1966088 | tf_op jit(solution)/shard_map/ppermute | solution.py:34
  114.7 2.3 %copy-start.4 = (bf16[256,640]{1,0:T(8,128)(2,1)}, bf16[256,640]{1,0:T(8,128)(2,1)S(1)}, u32[]{:S(2)}) copy-start(bf16[256,640]{1,0:T(8,128)(2,1)S(1)} %get-tuple-element.21) | copy-start | bytes 983044
  116.9 36.0 %collective-permute-start.11 = (bf16[640,512]{1,0:T(8,128)(2,1)}, bf16[640,512]{1,0:T(8,128)(2,1)}, u32[]{:S(2)}, u32[]{:S(2)}) collective-permute-start(bf16[640,512]{1,0:T(8,128)(2,1)} %convolution_convert_fusion.2), channel_id=1, source_target_pairs={{0,2},{1,3},{2,0},{3,1},{4,6},{5,7},{6,4},{7,5},{8,10},{9,11},{10,... | collective-permute-start | bytes 1966088 | tf_op jit(solution)/shard_map/ppermute | solution.py:34
  135.6 25.4 %all-to-all-start.2 = ((bf16[32,2,1152]{2,1,0:T(2,128)(2,1)}), bf16[32,2,1152]{2,1,0:T(2,128)(2,1)S(1)}, u32[]{:S(2)}, u32[]{:S(2)}) async-start(bf16[32,2,1152]{2,1,0:T(2,128)(2,1)} %reshape.35), calls=%async_computation.2 | async-start | bytes 294912 | tf_op jit(solution)/shard_map/all_to_all | solution.py:96
  148.3 4.6 %copy-start.3 = (bf16[256,640]{1,0:T(8,128)(2,1)S(1)}, bf16[256,640]{1,0:T(8,128)(2,1)}, u32[]{:S(2)}) copy-start(bf16[256,640]{1,0:T(8,128)(2,1)} %get-tuple-element.5) | copy-start | bytes 983044
  148.3 4.6 %copy-start.5 = (bf16[256,640]{1,0:T(8,128)(2,1)S(1)}, bf16[256,640]{1,0:T(8,128)(2,1)}, u32[]{:S(2)}) copy-start(bf16[256,640]{1,0:T(8,128)(2,1)} %copy-done.4) | copy-start | bytes 983044
  148.3 4.6 %copy-start.6 = (bf16[256,512]{1,0:T(8,128)(2,1)S(1)}, bf16[256,512]{1,0:T(8,128)(2,1)}, u32[]{:S(2)}) copy-start(bf16[256,512]{1,0:T(8,128)(2,1)} %get-tuple-element.13) | copy-start | bytes 786436
  148.4 4.6 %copy-start.7 = (bf16[256,512]{1,0:T(8,128)(2,1)S(1)}, bf16[256,512]{1,0:T(8,128)(2,1)}, u32[]{:S(2)}) copy-start(bf16[256,512]{1,0:T(8,128)(2,1)} %get-tuple-element.9) | copy-start | bytes 786436
  151.0 18.9 %collective-permute-start.10 = (bf16[512,640]{1,0:T(8,128)(2,1)}, bf16[512,640]{1,0:T(8,128)(2,1)}, u32[]{:S(2)}, u32[]{:S(2)}) collective-permute-start(bf16[512,640]{1,0:T(8,128)(2,1)} %convolution_convert_fusion.3), channel_id=1, source_target_pairs={{0,2},{1,3},{2,0},{3,1},{4,6},{5,7},{6,4},{7,5},{8,10},{9,11},{10,... | collective-permute-start | bytes 1966088 | tf_op jit(solution)/shard_map/ppermute | solution.py:34
  161.1 16.7 %collective-permute-start.3 = (bf16[32,2176]{1,0:T(8,128)(2,1)S(1)}, bf16[32,2176]{1,0:T(8,128)(2,1)S(1)}, u32[]{:S(2)}, u32[]{:S(2)}) collective-permute-start(bf16[32,2176]{1,0:T(8,128)(2,1)S(1)} %get-tuple-element.23), channel_id=1, source_target_pairs={{0,24},{4,28},{8,0},{12,4},{16,8},{20,12},{24,16},{28,20},{1,25},{... | collective-permute-start | bytes 417800 | tf_op jit(solution)/shard_map/ppermute | solution.py:30
  163.2 16.7 %collective-permute-start.2 = (bf16[32,2176]{1,0:T(8,128)(2,1)S(1)}, bf16[32,2176]{1,0:T(8,128)(2,1)S(1)}, u32[]{:S(2)}, u32[]{:S(2)}) collective-permute-start(bf16[32,2176]{1,0:T(8,128)(2,1)S(1)} %get-tuple-element.23), channel_id=1, source_target_pairs={{0,8},{4,12},{8,16},{12,20},{16,24},{20,28},{24,0},{28,4},{1,9},{5... | collective-permute-start | bytes 417800 | tf_op jit(solution)/shard_map/ppermute | solution.py:30
  167.8 19.9 %collective-permute-start = (bf16[32,2176]{1,0:T(8,128)(2,1)S(1)}, bf16[32,2176]{1,0:T(8,128)(2,1)S(1)}, u32[]{:S(2)}, u32[]{:S(2)}) collective-permute-start(bf16[32,2176]{1,0:T(8,128)(2,1)S(1)} %get-tuple-element.23), channel_id=1, source_target_pairs={{0,4},{4,8},{8,12},{12,16},{16,20},{20,24},{24,28},{28,0},{1,5},{5... | collective-permute-start | bytes 417800 | tf_op jit(solution)/shard_map/ppermute | solution.py:30
  172.7 23.3 %copy-start.8 = (s32[256]{0:T(256)S(1)}, s32[256]{0:T(256)}, u32[]{:S(2)}) copy-start(s32[256]{0:T(256)} %param.11) | copy-start | bytes 3076
  172.7 17.7 %collective-permute-start.1 = (bf16[32,2176]{1,0:T(8,128)(2,1)S(1)}, bf16[32,2176]{1,0:T(8,128)(2,1)S(1)}, u32[]{:S(2)}, u32[]{:S(2)}) collective-permute-start(bf16[32,2176]{1,0:T(8,128)(2,1)S(1)} %get-tuple-element.23), channel_id=1, source_target_pairs={{0,28},{4,0},{8,4},{12,8},{16,12},{20,16},{24,20},{28,24},{1,29},{... | collective-permute-start | bytes 417800 | tf_op jit(solution)/shard_map/ppermute | solution.py:30
  177.8 18.2 %collective-permute-start.7 = (bf16[16,2176]{1,0:T(8,128)(2,1)S(1)}, bf16[16,2176]{1,0:T(8,128)(2,1)S(1)}, u32[]{:S(2)}, u32[]{:S(2)}) collective-permute-start(bf16[16,2176]{1,0:T(8,128)(2,1)S(1)} %slice.57), channel_id=1, source_target_pairs={{0,24},{4,28},{8,0},{12,4},{16,8},{20,12},{24,16},{28,20},{1,25},{... | collective-permute-start | bytes 208904 | tf_op jit(solution)/shard_map/ppermute | solution.py:30
  179.9 16.0 %collective-permute-start.6 = (bf16[16,2176]{1,0:T(8,128)(2,1)S(1)}, bf16[16,2176]{1,0:T(8,128)(2,1)S(1)}, u32[]{:S(2)}, u32[]{:S(2)}) collective-permute-start(bf16[16,2176]{1,0:T(8,128)(2,1)S(1)} %slice.56), channel_id=1, source_target_pairs={{0,8},{4,12},{8,16},{12,20},{16,24},{20,28},{24,0},{28,4},{1,9},{5... | collective-permute-start | bytes 208904 | tf_op jit(solution)/shard_map/ppermute | solution.py:30
  184.5 11.3 %collective-permute-start.5 = (bf16[32,2176]{1,0:T(8,128)(2,1)S(1)}, bf16[32,2176]{1,0:T(8,128)(2,1)S(1)}, u32[]{:S(2)}, u32[]{:S(2)}) collective-permute-start(bf16[32,2176]{1,0:T(8,128)(2,1)S(1)} %collective-permute-done.3), channel_id=1, source_target_pairs={{0,28},{4,0},{8,4},{12,8},{16,12},{20,16},{24,20},{28,24},{1,29},{... | collective-permute-start | bytes 417800 | tf_op jit(solution)/shard_map/ppermute | solution.py:30
  187.7 8.2 %collective-permute-start.4 = (bf16[32,2176]{1,0:T(8,128)(2,1)S(1)}, bf16[32,2176]{1,0:T(8,128)(2,1)S(1)}, u32[]{:S(2)}, u32[]{:S(2)}) collective-permute-start(bf16[32,2176]{1,0:T(8,128)(2,1)S(1)} %collective-permute-done.2), channel_id=1, source_target_pairs={{0,4},{4,8},{8,12},{12,16},{16,20},{20,24},{24,28},{28,0},{1,5},{5... | collective-permute-start | bytes 417800 | tf_op jit(solution)/shard_map/ppermute | solution.py:30

commit v2 on v1

v2 whole, which is shorter than its diff:
```python
import functools
import math

import jax
import jax.numpy as jnp
from jax import lax
from jax.experimental import pallas as pl
from jax.experimental.pallas import tpu as pltpu
from jax.sharding import PartitionSpec as P

CAP = 8
LANES = 128
MIB = 1 << 20
VMEM = pl.BlockSpec(memory_space=pltpu.VMEM)
ANY = pl.BlockSpec(memory_space=pl.ANY)
SMEM = pl.BlockSpec(memory_space=pltpu.SMEM)
BF16 = jnp.bfloat16
F32 = jnp.float32

root_two_pi = math.sqrt(2.0 / math.pi)


def gelu_pair(pre):
    inner = root_two_pi * (pre + 0.044715 * pre * pre * pre)
    tangent = jnp.tanh(inner)
    half = 0.5 * (1.0 + tangent)
    slope = half + 0.5 * pre * (1.0 - tangent * tangent) * root_two_pi * (
        1.0 + 3.0 * 0.044715 * pre * pre
    )
    return pre * half, slope


def dot(left, right, over_left, over_right):
    return lax.dot_general(
        left, right, (((over_left,), (over_right,)), ((), ())), preferred_element_type=F32
    )


def iota(shape, dim):
    return lax.broadcasted_iota(jnp.int32, shape, dim)


def params(mib):
    return pltpu.CompilerParams(vmem_limit_bytes=mib * MIB)


def cost(flops, moved):
    return pl.CostEstimate(flops=flops, bytes_accessed=moved, transcendentals=0)


def slot_hits(expert_ref, slot_ref, kept_ref, slots):
    position = jnp.where(kept_ref[...] == 1, expert_ref[...] * CAP + slot_ref[...], -1)
    return iota((slots, position.shape[1]), 0) == position


def dispatch_kernel(slots, expert_ref, slot_ref, kept_ref, gate_ref, tokens_ref, grad_ref, out_ref):
    step = pl.program_id(0)
    hits = slot_hits(expert_ref, slot_ref, kept_ref, slots)

    @pl.when(step < 4)
    def _():
        pick = jnp.where(hits, 1.0, 0.0).astype(BF16)
        out_ref[...] = dot(pick, tokens_ref[...], 1, 0).astype(BF16)

    @pl.when(step >= 4)
    def _():
        pick = jnp.where(hits, gate_ref[...], 0.0).astype(BF16)
        out_ref[...] = dot(pick, grad_ref[...], 1, 0).astype(BF16)


def dispatch(slots, index_rows, gate_row, tokens, grad_out):
    count, width = tokens.shape
    block = width // 4
    row = pl.BlockSpec((1, count), lambda i: (0, 0))
    return pl.pallas_call(
        functools.partial(dispatch_kernel, slots),
        grid=(8,),
        out_shape=jax.ShapeDtypeStruct((slots, 2 * width), BF16),
        in_specs=[row, row, row, row]
        + [
            pl.BlockSpec((count, block), lambda i: (0, jnp.minimum(i, 3))),
            pl.BlockSpec((count, block), lambda i: (0, jnp.maximum(i - 4, 0))),
        ],
        out_specs=pl.BlockSpec((slots, block), lambda i: (0, i)),
        compiler_params=params(56),
        cost_estimate=cost(4 * slots * count * width, 8 * slots * width),
    )(*index_rows, gate_row, tokens, grad_out)


def expert_kernel(data_ref, came, w_in, w_out, rows_ref, acts_ref, x_ref, s_ref, in_ref, out_ref, sems):
    slots, width = x_ref.shape
    hidden_width = in_ref.shape[1]
    quarter = width // 4
    copies = [
        pltpu.make_async_copy(came.at[:, :width], x_ref, sems.at[0]),
        pltpu.make_async_copy(w_in, in_ref, sems.at[1]),
        pltpu.make_async_copy(came.at[:, width:], s_ref, sems.at[2]),
        pltpu.make_async_copy(w_out, out_ref, sems.at[3]),
    ]
    for copy in copies:
        copy.start()
    copies[0].wait()
    copies[1].wait()
    pre = dot(x_ref[...], in_ref[...], 1, 0)
    value, slope = gelu_pair(pre)
    hidden = value.astype(BF16)
    acts_ref[:, width + hidden_width :] = hidden
    copies[2].wait()
    copies[3].wait()
    back = dot(s_ref[...], out_ref[...], 1, 1)
    grad_pre = (back * slope).astype(BF16)
    acts_ref[:, width : width + hidden_width] = grad_pre
    gate = jnp.sum(hidden.astype(F32) * back, axis=1, keepdims=True)
    same = iota((slots, slots), 0) == iota((slots, slots), 1)
    gate_row = jnp.sum(jnp.where(same, gate, 0.0), axis=0, keepdims=True)
    gate_rows = jnp.broadcast_to(gate_row, (16, slots)).astype(BF16)
    parts = rows_ref.shape[0]
    block = width // parts
    for part in range(parts):
        term = dot(grad_pre, in_ref[part * block : (part + 1) * block, :], 1, 1)
        rows_ref[part, :slots, :] = term.astype(BF16)
        rows_ref[part, slots:, :] = gate_rows
    for k, ref in enumerate((x_ref, x_ref, s_ref, s_ref)):
        index = data_ref[0] ^ (1, 3)[k % 2]
        place = pl.ds(pl.multiple_of(index * quarter, quarter), quarter)
        acts_ref[:, k * quarter : (k + 1) * quarter] = ref[:, place]


def expert(data, came, w_in, w_out, parts):
    slots = came.shape[0]
    width, hidden_width = w_in.shape
    return pl.pallas_call(
        expert_kernel,
        out_shape=(
            jax.ShapeDtypeStruct((parts, slots + 16, width // parts), BF16),
            jax.ShapeDtypeStruct((slots, width + 2 * hidden_width), BF16),
        ),
        in_specs=[SMEM, ANY, ANY, ANY],
        out_specs=(VMEM, VMEM),
        scratch_shapes=[
            pltpu.VMEM((slots, width), BF16),
            pltpu.VMEM((slots, width), BF16),
            pltpu.VMEM(w_in.shape, BF16),
            pltpu.VMEM(w_out.shape, BF16),
            pltpu.SemaphoreType.DMA((4,)),
        ],
        compiler_params=params(56),
        cost_estimate=cost(
            6 * slots * width * hidden_width, 4 * width * (slots + hidden_width) + 4 * slots * width
        ),
    )(data, came, w_in, w_out)


def sum_kernel(terms_ref, out_ref):
    slots = out_ref.shape[0]
    block = terms_ref.shape[2]
    total = terms_ref[0].astype(F32)
    for part in range(1, terms_ref.shape[0]):
        total = total + terms_ref[part].astype(F32)
    out_ref[:, :block] = total[:slots].astype(BF16)
    same = iota((slots, slots), 0) == iota((slots, slots), 1)
    gate = jnp.sum(jnp.where(same, total[slots : slots + 1], 0.0), axis=1, keepdims=True)
    out_ref[:, block:] = jnp.broadcast_to(gate, (slots, LANES)).astype(BF16)


def sum_terms(terms, slots):
    parts, _, block = terms.shape
    return pl.pallas_call(
        sum_kernel,
        out_shape=jax.ShapeDtypeStruct((slots, block + LANES), BF16),
        in_specs=[VMEM],
        out_specs=VMEM,
        compiler_params=params(56),
        cost_estimate=cost(parts * slots * block, 2 * parts * slots * block),
    )(terms)


def finish_kernel(me_ref, expert_ref, slot_ref, kept_ref, gate_ref, home_ref, *refs):
    same_ref, low_ref, high_ref, tokens_ref, gates_ref = refs
    slots, block = home_ref.shape[0], same_ref.shape[1]
    hits = slot_hits(expert_ref, slot_ref, kept_ref, slots)
    column = home_ref[:, block : block + 1].astype(F32)
    gates_ref[...] = jnp.sum(jnp.where(hits, column, 0.0), axis=0, keepdims=True) / gate_ref[...]
    choose = jnp.where(hits, 1.0, 0.0).T.astype(BF16)
    odd = me_ref[0] & 1

    def store(index, piece):
        place = pl.multiple_of(index * block, block)
        tokens_ref[:, pl.ds(place, block)] = dot(choose, piece, 1, 0).astype(BF16)

    for k in range(4):
        store(2 * k + odd, same_ref[k * slots : (k + 1) * slots, :])
    for k in range(2):
        store(2 * k + 1 - odd, low_ref[k * slots : (k + 1) * slots, :])
        store(2 * k + 5 - odd, high_ref[k * slots : (k + 1) * slots, :])


def finish(me, index_rows, gate_row, home, pieces, width):
    count = gate_row.shape[1]
    return pl.pallas_call(
        finish_kernel,
        out_shape=(
            jax.ShapeDtypeStruct((count, width), BF16),
            jax.ShapeDtypeStruct((1, count), F32),
        ),
        in_specs=[SMEM] + [VMEM] * (5 + len(pieces)),
        out_specs=(VMEM, VMEM),
        compiler_params=params(56),
        cost_estimate=cost(2 * count * count * width, 4 * count * width),
    )(me, *index_rows, gate_row, home, *pieces)


def weight_kernel(turn, place_ref, x_ref, s_ref, acts_ref, other_ref, *refs):
    added, (in_ref, out_ref) = refs[:-2], refs[-2:]
    quarter, width = in_ref.shape
    grads = slice(4 * quarter, 4 * quarter + width)
    hiddens = slice(4 * quarter + width, 4 * quarter + 2 * width)
    x_other = other_ref[:, turn * quarter : (turn + 1) * quarter]
    s_other = other_ref[:, (turn + 2) * quarter : (turn + 3) * quarter]
    first = dot(x_ref[...], acts_ref[:, grads], 0, 0) + dot(x_other, other_ref[:, grads], 0, 0)
    if added:
        first = first + added[0][...].astype(F32)
    in_ref[...] = first.astype(BF16)
    second = dot(acts_ref[:, hiddens], s_ref[...], 0, 0) + dot(other_ref[:, hiddens], s_other, 0, 0)
    if added:
        second = second + added[1][...].astype(F32)
    out_ref[...] = second.astype(BF16)


def weight_terms(turn, place, came, acts, other, added=()):
    slots = came.shape[0]
    quarter = came.shape[1] // 8
    width = (acts.shape[1] - 4 * quarter) // 2
    left = pl.BlockSpec((slots, quarter), lambda i, place: (0, place[0]))
    right = pl.BlockSpec((slots, quarter), lambda i, place: (0, place[0] + 4))
    whole = lambda shape: pl.BlockSpec(shape, lambda i, place: (0, 0))
    outs = ((quarter, width), (width, quarter))
    return pl.pallas_call(
        functools.partial(weight_kernel, turn),
        grid_spec=pltpu.PrefetchScalarGridSpec(
            num_scalar_prefetch=1,
            grid=(1,),
            in_specs=[left, right, whole(acts.shape), whole(acts.shape)]
            + [whole(a.shape) for a in added],
            out_specs=tuple(whole(shape) for shape in outs),
        ),
        out_shape=tuple(jax.ShapeDtypeStruct(shape, BF16) for shape in outs),
        compiler_params=params(56),
        cost_estimate=cost(8 * slots * quarter * width, 8 * slots * (quarter + width) + 4 * quarter * width),
    )(place, came, came, acts, other, *added)


def shift(value, step):
    return lax.ppermute(value, "mp", [(i, (i + step) % 8) for i in range(8)])


def swap(value, bit):
    return lax.ppermute(value, "dp", [(i, i ^ bit) for i in range(4)])


def gather_pieces(piece):
    same = lax.all_gather(
        piece, "mp", axis=0, tiled=True, axis_index_groups=[[0, 2, 4, 6], [1, 3, 5, 7]]
    )
    half = same.shape[0] // 2
    return same, shift(same[:half], 1), shift(same[half:], -1)


def scatter(value, axis):
    return lax.all_to_all(value, axis, split_axis=0, concat_axis=0, tiled=True)


def local(grad_out, tokens, gate, expert_index, slot, kept, w_in, w_out):
    experts = lax.axis_size("expert")
    parts = lax.axis_size("mp")
    count, width = tokens.shape
    slots = experts * CAP
    index_rows = [value.reshape(1, count) for value in (expert_index, slot, kept)]
    gate_row = gate.astype(F32).reshape(1, count)
    me = lax.axis_index("mp").astype(jnp.int32).reshape(1)
    data = lax.axis_index("dp").astype(jnp.int32).reshape(1)

    send = dispatch(slots, index_rows, gate_row, tokens, grad_out)
    came = scatter(send.reshape(experts, CAP, 2 * width), "expert").reshape(slots, 2 * width)
    rows, acts = expert(data, came, w_in[0], w_out[0], parts)
    terms = scatter(rows, "mp")

    other = swap(acts, 1)
    sends = weight_terms(1, data ^ 2, came, acts, other)
    added = [swap(value, 2) for value in sends]
    grad_w_in, grad_w_out = weight_terms(0, data, came, acts, other, added)

    total = sum_terms(terms, slots)
    home = scatter(total.reshape(experts, CAP, total.shape[1]), "expert").reshape(total.shape)
    home, (grad_w_in, grad_w_out) = lax.optimization_barrier((home, (grad_w_in, grad_w_out)))
    pieces = gather_pieces(home[:, : width // parts])
    grad_tokens, grad_gate = finish(me, index_rows, gate_row, home, pieces, width)
    return (grad_tokens, grad_gate.reshape(count).astype(BF16), grad_w_in[None], grad_w_out[None])


def solution(mesh):
    placed = (
        P(("expert", "dp"), None),
        P(("expert", "dp"), None),
        P(("expert", "dp")),
        P(("expert", "dp")),
        P(("expert", "dp")),
        P(("expert", "dp")),
        P("expert", None, "mp"),
        P("expert", "mp", None),
    )
    return jax.shard_map(
        local,
        mesh=mesh,
        in_specs=placed,
        out_specs=(
            P(("expert", "dp"), None),
            P(("expert", "dp")),
            P("expert", "dp", "mp"),
            P("expert", "mp", "dp"),
        ),
        check_vma=False,
    )
```

time: 199 us -> 195 us (0.980)
  the two profiles are of different devices: /device:TPU:2 before, /device:TPU:18 now
where the time goes in v2:
time: 195 us
  waiting for transfers between devices  80.1 us (41%)
  starting transfers between devices  62.8 us (32%)
  Pallas kernels  26.9 us (14%)
  blocking collectives  15.8 us (8%)
  local copies, waits for them, and re-layouts  5.96 us (3%)
  other arithmetic  2.43 us (1%)
    all_to_all x3, waiting for transfers between devices, scatter(): return lax.all_to_all(value, axis, split_axis=0, concat_axis=0, tiled=True)  74.5 us
    all_to_all x3, starting transfers between devices, scatter(): return lax.all_to_all(value, axis, split_axis=0, concat_axis=0, tiled=True)  45.2 us
    all_gather x1, blocking collectives, gather_pieces(): lax.all_gather(piece, 'mp', axis=0, tiled=True, axis_index_groups=[[0, 2,...  15.8 us
    ppermute x3, starting transfers between devices, swap(): return lax.ppermute(value, 'dp', [(i, i ^ bit) for i in range(4)])  11.8 us
    pallas_call x2, Pallas kernels, weight_terms(): pl.pallas_call(functools.partial(weight_kernel, turn), grid_spec=pltpu.Pr...  8.25 us
    pallas_call x1, Pallas kernels, expert(): pl.pallas_call(expert_kernel, out_shape=(jax.ShapeDtypeStruct((parts, slo...  7.14 us
    pallas_call x1, Pallas kernels, dispatch(): pl.pallas_call(functools.partial(dispatch_kernel, slots), grid=(8,), out_...  6.64 us
    unnamed x18, local copies, waits for them, and re-layouts  5.91 us
  transfers between devices with their start and end apart: 8, of which 5 were waited for; matrix products, arithmetic and copies ran while one was open for 0% of the time, Pallas kernels for 5%

profile of v2, /device:TPU:18, one launch (start us, length us, event | category | flops | bytes accessed | tf_op | source)
XLA Modules:
  0.0 194.8 jit_solution(15288614963969380707)
XLA Ops:
  0.6 1.2 reshape.53
  1.9 6.6 %shard_map.111 = bf16[256,4096]{1,0:T(8,128)(2,1)} custom-call(s32[1,256]{1,0:T(1,128)} %bitcast.23, s32[1,256]{1,0:T(1,128)} %bitcast.25, s32[1,256]{1,0:T(1,128)} %bitcast.27, f32[1,256]{1,0:T(1,128)} %bitcast.29, bf16[256,2048]{1,0:T(8,128)(2,1)} %tokens_ref.1, bf16[256,2048]{1,0:T(8,128)(2,1)} %grad_ref.1), custom_call_target="tpu_custom_call" | custom-call | flops 536870912 | bytes 4194304 | tf_op jit(solution)/shard_map/pallas_call | solution.py:75
  8.5 12.3 %all-to-all-start = ((bf16[32,8,4096]{2,1,0:T(8,128)(2,1)}), bf16[32,8,4096]{2,1,0:T(8,128)(2,1)S(1)}, u32[]{:S(2)}, u32[]{:S(2)}) async-start(bf16[32,8,4096]{2,1,0:T(8,128)(2,1)} %bitcast.19), calls=%async_computation | async-start | bytes 4194304 | tf_op jit(solution)/shard_map/all_to_all | solution.py:270
  20.8 51.2 %all-to-all-done = bf16[32,8,4096]{2,1,0:T(8,128)(2,1)S(1)} async-done(((bf16[32,8,4096]{2,1,0:T(8,128)(2,1)}), bf16[32,8,4096]{2,1,0:T(8,128)(2,1)S(1)}, u32[]{:S(2)}, u32[]{:S(2)}) %all-to-all-start) | async-done | bytes 2097184 | tf_op jit(solution)/shard_map/all_to_all | solution.py:270
  72.0 0.0 copy-start
  72.0 1.3 copy-done
  73.4 7.1 %shard_map.112 = (bf16[8,272,256]{2,1,0:T(8,128)(2,1)}, bf16[256,3328]{1,0:T(8,128)(2,1)}) custom-call(s32[1]{0:T(128)} %bitcast.5.data_ref.place_ref, bf16[256,4096]{1,0:T(8,128)(2,1)} %bitcast.14, bf16[2048,640]{1,0:T(8,128)(2,1)} %bitcast.31, bf16[640,2048]{1,0:T(8,128)(2,1)} %bitcast.32), custom_call_target="tpu_custom_call" | custom-call | flops 2013265920 | bytes 9437184 | tf_op jit(solution)/shard_map/pallas_call | solution.py:132
  80.5 1.9 collective-permute-start
  82.4 16.5 %all-to-all-start.1 = ((bf16[8,272,256]{2,1,0:T(8,128)(2,1)}), bf16[8,272,256]{2,1,0:T(8,128)(2,1)S(1)}, u32[]{:S(2)}, u32[]{:S(2)}) async-start(bf16[8,272,256]{2,1,0:T(8,128)(2,1)} %get-tuple-element.15), calls=%async_computation.1 | async-start | bytes 2228224 | tf_op jit(solution)/shard_map/all_to_all | solution.py:270
  98.9 0.0 collective-permute-done.other_ref
  98.9 0.0 copy-start.1
  98.9 1.2 copy-done.1
  100.2 4.0 %shard_map.114 = (bf16[512,640]{1,0:T(8,128)(2,1)}, bf16[640,512]{1,0:T(8,128)(2,1)}) custom-call(s32[1]{0:T(128)S(6)} %xor.3.place_ref, bf16[256,4096]{1,0:T(8,128)(2,1)} %bitcast.15, bf16[256,4096]{1,0:T(8,128)(2,1)} %bitcast.16, bf16[256,3328]{1,0:T(8,128)(2,1)} %get-tuple-element.16.acts_ref, bf16[256,3328]{1,0:T(8,128)(2,1)} %copy-done.1), custom_call_target="tpu_custom_call" | custom-call | flops 671088640 | bytes 3670016 | tf_op jit(solution)/shard_map/pallas_call | solution.py:238
  104.1 7.9 %collective-permute-start.1 = (bf16[512,640]{1,0:T(8,128)(2,1)}, bf16[512,640]{1,0:T(8,128)(2,1)S(1)}, u32[]{:S(2)}, u32[]{:S(2)}) collective-permute-start(bf16[512,640]{1,0:T(8,128)(2,1)} %get-tuple-element.17), channel_id=1, source_target_pairs={{0,2},{1,3},{2,0},{3,1},{4,6},{5,7},{6,4},{7,5},{8,10},{9,11},{10,... | collective-permute-start | bytes 1966088 | tf_op jit(solution)/shard_map/ppermute | solution.py:258
  112.1 1.9 collective-permute-start.2
  114.0 15.8 %all-to-all-done.1.terms_ref = bf16[8,272,256]{2,1,0:T(8,128)(2,1)S(1)} async-done(((bf16[8,272,256]{2,1,0:T(8,128)(2,1)}), bf16[8,272,256]{2,1,0:T(8,128)(2,1)S(1)}, u32[]{:S(2)}, u32[]{:S(2)}) %all-to-all-start.1) | async-done | bytes 1114144 | tf_op jit(solution)/shard_map/all_to_all | solution.py:270
  129.8 0.0 copy-start.3
  129.8 1.0 copy-done.3
  130.8 2.1 %shard_map.113 = bf16[256,384]{1,0:T(8,128)(2,1)} custom-call(bf16[8,272,256]{2,1,0:T(8,128)(2,1)} %copy-done.3), custom_call_target="tpu_custom_call" | custom-call | flops 524288 | bytes 1048576 | tf_op jit(solution)/shard_map/pallas_call | solution.py:168
  132.9 16.4 %all-to-all-start.2 = ((bf16[32,8,384]{2,1,0:T(8,128)(2,1)}), bf16[32,8,384]{2,1,0:T(8,128)(2,1)S(1)}, u32[]{:S(2)}, u32[]{:S(2)}) async-start(bf16[32,8,384]{2,1,0:T(8,128)(2,1)} %bitcast.22), calls=%async_computation.2 | async-start | bytes 393216 | tf_op jit(solution)/shard_map/all_to_all | solution.py:270
  149.4 0.0 collective-permute-done.1.refs_0_
  149.4 0.0 copy-start.5
  149.4 0.0 collective-permute-done.2.refs_1_
  149.4 0.8 copy-done.5
  150.2 0.0 copy-start.6
  150.2 0.8 copy-done.6
  151.1 4.3 %shard_map.115 = (bf16[512,640]{1,0:T(8,128)(2,1)}, bf16[640,512]{1,0:T(8,128)(2,1)}) custom-call(s32[1]{0:T(128)} %bitcast.5.data_ref.place_ref, bf16[256,4096]{1,0:T(8,128)(2,1)} %bitcast.17, bf16[256,4096]{1,0:T(8,128)(2,1)} %bitcast.18, bf16[256,3328]{1,0:T(8,128)(2,1)} %get-tuple-element.16.acts_ref, bf16[256,3328]{1,0:T(8,128)(2,1)} %copy-done.1, ...), custom_call_target="tpu_custom_call" | custom-call | flops 671088640 | bytes 3670016 | tf_op jit(solution)/shard_map/pallas_call | solution.py:238
  155.3 7.5 %all-to-all-done.2 = bf16[32,8,384]{2,1,0:T(8,128)(2,1)S(1)} async-done(((bf16[32,8,384]{2,1,0:T(8,128)(2,1)}), bf16[32,8,384]{2,1,0:T(8,128)(2,1)S(1)}, u32[]{:S(2)}, u32[]{:S(2)}) %all-to-all-start.2) | async-done | bytes 196640 | tf_op jit(solution)/shard_map/all_to_all | solution.py:270
  162.9 0.0 copy-start.4
  162.9 15.8 %all_gather.3.refs_0_ = bf16[1024,256]{1,0:T(8,128)(2,1)S(1)} all-gather(bf16[256,256]{1,0:T(8,128)(2,1)S(1)} %slice.9), channel_id=1, replica_groups={{0,8,16,24},{4,12,20,28},{1,9,17,25},{5,13,21,29},{2,10,18,26},{6,14,22..., dimensions={0}, use_global_device_ids=true | all-gather | bytes 655360 | tf_op jit(solution)/shard_map/all_gather | solution.py:262
  178.7 0.0 copy-start.2
  178.7 1.9 collective-permute-start.4
  180.6 3.9 %collective-permute-start.3 = (bf16[512,256]{1,0:T(8,128)(2,1)S(1)}, bf16[512,256]{1,0:T(8,128)(2,1)S(1)}, u32[]{:S(2)}, u32[]{:S(2)}) collective-permute-start(bf16[512,256]{1,0:T(8,128)(2,1)S(1)} %get-tuple-element.27), channel_id=1, source_target_pairs={{0,4},{4,8},{8,12},{12,16},{16,20},{20,24},{24,28},{28,0},{1,5},{5... | collective-permute-start | bytes 786440 | tf_op jit(solution)/shard_map/ppermute | solution.py:254
  184.6 2.4 %collective-permute-done.4.refs_2_ = bf16[512,256]{1,0:T(8,128)(2,1)S(1)} collective-permute-done((bf16[512,256]{1,0:T(8,128)(2,1)S(1)}, bf16[512,256]{1,0:T(8,128)(2,1)S(1)}, u32[]{:S(2)}, u32[]{:S(2)}) %collective-permute-start.4) | collective-permute-done | bytes 262176 | tf_op jit(solution)/shard_map/ppermute | solution.py:254
  187.0 0.0 copy-start.7
  187.0 3.1 %collective-permute-done.3.refs_1_ = bf16[512,256]{1,0:T(8,128)(2,1)S(1)} collective-permute-done((bf16[512,256]{1,0:T(8,128)(2,1)S(1)}, bf16[512,256]{1,0:T(8,128)(2,1)S(1)}, u32[]{:S(2)}, u32[]{:S(2)}) %collective-permute-start.3) | collective-permute-done | bytes 262176 | tf_op jit(solution)/shard_map/ppermute | solution.py:254
  190.1 0.0 copy-start.8
  190.1 0.0 copy-done.4
  190.1 0.0 copy-done.2
  190.1 0.0 copy-done.7
  190.1 0.7 copy-done.8
  190.8 2.8 %shard_map.116 = (bf16[256,2048]{1,0:T(8,128)(2,1)}, f32[1,256]{1,0:T(1,128)}) custom-call(s32[1]{0:T(128)} %bitcast.me_ref, s32[1,256]{1,0:T(1,128)} %bitcast.24, s32[1,256]{1,0:T(1,128)} %bitcast.26, s32[1,256]{1,0:T(1,128)} %bitcast.28, f32[1,256]{1,0:T(1,128)} %bitcast.30, bf16[256,384]{1,0:T(8,128)(2,1)} %bitcast.21, bf16[1024,256]{1,0:T(8,128)(2,1)} %copy-done.2, ...), custom_call_target="tpu_custom_call" | custom-call | flops 268435456 | bytes 2097152 | tf_op jit(solution)/shard_map/pallas_call | solution.py:200
  193.6 1.2 convert_reduce_fusion
  (2 shorter events, 0.0 us)
Async XLA Ops:
  8.5 63.5 %all-to-all-start = ((bf16[32,8,4096]{2,1,0:T(8,128)(2,1)}), bf16[32,8,4096]{2,1,0:T(8,128)(2,1)S(1)}, u32[]{:S(2)}, u32[]{:S(2)}) async-start(bf16[32,8,4096]{2,1,0:T(8,128)(2,1)} %bitcast.19), calls=%async_computation | async-start | bytes 4194304 | tf_op jit(solution)/shard_map/all_to_all | solution.py:270
  72.0 1.3 copy-start
  80.5 18.4 %collective-permute-start = (bf16[256,3328]{1,0:T(8,128)(2,1)}, bf16[256,3328]{1,0:T(8,128)(2,1)S(1)}, u32[]{:S(2)}, u32[]{:S(2)}) collective-permute-start(bf16[256,3328]{1,0:T(8,128)(2,1)} %get-tuple-element.16.acts_ref), channel_id=1, source_target_pairs={{0,1},{1,0},{2,3},{3,2},{4,5},{5,4},{6,7},{7,6},{8,9},{9,8},{10,11... | collective-permute-start | bytes 5111816 | tf_op jit(solution)/shard_map/ppermute | solution.py:258
  82.4 47.3 %all-to-all-start.1 = ((bf16[8,272,256]{2,1,0:T(8,128)(2,1)}), bf16[8,272,256]{2,1,0:T(8,128)(2,1)S(1)}, u32[]{:S(2)}, u32[]{:S(2)}) async-start(bf16[8,272,256]{2,1,0:T(8,128)(2,1)} %get-tuple-element.15), calls=%async_computation.1 | async-start | bytes 2228224 | tf_op jit(solution)/shard_map/all_to_all | solution.py:270
  98.9 1.2 copy-start.1
  104.1 45.2 %collective-permute-start.1 = (bf16[512,640]{1,0:T(8,128)(2,1)}, bf16[512,640]{1,0:T(8,128)(2,1)S(1)}, u32[]{:S(2)}, u32[]{:S(2)}) collective-permute-start(bf16[512,640]{1,0:T(8,128)(2,1)} %get-tuple-element.17), channel_id=1, source_target_pairs={{0,2},{1,3},{2,0},{3,1},{4,6},{5,7},{6,4},{7,5},{8,10},{9,11},{10,... | collective-permute-start | bytes 1966088 | tf_op jit(solution)/shard_map/ppermute | solution.py:258
  112.1 37.3 %collective-permute-start.2 = (bf16[640,512]{1,0:T(8,128)(2,1)}, bf16[640,512]{1,0:T(8,128)(2,1)S(1)}, u32[]{:S(2)}, u32[]{:S(2)}) collective-permute-start(bf16[640,512]{1,0:T(8,128)(2,1)} %get-tuple-element.18), channel_id=1, source_target_pairs={{0,2},{1,3},{2,0},{3,1},{4,6},{5,7},{6,4},{7,5},{8,10},{9,11},{10,... | collective-permute-start | bytes 1966088 | tf_op jit(solution)/shard_map/ppermute | solution.py:258
  129.8 1.0 copy-start.3
  132.9 29.9 %all-to-all-start.2 = ((bf16[32,8,384]{2,1,0:T(8,128)(2,1)}), bf16[32,8,384]{2,1,0:T(8,128)(2,1)S(1)}, u32[]{:S(2)}, u32[]{:S(2)}) async-start(bf16[32,8,384]{2,1,0:T(8,128)(2,1)} %bitcast.22), calls=%async_computation.2 | async-start | bytes 393216 | tf_op jit(solution)/shard_map/all_to_all | solution.py:270
  149.4 0.8 copy-start.5
  150.2 0.8 copy-start.6
  162.9 27.3 %copy-start.4 = (bf16[32,8,384]{2,1,0:T(8,128)(2,1)}, bf16[32,8,384]{2,1,0:T(8,128)(2,1)S(1)}, u32[]{:S(2)}) copy-start(bf16[32,8,384]{2,1,0:T(8,128)(2,1)S(1)} %all-to-all-done.2) | copy-start | bytes 589828
  178.7 11.5 %copy-start.2 = (bf16[1024,256]{1,0:T(8,128)(2,1)}, bf16[1024,256]{1,0:T(8,128)(2,1)S(1)}, u32[]{:S(2)}) copy-start(bf16[1024,256]{1,0:T(8,128)(2,1)S(1)} %all_gather.3.refs_0_) | copy-start | bytes 1572868
  178.7 8.3 %collective-permute-start.4 = (bf16[512,256]{1,0:T(8,128)(2,1)S(1)}, bf16[512,256]{1,0:T(8,128)(2,1)S(1)}, u32[]{:S(2)}, u32[]{:S(2)}) collective-permute-start(bf16[512,256]{1,0:T(8,128)(2,1)S(1)} %get-tuple-element.26), channel_id=1, source_target_pairs={{0,28},{4,0},{8,4},{12,8},{16,12},{20,16},{24,20},{28,24},{1,29},{... | collective-permute-start | bytes 786440 | tf_op jit(solution)/shard_map/ppermute | solution.py:254
  180.6 9.5 %collective-permute-start.3 = (bf16[512,256]{1,0:T(8,128)(2,1)S(1)}, bf16[512,256]{1,0:T(8,128)(2,1)S(1)}, u32[]{:S(2)}, u32[]{:S(2)}) collective-permute-start(bf16[512,256]{1,0:T(8,128)(2,1)S(1)} %get-tuple-element.27), channel_id=1, source_target_pairs={{0,4},{4,8},{8,12},{12,16},{16,20},{20,24},{24,28},{28,0},{1,5},{5... | collective-permute-start | bytes 786440 | tf_op jit(solution)/shard_map/ppermute | solution.py:254
  187.0 3.1 %copy-start.7 = (bf16[512,256]{1,0:T(8,128)(2,1)}, bf16[512,256]{1,0:T(8,128)(2,1)S(1)}, u32[]{:S(2)}) copy-start(bf16[512,256]{1,0:T(8,128)(2,1)S(1)} %collective-permute-done.4.refs_2_) | copy-start | bytes 786436
  190.1 0.7 copy-start.8

commit v3 on v2

v3 whole, which is shorter than its diff:
```python
import functools
import math

import jax
import jax.numpy as jnp
from jax import lax
from jax.experimental import pallas as pl
from jax.experimental.pallas import tpu as pltpu
from jax.sharding import PartitionSpec as P

CAP = 8
LANES = 128
MIB = 1 << 20
VMEM = pl.BlockSpec(memory_space=pltpu.VMEM)
ANY = pl.BlockSpec(memory_space=pl.ANY)
SMEM = pl.BlockSpec(memory_space=pltpu.SMEM)
BF16 = jnp.bfloat16
F32 = jnp.float32

root_two_pi = math.sqrt(2.0 / math.pi)


def gelu_pair(pre):
    inner = root_two_pi * (pre + 0.044715 * pre * pre * pre)
    tangent = jnp.tanh(inner)
    half = 0.5 * (1.0 + tangent)
    slope = half + 0.5 * pre * (1.0 - tangent * tangent) * root_two_pi * (
        1.0 + 3.0 * 0.044715 * pre * pre
    )
    return pre * half, slope


def dot(left, right, over_left, over_right):
    return lax.dot_general(
        left, right, (((over_left,), (over_right,)), ((), ())), preferred_element_type=F32
    )


def iota(shape, dim):
    return lax.broadcasted_iota(jnp.int32, shape, dim)


def params(mib):
    return pltpu.CompilerParams(vmem_limit_bytes=mib * MIB)


def cost(flops, moved):
    return pl.CostEstimate(flops=flops, bytes_accessed=moved, transcendentals=0)


def slot_hits(expert_ref, slot_ref, kept_ref, slots):
    position = jnp.where(kept_ref[...] == 1, expert_ref[...] * CAP + slot_ref[...], -1)
    return iota((slots, position.shape[1]), 0) == position


def dispatch_kernel(me_ref, expert_ref, slot_ref, kept_ref, gate_ref, tokens, grad_out, send_ref, x_ref, dy_ref, sems):
    rows, half = send_ref.shape
    loads = [
        pltpu.make_async_copy(tokens, x_ref, sems.at[0]),
        pltpu.make_async_copy(grad_out, dy_ref, sems.at[1]),
    ]
    for load in loads:
        load.start()
    position = jnp.where(kept_ref[...] == 1, expert_ref[...] * CAP + slot_ref[...], -1)
    shape = (rows, position.shape[1])
    row = iota(shape, 0)
    hits = (row & ~7) + (me_ref[0] & 3) + 4 * (row & 1) == position
    quarter = (row >> 1) & 3
    total = None
    for q, (ref, factor) in enumerate(
        ((x_ref, 1.0), (x_ref, 1.0), (dy_ref, gate_ref[...]), (dy_ref, gate_ref[...]))
    ):
        pick = jnp.where(hits & (quarter == q), factor, 0.0).astype(BF16)
        if q % 2 == 0:
            loads[q // 2].wait()
        low = (q % 2) * half
        term = dot(pick, ref[:, low : low + half], 1, 0)
        total = term if total is None else total + term
    send_ref[...] = total.astype(BF16)


def dispatch(me, slots, index_rows, gate_row, tokens, grad_out):
    count, width = tokens.shape
    return pl.pallas_call(
        dispatch_kernel,
        out_shape=jax.ShapeDtypeStruct((slots, width // 2), BF16),
        in_specs=[SMEM] + [VMEM] * 4 + [ANY] * 2,
        out_specs=VMEM,
        scratch_shapes=[
            pltpu.VMEM((count, width), BF16),
            pltpu.VMEM((count, width), BF16),
            pltpu.SemaphoreType.DMA((2,)),
        ],
        compiler_params=params(58),
        cost_estimate=cost(4 * slots * count * width, 5 * slots * width),
    )(me, *index_rows, gate_row, tokens, grad_out)


def expert_kernel(
    me_ref, data_ref, own, before, after, low, high, w_in, w_out, rows, acts, mine,
    packed, x_ref, s_ref, in_ref, out_ref, rows_ref, acts_ref, mine_ref, sems,
):
    slots, width = x_ref.shape
    hidden_width = in_ref.shape[1]
    quarter, half, part_rows = width // 4, slots // 2, slots // 4
    loads = [
        pltpu.make_async_copy(own, packed.at[0], sems.at[0]),
        pltpu.make_async_copy(before, packed.at[1], sems.at[1]),
        pltpu.make_async_copy(after, packed.at[2], sems.at[2]),
        pltpu.make_async_copy(low, packed.at[3, :half], sems.at[3]),
        pltpu.make_async_copy(high, packed.at[3, half:], sems.at[4]),
        pltpu.make_async_copy(w_in, in_ref, sems.at[5]),
        pltpu.make_async_copy(w_out, out_ref, sems.at[6]),
    ]
    for load in loads:
        load.start()
    square = (slots, slots)
    to, at = iota(square, 0), iota(square, 1)
    inner = to % part_rows
    unpack = jnp.where(at == (inner >> 1) * 8 + (to // part_rows) * 2 + (inner & 1), 1.0, 0.0).astype(BF16)
    for k, offset in enumerate((0, 3, 1, 2)):
        loads[k].wait()
        if k == 3:
            loads[4].wait()
        plain = dot(unpack, packed[k], 1, 0).astype(BF16)
        group = (me_ref[0] + offset) & 3
        place = pl.ds(pl.multiple_of(group * part_rows, part_rows), part_rows)
        for q, ref in enumerate((x_ref, x_ref, s_ref, s_ref)):
            first = (q % 2) * (width // 2)
            ref[place, first : first + width // 2] = plain[q * part_rows : (q + 1) * part_rows]
    loads[5].wait()
    pre = dot(x_ref[...], in_ref[...], 1, 0)
    value, slope = gelu_pair(pre)
    hidden = value.astype(BF16)
    acts_ref[:, width + hidden_width :] = hidden
    loads[6].wait()
    back = dot(s_ref[...], out_ref[...], 1, 1)
    grad_pre = (back * slope).astype(BF16)
    acts_ref[:, width : width + hidden_width] = grad_pre
    gate = jnp.sum(hidden.astype(F32) * back, axis=1, keepdims=True)
    gate_row = jnp.sum(jnp.where(to == at, gate, 0.0), axis=0, keepdims=True)
    gate_rows = jnp.broadcast_to(gate_row, (16, slots)).astype(BF16)
    parts = rows_ref.shape[0]
    block = width // parts
    stores = []
    for part in range(parts):
        term = dot(grad_pre, in_ref[part * block : (part + 1) * block, :], 1, 1)
        rows_ref[part, :slots, :] = term.astype(BF16)
        rows_ref[part, slots:, :] = gate_rows
        stores.append(pltpu.make_async_copy(rows_ref.at[part], rows.at[part], sems.at[7 + part]))
        stores[-1].start()
    for k, ref in enumerate((x_ref, x_ref, s_ref, s_ref)):
        for target, mask in ((mine_ref, (0, 2)[k % 2]), (acts_ref, (1, 3)[k % 2])):
            place = pl.ds(pl.multiple_of((data_ref[0] ^ mask) * quarter, quarter), quarter)
            target[:, k * quarter : (k + 1) * quarter] = ref[:, place]
    stores.append(pltpu.make_async_copy(acts_ref, acts, sems.at[7 + parts]))
    stores.append(pltpu.make_async_copy(mine_ref, mine, sems.at[8 + parts]))
    for store in stores[-2:]:
        store.start()
    for store in stores:
        store.wait()


def expert(me, data, packs, w_in, w_out, parts):
    slots = packs[0].shape[0]
    width, hidden_width = w_in.shape
    outs = (
        (parts, slots + 16, width // parts),
        (slots, width + 2 * hidden_width),
        (slots, width),
    )
    return pl.pallas_call(
        expert_kernel,
        out_shape=tuple(jax.ShapeDtypeStruct(shape, BF16) for shape in outs),
        in_specs=[SMEM, SMEM] + [ANY] * 7,
        out_specs=(ANY, ANY, ANY),
        scratch_shapes=[
            pltpu.VMEM((4, slots, width // 2), BF16),
            pltpu.VMEM((slots, width), BF16),
            pltpu.VMEM((slots, width), BF16),
            pltpu.VMEM(w_in.shape, BF16),
            pltpu.VMEM(w_out.shape, BF16),
        ]
        + [pltpu.VMEM(shape, BF16) for shape in outs]
        + [pltpu.SemaphoreType.DMA((9 + parts,))],
        compiler_params=params(59),
        cost_estimate=cost(
            6 * slots * width * hidden_width, 4 * width * (slots + hidden_width) + 8 * slots * width
        ),
    )(me, data, *packs, w_in, w_out)


def sum_kernel(terms_ref, out_ref):
    slots = out_ref.shape[0]
    block = terms_ref.shape[2]
    total = terms_ref[0].astype(F32)
    for part in range(1, terms_ref.shape[0]):
        total = total + terms_ref[part].astype(F32)
    to, at = iota((slots, slots), 0), iota((slots, slots), 1)
    from_row = (to & 3) * (slots // 4) + (to >> 3) * 2 + ((to >> 2) & 1)
    order = jnp.where(at == from_row, 1.0, 0.0)
    gate = jnp.sum(order * total[slots : slots + 1], axis=1, keepdims=True)
    sums = dot(order.astype(BF16), total[:slots].astype(BF16), 1, 0)
    out_ref[:, :block] = sums.astype(BF16)
    out_ref[:, block:] = jnp.broadcast_to(gate, (slots, LANES)).astype(BF16)


def sum_terms(terms, slots):
    parts, _, block = terms.shape
    return pl.pallas_call(
        sum_kernel,
        out_shape=jax.ShapeDtypeStruct((slots, block + LANES), BF16),
        in_specs=[VMEM],
        out_specs=VMEM,
        compiler_params=params(24),
        cost_estimate=cost(parts * slots * block, 2 * parts * slots * block),
    )(terms)


def finish_kernel(me_ref, expert_ref, slot_ref, kept_ref, gate_ref, home_ref, *refs):
    same_ref, low_ref, high_ref, tokens_ref, gates_ref = refs
    slots, block = home_ref.shape[0], same_ref.shape[1]
    hits = slot_hits(expert_ref, slot_ref, kept_ref, slots)
    column = home_ref[:, block : block + 1].astype(F32)
    gates_ref[...] = jnp.sum(jnp.where(hits, column, 0.0), axis=0, keepdims=True) / gate_ref[...]
    choose = jnp.where(hits, 1.0, 0.0).T.astype(BF16)
    odd = me_ref[0] & 1

    def store(index, piece):
        place = pl.multiple_of(index * block, block)
        tokens_ref[:, pl.ds(place, block)] = dot(choose, piece, 1, 0).astype(BF16)

    for k in range(4):
        store(2 * k + odd, same_ref[k * slots : (k + 1) * slots, :])
    for k in range(2):
        store(2 * k + 1 - odd, low_ref[k * slots : (k + 1) * slots, :])
        store(2 * k + 5 - odd, high_ref[k * slots : (k + 1) * slots, :])


def finish(me, index_rows, gate_row, home, pieces, width):
    count = gate_row.shape[1]
    return pl.pallas_call(
        finish_kernel,
        out_shape=(
            jax.ShapeDtypeStruct((count, width), BF16),
            jax.ShapeDtypeStruct((1, count), F32),
        ),
        in_specs=[SMEM] + [VMEM] * (5 + len(pieces)),
        out_specs=(VMEM, VMEM),
        compiler_params=params(24),
        cost_estimate=cost(2 * count * count * width, 4 * count * width),
    )(me, *index_rows, gate_row, home, *pieces)


def weight_kernel(turn, mine_ref, acts_ref, other_ref, *refs):
    added, (in_ref, out_ref) = refs[:-2], refs[-2:]
    quarter, width = in_ref.shape
    grads = slice(4 * quarter, 4 * quarter + width)
    hiddens = slice(4 * quarter + width, 4 * quarter + 2 * width)
    x_cols = slice(turn * quarter, (turn + 1) * quarter)
    s_cols = slice((turn + 2) * quarter, (turn + 3) * quarter)
    first = dot(mine_ref[:, x_cols], acts_ref[:, grads], 0, 0)
    first = first + dot(other_ref[:, x_cols], other_ref[:, grads], 0, 0)
    if added:
        first = first + added[0][...].astype(F32)
    in_ref[...] = first.astype(BF16)
    second = dot(acts_ref[:, hiddens], mine_ref[:, s_cols], 0, 0)
    second = second + dot(other_ref[:, hiddens], other_ref[:, s_cols], 0, 0)
    if added:
        second = second + added[1][...].astype(F32)
    out_ref[...] = second.astype(BF16)


def weight_terms(turn, mine, acts, other, added=()):
    slots = mine.shape[0]
    quarter = mine.shape[1] // 4
    width = (acts.shape[1] - 4 * quarter) // 2
    return pl.pallas_call(
        functools.partial(weight_kernel, turn),
        in_specs=[VMEM] * (3 + len(added)),
        out_specs=(VMEM, VMEM),
        out_shape=(
            jax.ShapeDtypeStruct((quarter, width), BF16),
            jax.ShapeDtypeStruct((width, quarter), BF16),
        ),
        compiler_params=params(24),
        cost_estimate=cost(8 * slots * quarter * width, 8 * slots * (quarter + width) + 4 * quarter * width),
    )(mine, acts, other, *added)


def shift(value, step):
    return lax.ppermute(value, "mp", [(i, (i + step) % 8) for i in range(8)])


def swap(value, bit):
    return lax.ppermute(value, "dp", [(i, i ^ bit) for i in range(4)])


def gather_pieces(piece):
    same = lax.all_gather(
        piece, "mp", axis=0, tiled=True, axis_index_groups=[[0, 2, 4, 6], [1, 3, 5, 7]]
    )
    half = same.shape[0] // 2
    return same, shift(same[:half], 1), shift(same[half:], -1)


def scatter(value, axis):
    return lax.all_to_all(value, axis, split_axis=0, concat_axis=0, tiled=True)


def local(grad_out, tokens, gate, expert_index, slot, kept, w_in, w_out):
    experts = lax.axis_size("expert")
    parts = lax.axis_size("mp")
    count, width = tokens.shape
    slots = experts * CAP
    index_rows = [value.reshape(1, count) for value in (expert_index, slot, kept)]
    gate_row = gate.astype(F32).reshape(1, count)
    me = lax.axis_index("mp").astype(jnp.int32).reshape(1)
    data = lax.axis_index("dp").astype(jnp.int32).reshape(1)

    send = dispatch(me, slots, index_rows, gate_row, tokens, grad_out)
    came = scatter(send.reshape(experts, CAP, width // 2), "expert").reshape(send.shape)
    packs = (came, shift(came, 1), shift(came, -1), shift(came[: slots // 2], 2), shift(came[slots // 2 :], -2))
    rows, acts, mine = expert(me, data, packs, w_in[0], w_out[0], parts)
    terms = scatter(rows, "mp")

    other = swap(acts, 1)
    added = [swap(value, 2) for value in weight_terms(1, mine, acts, other)]

    total = sum_terms(terms, slots)
    home = scatter(total.reshape(experts, CAP, total.shape[1]), "expert").reshape(total.shape)
    home, added = lax.optimization_barrier((home, added))
    grad_w_in, grad_w_out = weight_terms(0, mine, acts, other, added)
    pieces = gather_pieces(home[:, : width // parts])
    grad_tokens, grad_gate = finish(me, index_rows, gate_row, home, pieces, width)
    return (grad_tokens, grad_gate.reshape(count).astype(BF16), grad_w_in[None], grad_w_out[None])


def solution(mesh):
    placed = (
        P(("expert", "dp"), None),
        P(("expert", "dp"), None),
        P(("expert", "dp")),
        P(("expert", "dp")),
        P(("expert", "dp")),
        P(("expert", "dp")),
        P("expert", None, "mp"),
        P("expert", "mp", None),
    )
    return jax.shard_map(
        local,
        mesh=mesh,
        in_specs=placed,
        out_specs=(
            P(("expert", "dp"), None),
            P(("expert", "dp")),
            P("expert", "dp", "mp"),
            P("expert", "mp", "dp"),
        ),
        check_vma=False,
    )
```

time: 195 us -> 177 us (0.908)
  the two profiles are of different devices: /device:TPU:18 before, /device:TPU:2 now
where the time goes in v3:
time: 177 us; the launch traced here: 176 us
  blocking collectives  68.8 us (39%)
  starting transfers between devices  43.7 us (25%)
  waiting for transfers between devices  39.4 us (22%)
  Pallas kernels  19.2 us (11%)
  local copies, waits for them, and re-layouts  2.35 us (1%)
    all_to_all x2, blocking collectives, scatter(): return lax.all_to_all(value, axis, split_axis=0, concat_axis=0, tiled=True)  53.5 us
    ppermute x6, starting transfers between devices, shift(): return lax.ppermute(value, 'mp', [(i, (i + step) % 8) for i in range(8)])  31.6 us
    all_to_all x1, waiting for transfers between devices, scatter(): return lax.all_to_all(value, axis, split_axis=0, concat_axis=0, tiled=True)  22.2 us
    ppermute x6, waiting for transfers between devices, shift(): return lax.ppermute(value, 'mp', [(i, (i + step) % 8) for i in range(8)])  17.2 us
    all_gather x1, blocking collectives, gather_pieces(): lax.all_gather(piece, 'mp', axis=0, tiled=True, axis_index_groups=[[0, 2,...  15.3 us
    ppermute x3, starting transfers between devices, swap(): return lax.ppermute(value, 'dp', [(i, i ^ bit) for i in range(4)])  7.89 us
    pallas_call x1, Pallas kernels, expert(): pl.pallas_call(expert_kernel, out_shape=tuple((jax.ShapeDtypeStruct(shape...  7.68 us
    pallas_call x2, Pallas kernels, weight_terms(): pl.pallas_call(functools.partial(weight_kernel, turn), in_specs=[VMEM] *...  4.91 us
  transfers between devices with their start and end apart: 10, of which 4 were waited for; matrix products, arithmetic and copies ran while one was open for 0% of the time, Pallas kernels for 4%

profile of v3, /device:TPU:2, one launch (start us, length us, event | category | flops | bytes accessed | tf_op | source)
XLA Modules:
  0.0 176.2 jit_solution(15641171833517733382)
XLA Ops:
  0.6 1.2 reshape.55
  1.9 3.5 %shard_map.111 = bf16[256,1024]{1,0:T(8,128)(2,1)} custom-call(s32[1]{0:T(128)} %bitcast.me_ref, s32[1,256]{1,0:T(1,128)} %bitcast.21, s32[1,256]{1,0:T(1,128)} %bitcast.23, s32[1,256]{1,0:T(1,128)} %bitcast.25, f32[1,256]{1,0:T(1,128)} %bitcast.27, bf16[256,2048]{1,0:T(8,128)(2,1)} %tokens.1, bf16[256,2048]{1,0:T(8,128)(2,1)} %grad_out.1), custom_call_target="tpu_custom_call" | custom-call | flops 536870912 | bytes 2621440 | tf_op jit(solution)/shard_map/pallas_call | solution.py:84
  5.4 32.9 %all_to_all.15 = bf16[32,8,1024]{2,1,0:T(8,128)(2,1)S(1)} all-to-all(bf16[32,8,1024]{2,1,0:T(8,128)(2,1)} %bitcast.32), channel_id=1, replica_groups=mesh['expert'=32,'mp'=8,'dp'=4] {'expert'}, dimensions={0} | all-to-all | bytes 1048576 | tf_op jit(solution)/shard_map/all_to_all | solution.py:308
  38.3 17.1 %collective-permute-start.1 = (bf16[256,1024]{1,0:T(8,128)(2,1)S(1)}, bf16[256,1024]{1,0:T(8,128)(2,1)S(1)}, u32[]{:S(2)}, u32[]{:S(2)}) collective-permute-start(bf16[256,1024]{1,0:T(8,128)(2,1)S(1)} %bitcast.29), channel_id=1, source_target_pairs={{0,28},{4,0},{8,4},{12,8},{16,12},{20,16},{24,20},{28,24},{1,29},{... | collective-permute-start | bytes 1572872 | tf_op jit(solution)/shard_map/ppermute | solution.py:292
  55.4 1.9 %collective-permute-start = (bf16[256,1024]{1,0:T(8,128)(2,1)S(1)}, bf16[256,1024]{1,0:T(8,128)(2,1)S(1)}, u32[]{:S(2)}, u32[]{:S(2)}) collective-permute-start(bf16[256,1024]{1,0:T(8,128)(2,1)S(1)} %bitcast.30), channel_id=1, source_target_pairs={{0,4},{4,8},{8,12},{12,16},{16,20},{20,24},{24,28},{28,0},{1,5},{5... | collective-permute-start | bytes 1572872 | tf_op jit(solution)/shard_map/ppermute | solution.py:292
  57.4 3.4 %collective-permute-start.3 = (bf16[128,1024]{1,0:T(8,128)(2,1)S(1)}, bf16[128,1024]{1,0:T(8,128)(2,1)S(1)}, u32[]{:S(2)}, u32[]{:S(2)}) collective-permute-start(bf16[128,1024]{1,0:T(8,128)(2,1)S(1)} %get-tuple-element.30), channel_id=1, source_target_pairs={{0,24},{4,28},{8,0},{12,4},{16,8},{20,12},{24,16},{28,20},{1,25},{... | collective-permute-start | bytes 786440 | tf_op jit(solution)/shard_map/ppermute | solution.py:292
  60.8 3.4 %collective-permute-start.2 = (bf16[128,1024]{1,0:T(8,128)(2,1)S(1)}, bf16[128,1024]{1,0:T(8,128)(2,1)S(1)}, u32[]{:S(2)}, u32[]{:S(2)}) collective-permute-start(bf16[128,1024]{1,0:T(8,128)(2,1)S(1)} %get-tuple-element.31), channel_id=1, source_target_pairs={{0,8},{4,12},{8,16},{12,20},{16,24},{20,28},{24,0},{28,4},{1,9},{5... | collective-permute-start | bytes 786440 | tf_op jit(solution)/shard_map/ppermute | solution.py:292
  64.2 10.8 %collective-permute-done.3.high = bf16[128,1024]{1,0:T(8,128)(2,1)S(1)} collective-permute-done((bf16[128,1024]{1,0:T(8,128)(2,1)S(1)}, bf16[128,1024]{1,0:T(8,128)(2,1)S(1)}, u32[]{:S(2)}, u32[]{:S(2)}) %collective-permute-start.3) | collective-permute-done | bytes 262176 | tf_op jit(solution)/shard_map/ppermute | solution.py:292
  75.0 3.9 %collective-permute-done.2.low = bf16[128,1024]{1,0:T(8,128)(2,1)S(1)} collective-permute-done((bf16[128,1024]{1,0:T(8,128)(2,1)S(1)}, bf16[128,1024]{1,0:T(8,128)(2,1)S(1)}, u32[]{:S(2)}, u32[]{:S(2)}) %collective-permute-start.2) | collective-permute-done | bytes 262176 | tf_op jit(solution)/shard_map/ppermute | solution.py:292
  78.9 0.0 collective-permute-done.1.after
  78.9 0.0 collective-permute-done.before
  78.9 0.0 copy-start.9
  78.9 0.0 copy-done.7
  79.0 0.0 copy-done.10
  79.0 0.7 copy-done.11
  79.6 0.2 copy-done.8
  79.8 0.2 copy-done.9
  80.0 7.7 %shard_map.112 = (bf16[8,272,256]{2,1,0:T(8,128)(2,1)}, bf16[256,3328]{1,0:T(8,128)(2,1)}, bf16[256,2048]{1,0:T(8,128)(2,1)}) custom-call(s32[1]{0:T(128)} %bitcast.me_ref, s32[1]{0:T(128)} %bitcast.5.data_ref, bf16[256,1024]{1,0:T(8,128)(2,1)} %bitcast.31, bf16[256,1024]{1,0:T(8,128)(2,1)} %copy-done.9, bf16[256,1024]{1,0:T(8,128)(2,1)} %copy-done.8, ...), custom_call_target="tpu_custom_call" | custom-call | flops 2013265920 | bytes 11534336 | tf_op jit(solution)/shard_map/pallas_call | solution.py:172
  87.7 0.0 copy-start
  87.7 2.1 %collective-permute-start.4 = (bf16[256,3328]{1,0:T(8,128)(2,1)}, bf16[256,3328]{1,0:T(8,128)(2,1)S(1)}, u32[]{:S(2)}, u32[]{:S(2)}) collective-permute-start(bf16[256,3328]{1,0:T(8,128)(2,1)} %get-tuple-element.18.acts_ref), channel_id=1, source_target_pairs={{0,1},{1,0},{2,3},{3,2},{4,5},{5,4},{6,7},{7,6},{8,9},{9,8},{10,11... | collective-permute-start | bytes 5111816 | tf_op jit(solution)/shard_map/ppermute | solution.py:296
  89.7 4.3 %all-to-all-start.1 = ((bf16[8,272,256]{2,1,0:T(8,128)(2,1)}), bf16[8,272,256]{2,1,0:T(8,128)(2,1)}, u32[]{:S(2)}, u32[]{:S(2)}) async-start(bf16[8,272,256]{2,1,0:T(8,128)(2,1)} %get-tuple-element.16), calls=%async_computation.1 | async-start | bytes 2228224 | tf_op jit(solution)/shard_map/all_to_all | solution.py:308
  94.0 0.0 collective-permute-done.4.other_ref
  94.0 0.0 copy-done
  94.0 0.0 copy-start.1
  94.0 1.2 copy-done.1
  95.3 1.8 %shard_map.114 = (bf16[512,640]{1,0:T(8,128)(2,1)}, bf16[640,512]{1,0:T(8,128)(2,1)}) custom-call(bf16[256,2048]{1,0:T(8,128)(2,1)S(1)} %copy-done.1, bf16[256,3328]{1,0:T(8,128)(2,1)S(1)} %copy-done, bf16[256,3328]{1,0:T(8,128)(2,1)S(1)} %collective-permute-done.4.other_ref), custom_call_target="tpu_custom_call" | custom-call | flops 671088640 | bytes 3670016 | tf_op jit(solution)/shard_map/pallas_call | solution.py:278
  97.1 2.7 %collective-permute-start.5 = (bf16[512,640]{1,0:T(8,128)(2,1)}, bf16[512,640]{1,0:T(8,128)(2,1)}, u32[]{:S(2)}, u32[]{:S(2)}) collective-permute-start(bf16[512,640]{1,0:T(8,128)(2,1)} %get-tuple-element.19), channel_id=1, source_target_pairs={{0,2},{1,3},{2,0},{3,1},{4,6},{5,7},{6,4},{7,5},{8,10},{9,11},{10,... | collective-permute-start | bytes 1966088 | tf_op jit(solution)/shard_map/ppermute | solution.py:296
  99.8 3.1 %collective-permute-start.6 = (bf16[640,512]{1,0:T(8,128)(2,1)}, bf16[640,512]{1,0:T(8,128)(2,1)}, u32[]{:S(2)}, u32[]{:S(2)}) collective-permute-start(bf16[640,512]{1,0:T(8,128)(2,1)} %get-tuple-element.20), channel_id=1, source_target_pairs={{0,2},{1,3},{2,0},{3,1},{4,6},{5,7},{6,4},{7,5},{8,10},{9,11},{10,... | collective-permute-start | bytes 1966088 | tf_op jit(solution)/shard_map/ppermute | solution.py:296
  103.0 22.2 %all-to-all-done.1.terms_ref = bf16[8,272,256]{2,1,0:T(8,128)(2,1)} async-done(((bf16[8,272,256]{2,1,0:T(8,128)(2,1)}), bf16[8,272,256]{2,1,0:T(8,128)(2,1)}, u32[]{:S(2)}, u32[]{:S(2)}) %all-to-all-start.1) | async-done | bytes 1114144 | tf_op jit(solution)/shard_map/all_to_all | solution.py:308
  125.1 1.6 shard_map.113
  126.8 20.6 %all_to_all.16 = bf16[32,8,384]{2,1,0:T(8,128)(2,1)S(1)} all-to-all(bf16[32,8,384]{2,1,0:T(8,128)(2,1)S(1)} %bitcast.20), channel_id=1, replica_groups=mesh['expert'=32,'mp'=8,'dp'=4] {'expert'}, dimensions={0} | all-to-all | bytes 393216 | tf_op jit(solution)/shard_map/all_to_all | solution.py:308
  147.4 0.0 collective-permute-done.5.refs_0_
  147.4 0.0 collective-permute-done.6.refs_1_
  147.4 15.3 %all_gather.3.refs_0_ = bf16[1024,256]{1,0:T(8,128)(2,1)S(1)} all-gather(bf16[256,256]{1,0:T(8,128)(2,1)S(1)} %slice.25), channel_id=1, replica_groups={{0,8,16,24},{4,12,20,28},{1,9,17,25},{5,13,21,29},{2,10,18,26},{6,14,22..., dimensions={0}, use_global_device_ids=true | all-gather | bytes 655360 | tf_op jit(solution)/shard_map/all_gather | solution.py:300
  162.7 1.9 %collective-permute-start.8 = (bf16[512,256]{1,0:T(8,128)(2,1)S(1)}, bf16[512,256]{1,0:T(8,128)(2,1)S(1)}, u32[]{:S(2)}, u32[]{:S(2)}) collective-permute-start(bf16[512,256]{1,0:T(8,128)(2,1)S(1)} %get-tuple-element.28), channel_id=1, source_target_pairs={{0,28},{4,0},{8,4},{12,8},{16,12},{20,16},{24,20},{28,24},{1,29},{... | collective-permute-start | bytes 786440 | tf_op jit(solution)/shard_map/ppermute | solution.py:292
  164.7 0.0 copy-start.3
  164.7 0.0 copy-start.4
  164.7 0.0 copy-start.5
  164.7 0.0 copy-start.6
  164.7 3.9 %collective-permute-start.7 = (bf16[512,256]{1,0:T(8,128)(2,1)S(1)}, bf16[512,256]{1,0:T(8,128)(2,1)S(1)}, u32[]{:S(2)}, u32[]{:S(2)}) collective-permute-start(bf16[512,256]{1,0:T(8,128)(2,1)S(1)} %get-tuple-element.29), channel_id=1, source_target_pairs={{0,4},{4,8},{8,12},{12,16},{16,20},{20,24},{24,28},{28,0},{1,5},{5... | collective-permute-start | bytes 786440 | tf_op jit(solution)/shard_map/ppermute | solution.py:292
  168.6 0.0 copy-done.2
  168.7 3.1 %shard_map.116 = (bf16[512,640]{1,0:T(8,128)(2,1)}, bf16[640,512]{1,0:T(8,128)(2,1)}) custom-call(bf16[256,2048]{1,0:T(8,128)(2,1)S(1)} %copy-done.2, bf16[256,3328]{1,0:T(8,128)(2,1)S(1)} %copy-done, bf16[256,3328]{1,0:T(8,128)(2,1)S(1)} %collective-permute-done.4.other_ref, bf16[512,640]{1,0:T(8,128)(2,1)} %collective-permute-done.5.refs_0_, ...), custom_call_target="tpu_custom_call" | custom-call | flops 671088640 | bytes 3670016 | tf_op jit(solution)/shard_map/pallas_call | solution.py:278
  171.7 0.0 collective-permute-done.8.refs_2_
  171.7 2.5 %collective-permute-done.7.refs_1_ = bf16[512,256]{1,0:T(8,128)(2,1)S(1)} collective-permute-done((bf16[512,256]{1,0:T(8,128)(2,1)S(1)}, bf16[512,256]{1,0:T(8,128)(2,1)S(1)}, u32[]{:S(2)}, u32[]{:S(2)}) %collective-permute-start.7) | collective-permute-done | bytes 262176 | tf_op jit(solution)/shard_map/ppermute | solution.py:292
  174.2 0.0 copy-done.3
  174.2 0.0 copy-done.6
  174.2 1.5 shard_map.115
  175.7 0.5 convert_reduce_fusion
  (10 shorter events, 0.1 us)
Async XLA Ops:
  38.3 40.6 %copy-start.7 = (bf16[32,8,1024]{2,1,0:T(8,128)(2,1)}, bf16[32,8,1024]{2,1,0:T(8,128)(2,1)S(1)}, u32[]{:S(2)}) copy-start(bf16[32,8,1024]{2,1,0:T(8,128)(2,1)S(1)} %all_to_all.15) | copy-start | bytes 1572868
  38.3 40.6 %collective-permute-start.1 = (bf16[256,1024]{1,0:T(8,128)(2,1)S(1)}, bf16[256,1024]{1,0:T(8,128)(2,1)S(1)}, u32[]{:S(2)}, u32[]{:S(2)}) collective-permute-start(bf16[256,1024]{1,0:T(8,128)(2,1)S(1)} %bitcast.29), channel_id=1, source_target_pairs={{0,28},{4,0},{8,4},{12,8},{16,12},{20,16},{24,20},{28,24},{1,29},{... | collective-permute-start | bytes 1572872 | tf_op jit(solution)/shard_map/ppermute | solution.py:292
  55.4 23.5 %collective-permute-start = (bf16[256,1024]{1,0:T(8,128)(2,1)S(1)}, bf16[256,1024]{1,0:T(8,128)(2,1)S(1)}, u32[]{:S(2)}, u32[]{:S(2)}) collective-permute-start(bf16[256,1024]{1,0:T(8,128)(2,1)S(1)} %bitcast.30), channel_id=1, source_target_pairs={{0,4},{4,8},{8,12},{12,16},{16,20},{20,24},{24,28},{28,0},{1,5},{5... | collective-permute-start | bytes 1572872 | tf_op jit(solution)/shard_map/ppermute | solution.py:292
  57.4 17.6 %collective-permute-start.3 = (bf16[128,1024]{1,0:T(8,128)(2,1)S(1)}, bf16[128,1024]{1,0:T(8,128)(2,1)S(1)}, u32[]{:S(2)}, u32[]{:S(2)}) collective-permute-start(bf16[128,1024]{1,0:T(8,128)(2,1)S(1)} %get-tuple-element.30), channel_id=1, source_target_pairs={{0,24},{4,28},{8,0},{12,4},{16,8},{20,12},{24,16},{28,20},{1,25},{... | collective-permute-start | bytes 786440 | tf_op jit(solution)/shard_map/ppermute | solution.py:292
  60.8 18.1 %collective-permute-start.2 = (bf16[128,1024]{1,0:T(8,128)(2,1)S(1)}, bf16[128,1024]{1,0:T(8,128)(2,1)S(1)}, u32[]{:S(2)}, u32[]{:S(2)}) collective-permute-start(bf16[128,1024]{1,0:T(8,128)(2,1)S(1)} %get-tuple-element.31), channel_id=1, source_target_pairs={{0,8},{4,12},{8,16},{12,20},{16,24},{20,28},{24,0},{28,4},{1,9},{5... | collective-permute-start | bytes 786440 | tf_op jit(solution)/shard_map/ppermute | solution.py:292
  75.0 4.0 %copy-start.10 = (bf16[128,1024]{1,0:T(8,128)(2,1)}, bf16[128,1024]{1,0:T(8,128)(2,1)S(1)}, u32[]{:S(2)}) copy-start(bf16[128,1024]{1,0:T(8,128)(2,1)S(1)} %collective-permute-done.3.high) | copy-start | bytes 786436
  78.9 0.7 copy-start.11
  78.9 0.9 copy-start.8
  78.9 1.0 copy-start.9
  87.7 6.4 %copy-start = (bf16[256,3328]{1,0:T(8,128)(2,1)S(1)}, bf16[256,3328]{1,0:T(8,128)(2,1)}, u32[]{:S(2)}) copy-start(bf16[256,3328]{1,0:T(8,128)(2,1)} %get-tuple-element.18.acts_ref) | copy-start | bytes 5111812
  87.7 6.3 %collective-permute-start.4 = (bf16[256,3328]{1,0:T(8,128)(2,1)}, bf16[256,3328]{1,0:T(8,128)(2,1)S(1)}, u32[]{:S(2)}, u32[]{:S(2)}) collective-permute-start(bf16[256,3328]{1,0:T(8,128)(2,1)} %get-tuple-element.18.acts_ref), channel_id=1, source_target_pairs={{0,1},{1,0},{2,3},{3,2},{4,5},{5,4},{6,7},{7,6},{8,9},{9,8},{10,11... | collective-permute-start | bytes 5111816 | tf_op jit(solution)/shard_map/ppermute | solution.py:296
  89.7 35.4 %all-to-all-start.1 = ((bf16[8,272,256]{2,1,0:T(8,128)(2,1)}), bf16[8,272,256]{2,1,0:T(8,128)(2,1)}, u32[]{:S(2)}, u32[]{:S(2)}) async-start(bf16[8,272,256]{2,1,0:T(8,128)(2,1)} %get-tuple-element.16), calls=%async_computation.1 | async-start | bytes 2228224 | tf_op jit(solution)/shard_map/all_to_all | solution.py:308
  94.0 1.2 copy-start.1
  97.1 50.3 %collective-permute-start.5 = (bf16[512,640]{1,0:T(8,128)(2,1)}, bf16[512,640]{1,0:T(8,128)(2,1)}, u32[]{:S(2)}, u32[]{:S(2)}) collective-permute-start(bf16[512,640]{1,0:T(8,128)(2,1)} %get-tuple-element.19), channel_id=1, source_target_pairs={{0,2},{1,3},{2,0},{3,1},{4,6},{5,7},{6,4},{7,5},{8,10},{9,11},{10,... | collective-permute-start | bytes 1966088 | tf_op jit(solution)/shard_map/ppermute | solution.py:296
  99.8 47.5 %collective-permute-start.6 = (bf16[640,512]{1,0:T(8,128)(2,1)}, bf16[640,512]{1,0:T(8,128)(2,1)}, u32[]{:S(2)}, u32[]{:S(2)}) collective-permute-start(bf16[640,512]{1,0:T(8,128)(2,1)} %get-tuple-element.20), channel_id=1, source_target_pairs={{0,2},{1,3},{2,0},{3,1},{4,6},{5,7},{6,4},{7,5},{8,10},{9,11},{10,... | collective-permute-start | bytes 1966088 | tf_op jit(solution)/shard_map/ppermute | solution.py:296
  125.1 43.5 %copy-start.2 = (bf16[256,2048]{1,0:T(8,128)(2,1)S(1)}, bf16[256,2048]{1,0:T(8,128)(2,1)}, u32[]{:S(2)}) copy-start(bf16[256,2048]{1,0:T(8,128)(2,1)} %get-tuple-element.17.mine_ref) | copy-start | bytes 3145732
  162.7 9.0 %collective-permute-start.8 = (bf16[512,256]{1,0:T(8,128)(2,1)S(1)}, bf16[512,256]{1,0:T(8,128)(2,1)S(1)}, u32[]{:S(2)}, u32[]{:S(2)}) collective-permute-start(bf16[512,256]{1,0:T(8,128)(2,1)S(1)} %get-tuple-element.28), channel_id=1, source_target_pairs={{0,28},{4,0},{8,4},{12,8},{16,12},{20,16},{24,20},{28,24},{1,29},{... | collective-permute-start | bytes 786440 | tf_op jit(solution)/shard_map/ppermute | solution.py:292
  164.7 9.5 %copy-start.3 = (s32[256]{0:T(256)S(1)}, s32[256]{0:T(256)}, u32[]{:S(2)}) copy-start(s32[256]{0:T(256)} %param.11) | copy-start | bytes 3076
  164.7 9.5 %copy-start.4 = (s32[256]{0:T(256)S(1)}, s32[256]{0:T(256)}, u32[]{:S(2)}) copy-start(s32[256]{0:T(256)} %param.12) | copy-start | bytes 3076
  164.7 9.5 %copy-start.5 = (s32[256]{0:T(256)S(1)}, s32[256]{0:T(256)}, u32[]{:S(2)}) copy-start(s32[256]{0:T(256)} %param.13) | copy-start | bytes 3076
  164.7 9.5 %copy-start.6 = (f32[256]{0:T(256)S(1)}, f32[256]{0:T(256)}, u32[]{:S(2)}) copy-start(f32[256]{0:T(256)} %reshape.55) | copy-start | bytes 3076
  164.7 9.5 %collective-permute-start.7 = (bf16[512,256]{1,0:T(8,128)(2,1)S(1)}, bf16[512,256]{1,0:T(8,128)(2,1)S(1)}, u32[]{:S(2)}, u32[]{:S(2)}) collective-permute-start(bf16[512,256]{1,0:T(8,128)(2,1)S(1)} %get-tuple-element.29), channel_id=1, source_target_pairs={{0,4},{4,8},{8,12},{12,16},{16,20},{20,24},{24,28},{28,0},{1,5},{5... | collective-permute-start | bytes 786440 | tf_op jit(solution)/shard_map/ppermute | solution.py:292

commit v4 on v3

--- a/solution.py
+++ b/solution.py
@@ -15,6 +15,7 @@
 ANY = pl.BlockSpec(memory_space=pl.ANY)
 SMEM = pl.BlockSpec(memory_space=pltpu.SMEM)
 BF16 = jnp.bfloat16
+PARITIES = [[0, 2, 4, 6], [1, 3, 5, 7]]
 F32 = jnp.float32
 
 root_two_pi = math.sqrt(2.0 / math.pi)
@@ -66,9 +67,10 @@
     row = iota(shape, 0)
     hits = (row & ~7) + (me_ref[0] & 3) + 4 * (row & 1) == position
     quarter = (row >> 1) & 3
+    gate_row = gate_ref[...].astype(F32).reshape(1, -1)
     total = None
     for q, (ref, factor) in enumerate(
-        ((x_ref, 1.0), (x_ref, 1.0), (dy_ref, gate_ref[...]), (dy_ref, gate_ref[...]))
+        ((x_ref, 1.0), (x_ref, 1.0), (dy_ref, gate_row), (dy_ref, gate_row))
     ):
         pick = jnp.where(hits & (quarter == q), factor, 0.0).astype(BF16)
         if q % 2 == 0:
@@ -79,7 +81,7 @@
     send_ref[...] = total.astype(BF16)
 
 
-def dispatch(me, slots, index_rows, gate_row, tokens, grad_out):
+def dispatch(me, slots, index_rows, gate, tokens, grad_out):
     count, width = tokens.shape
     return pl.pallas_call(
         dispatch_kernel,
@@ -93,16 +95,17 @@
         ],
         compiler_params=params(58),
         cost_estimate=cost(4 * slots * count * width, 5 * slots * width),
-    )(me, *index_rows, gate_row, tokens, grad_out)
+    )(me, *index_rows, gate, tokens, grad_out)
 
 
 def expert_kernel(
-    me_ref, data_ref, own, before, after, low, high, w_in, w_out, rows, acts, mine,
+    me_ref, data_ref, own, before, after, low, high, w_in, w_out, same, first, second, acts, mine,
     packed, x_ref, s_ref, in_ref, out_ref, rows_ref, acts_ref, mine_ref, sems,
 ):
     slots, width = x_ref.shape
     hidden_width = in_ref.shape[1]
     quarter, half, part_rows = width // 4, slots // 2, slots // 4
+    parts = rows_ref.shape[0]
     loads = [
         pltpu.make_async_copy(own, packed.at[0], sems.at[0]),
         pltpu.make_async_copy(before, packed.at[1], sems.at[1]),
@@ -126,8 +129,17 @@
         group = (me_ref[0] + offset) & 3
         place = pl.ds(pl.multiple_of(group * part_rows, part_rows), part_rows)
         for q, ref in enumerate((x_ref, x_ref, s_ref, s_ref)):
-            first = (q % 2) * (width // 2)
-            ref[place, first : first + width // 2] = plain[q * part_rows : (q + 1) * part_rows]
+            start = (q % 2) * (width // 2)
+            ref[place, start : start + width // 2] = plain[q * part_rows : (q + 1) * part_rows]
+    for k, ref in enumerate((x_ref, x_ref, s_ref, s_ref)):
+        for target, mask in ((mine_ref, (0, 2)[k % 2]), (acts_ref, (1, 3)[k % 2])):
+            place = pl.ds(pl.multiple_of((data_ref[0] ^ mask) * quarter, quarter), quarter)
+            target[:, k * quarter : (k + 1) * quarter] = ref[:, place]
+    stores = [
+        pltpu.make_async_copy(mine_ref, mine, sems.at[7 + parts]),
+        pltpu.make_async_copy(acts_ref, acts, sems.at[8 + parts]),
+    ]
+    stores[0].start()
     loads[5].wait()
     pre = dot(x_ref[...], in_ref[...], 1, 0)
     value, slope = gelu_pair(pre)
@@ -137,26 +149,24 @@
     back = dot(s_ref[...], out_ref[...], 1, 1)
     grad_pre = (back * slope).astype(BF16)
     acts_ref[:, width : width + hidden_width] = grad_pre
+    stores[1].start()
     gate = jnp.sum(hidden.astype(F32) * back, axis=1, keepdims=True)
     gate_row = jnp.sum(jnp.where(to == at, gate, 0.0), axis=0, keepdims=True)
     gate_rows = jnp.broadcast_to(gate_row, (16, slots)).astype(BF16)
-    parts = rows_ref.shape[0]
     block = width // parts
-    stores = []
+    odd = me_ref[0] & 1
+    half_parts = parts // 2
     for part in range(parts):
-        term = dot(grad_pre, in_ref[part * block : (part + 1) * block, :], 1, 1)
-        rows_ref[part, :slots, :] = term.astype(BF16)
+        index = 2 * (part % half_parts) + (odd if part >= half_parts else 1 - odd)
+        place = pl.ds(pl.multiple_of(index * block, block), block)
+        rows_ref[part, :slots, :] = dot(grad_pre, in_ref[place, :], 1, 1).astype(BF16)
         rows_ref[part, slots:, :] = gate_rows
-        stores.append(pltpu.make_async_copy(rows_ref.at[part], rows.at[part], sems.at[7 + part]))
+        if part >= half_parts:
+            target = same.at[part - half_parts]
+        else:
+            target = (first, second)[part // 2].at[part % 2]
+        stores.append(pltpu.make_async_copy(rows_ref.at[part], target, sems.at[7 + part]))
         stores[-1].start()
-    for k, ref in enumerate((x_ref, x_ref, s_ref, s_ref)):
-        for target, mask in ((mine_ref, (0, 2)[k % 2]), (acts_ref, (1, 3)[k % 2])):
-            place = pl.ds(pl.multiple_of((data_ref[0] ^ mask) * quarter, quarter), quarter)
-            target[:, k * quarter : (k + 1) * quarter] = ref[:, place]
-    stores.append(pltpu.make_async_copy(acts_ref, acts, sems.at[7 + parts]))
-    stores.append(pltpu.make_async_copy(mine_ref, mine, sems.at[8 + parts]))
-    for store in stores[-2:]:
-        store.start()
     for store in stores:
         store.wait()
 
@@ -164,8 +174,11 @@
 def expert(me, data, packs, w_in, w_out, parts):
     slots = packs[0].shape[0]
     width, hidden_width = w_in.shape
+    rows = (slots + 16, width // parts)
     outs = (
-        (parts, slots + 16, width // parts),
+        (parts // 2,) + rows,
+        (2,) + rows,
+        (2,) + rows,
         (slots, width + 2 * hidden_width),
         (slots, width),
     )
@@ -173,7 +186,7 @@
         expert_kernel,
         out_shape=tuple(jax.ShapeDtypeStruct(shape, BF16) for shape in outs),
         in_specs=[SMEM, SMEM] + [ANY] * 7,
-        out_specs=(ANY, ANY, ANY),
+        out_specs=(ANY,) * 5,
         scratch_shapes=[
             pltpu.VMEM((4, slots, width // 2), BF16),
             pltpu.VMEM((slots, width), BF16),
@@ -181,13 +194,30 @@
             pltpu.VMEM(w_in.shape, BF16),
             pltpu.VMEM(w_out.shape, BF16),
         ]
-        + [pltpu.VMEM(shape, BF16) for shape in outs]
+        + [pltpu.VMEM(shape, BF16) for shape in ((parts,) + rows,) + outs[3:]]
         + [pltpu.SemaphoreType.DMA((9 + parts,))],
         compiler_params=params(59),
         cost_estimate=cost(
             6 * slots * width * hidden_width, 4 * width * (slots + hidden_width) + 8 * slots * width
         ),
     )(me, data, *packs, w_in, w_out)
+
+
+def add_kernel(same_ref, first_ref, second_ref, out_ref):
+    for k in range(4):
+        other = (first_ref, second_ref)[k // 2]
+        out_ref[k] = (same_ref[k].astype(F32) + other[k % 2].astype(F32)).astype(BF16)
+
+
+def add_terms(same, first, second):
+    return pl.pallas_call(
+        add_kernel,
+        out_shape=jax.ShapeDtypeStruct(same.shape, BF16),
+        in_specs=[VMEM] * 3,
+        out_specs=VMEM,
+        compiler_params=params(24),
+        cost_estimate=cost(same.size, 6 * same.size),
+    )(same, first, second)
 
 
 def sum_kernel(terms_ref, out_ref):
@@ -222,7 +252,9 @@
     slots, block = home_ref.shape[0], same_ref.shape[1]
     hits = slot_hits(expert_ref, slot_ref, kept_ref, slots)
     column = home_ref[:, block : block + 1].astype(F32)
-    gates_ref[...] = jnp.sum(jnp.where(hits, column, 0.0), axis=0, keepdims=True) / gate_ref[...]
+    picked = jnp.sum(jnp.where(hits, column, 0.0), axis=0, keepdims=True)
+    gate_row = gate_ref[...].astype(F32).reshape(1, -1)
+    gates_ref[...] = (picked / gate_row).astype(BF16).reshape(-1)
     choose = jnp.where(hits, 1.0, 0.0).T.astype(BF16)
     odd = me_ref[0] & 1
 
@@ -237,19 +269,19 @@
         store(2 * k + 5 - odd, high_ref[k * slots : (k + 1) * slots, :])
 
 
-def finish(me, index_rows, gate_row, home, pieces, width):
-    count = gate_row.shape[1]
+def finish(me, index_rows, gate, home, pieces, width):
+    count = gate.shape[0]
     return pl.pallas_call(
         finish_kernel,
         out_shape=(
             jax.ShapeDtypeStruct((count, width), BF16),
-            jax.ShapeDtypeStruct((1, count), F32),
+            jax.ShapeDtypeStruct((count,), BF16),
         ),
         in_specs=[SMEM] + [VMEM] * (5 + len(pieces)),
         out_specs=(VMEM, VMEM),
         compiler_params=params(24),
         cost_estimate=cost(2 * count * count * width, 4 * count * width),
-    )(me, *index_rows, gate_row, home, *pieces)
+    )(me, *index_rows, gate, home, *pieces)
 
 
 def weight_kernel(turn, mine_ref, acts_ref, other_ref, *refs):
@@ -298,7 +330,7 @@
 
 def gather_pieces(piece):
     same = lax.all_gather(
-        piece, "mp", axis=0, tiled=True, axis_index_groups=[[0, 2, 4, 6], [1, 3, 5, 7]]
+        piece, "mp", axis=0, tiled=True, axis_index_groups=PARITIES
     )
     half = same.shape[0] // 2
     return same, shift(same[:half], 1), shift(same[half:], -1)
@@ -314,15 +346,15 @@
     count, width = tokens.shape
     slots = experts * CAP
     index_rows = [value.reshape(1, count) for value in (expert_index, slot, kept)]
-    gate_row = gate.astype(F32).reshape(1, count)
     me = lax.axis_index("mp").astype(jnp.int32).reshape(1)
     data = lax.axis_index("dp").astype(jnp.int32).reshape(1)
 
-    send = dispatch(me, slots, index_rows, gate_row, tokens, grad_out)
+    send = dispatch(me, slots, index_rows, gate, tokens, grad_out)
     came = scatter(send.reshape(experts, CAP, width // 2), "expert").reshape(send.shape)
     packs = (came, shift(came, 1), shift(came, -1), shift(came[: slots // 2], 2), shift(came[slots // 2 :], -2))
-    rows, acts, mine = expert(me, data, packs, w_in[0], w_out[0], parts)
-    terms = scatter(rows, "mp")
+    same, first, second, acts, mine = expert(me, data, packs, w_in[0], w_out[0], parts)
+    pairs = add_terms(same, shift(first, 1), shift(second, -1))
+    terms = lax.all_to_all(pairs, "mp", 0, 0, axis_index_groups=PARITIES, tiled=True)
 
     other = swap(acts, 1)
     added = [swap(value, 2) for value in weight_terms(1, mine, acts, other)]
@@ -332,8 +364,8 @@
     home, added = lax.optimization_barrier((home, added))
     grad_w_in, grad_w_out = weight_terms(0, mine, acts, other, added)
     pieces = gather_pieces(home[:, : width // parts])
-    grad_tokens, grad_gate = finish(me, index_rows, gate_row, home, pieces, width)
-    return (grad_tokens, grad_gate.reshape(count).astype(BF16), grad_w_in[None], grad_w_out[None])
+    grad_tokens, grad_gate = finish(me, index_rows, gate, home, pieces, width)
+    return (grad_tokens, grad_gate, grad_w_in[None], grad_w_out[None])
 
 
 def solution(mesh):

time: 177 us -> 184 us (1.040)
  the two profiles are of different devices: /device:TPU:2 before, /device:TPU:16 now
where the time goes in v4:
time: 184 us; the launch traced here: 183 us
  blocking collectives  74.4 us (40%)
  starting transfers between devices  51 us (28%)
  waiting for transfers between devices  34.6 us (19%)
  Pallas kernels  18.2 us (10%)
  local copies, waits for them, and re-layouts  4.26 us (2%)
    all_to_all x2, blocking collectives, scatter(): return lax.all_to_all(value, axis, split_axis=0, concat_axis=0, tiled=True)  56.5 us
    ppermute x8, starting transfers between devices, shift(): return lax.ppermute(value, 'mp', [(i, (i + step) % 8) for i in range(8)])  39 us
    ppermute x8, waiting for transfers between devices, shift(): return lax.ppermute(value, 'mp', [(i, (i + step) % 8) for i in range(8)])  27.7 us
    all_gather x1, blocking collectives, gather_pieces(): lax.all_gather(piece, 'mp', axis=0, tiled=True, axis_index_groups=PARITIES)  18 us
    ppermute x3, starting transfers between devices, swap(): return lax.ppermute(value, 'dp', [(i, i ^ bit) for i in range(4)])  7.89 us
    all_to_all x1, waiting for transfers between devices, local(): lax.all_to_all(pairs, 'mp', 0, 0, axis_index_groups=PARITIES, tiled=True)  6.87 us
    pallas_call x1, Pallas kernels, expert(): pl.pallas_call(expert_kernel, out_shape=tuple((jax.ShapeDtypeStruct(shape...  6.82 us
    pallas_call x2, Pallas kernels, weight_terms(): pl.pallas_call(functools.partial(weight_kernel, turn), in_specs=[VMEM] *...  4.91 us
  transfers between devices with their start and end apart: 12, of which 6 were waited for; matrix products, arithmetic and copies ran while one was open for 0% of the time, Pallas kernels for 4%

profile of v4, /device:TPU:16, one launch (start us, length us, event | category | flops | bytes accessed | tf_op | source)
XLA Modules:
  0.0 183.4 jit_solution(18220290045675710653)
XLA Ops:
  0.6 3.5 %shard_map.111 = bf16[256,1024]{1,0:T(8,128)(2,1)} custom-call(s32[1]{0:T(128)} %bitcast.me_ref, s32[1,256]{1,0:T(1,128)} %bitcast.20, s32[1,256]{1,0:T(1,128)} %bitcast.22, s32[1,256]{1,0:T(1,128)} %bitcast.24, bf16[256]{0:T(256)(128)(2,1)} %gate_ref.3, bf16[256,2048]{1,0:T(8,128)(2,1)} %tokens.1, bf16[256,2048]{1,0:T(8,128)(2,1)} %grad_out.1), custom_call_target="tpu_custom_call" | custom-call | flops 536870912 | bytes 2621440 | tf_op jit(solution)/shard_map/pallas_call | solution.py:86
  4.2 30.8 %all_to_all.15 = bf16[32,8,1024]{2,1,0:T(8,128)(2,1)S(1)} all-to-all(bf16[32,8,1024]{2,1,0:T(8,128)(2,1)} %bitcast.26), channel_id=1, replica_groups=mesh['expert'=32,'mp'=8,'dp'=4] {'expert'}, dimensions={0} | all-to-all | bytes 1048576 | tf_op jit(solution)/shard_map/all_to_all | solution.py:340
  34.9 17.3 %collective-permute-start.1 = (bf16[256,1024]{1,0:T(8,128)(2,1)S(1)}, bf16[256,1024]{1,0:T(8,128)(2,1)S(1)}, u32[]{:S(2)}, u32[]{:S(2)}) collective-permute-start(bf16[256,1024]{1,0:T(8,128)(2,1)S(1)} %bitcast.27), channel_id=1, source_target_pairs={{0,28},{4,0},{8,4},{12,8},{16,12},{20,16},{24,20},{28,24},{1,29},{... | collective-permute-start | bytes 1572872 | tf_op jit(solution)/shard_map/ppermute | solution.py:324
  52.2 1.9 %collective-permute-start = (bf16[256,1024]{1,0:T(8,128)(2,1)S(1)}, bf16[256,1024]{1,0:T(8,128)(2,1)S(1)}, u32[]{:S(2)}, u32[]{:S(2)}) collective-permute-start(bf16[256,1024]{1,0:T(8,128)(2,1)S(1)} %bitcast.28), channel_id=1, source_target_pairs={{0,4},{4,8},{8,12},{12,16},{16,20},{20,24},{24,28},{28,0},{1,5},{5... | collective-permute-start | bytes 1572872 | tf_op jit(solution)/shard_map/ppermute | solution.py:324
  54.2 3.4 %collective-permute-start.3 = (bf16[128,1024]{1,0:T(8,128)(2,1)S(1)}, bf16[128,1024]{1,0:T(8,128)(2,1)S(1)}, u32[]{:S(2)}, u32[]{:S(2)}) collective-permute-start(bf16[128,1024]{1,0:T(8,128)(2,1)S(1)} %get-tuple-element.34), channel_id=1, source_target_pairs={{0,24},{4,28},{8,0},{12,4},{16,8},{20,12},{24,16},{28,20},{1,25},{... | collective-permute-start | bytes 786440 | tf_op jit(solution)/shard_map/ppermute | solution.py:324
  57.5 3.4 %collective-permute-start.2 = (bf16[128,1024]{1,0:T(8,128)(2,1)S(1)}, bf16[128,1024]{1,0:T(8,128)(2,1)S(1)}, u32[]{:S(2)}, u32[]{:S(2)}) collective-permute-start(bf16[128,1024]{1,0:T(8,128)(2,1)S(1)} %get-tuple-element.35), channel_id=1, source_target_pairs={{0,8},{4,12},{8,16},{12,20},{16,24},{20,28},{24,0},{28,4},{1,9},{5... | collective-permute-start | bytes 786440 | tf_op jit(solution)/shard_map/ppermute | solution.py:324
  60.9 11.7 %collective-permute-done.3.high = bf16[128,1024]{1,0:T(8,128)(2,1)S(1)} collective-permute-done((bf16[128,1024]{1,0:T(8,128)(2,1)S(1)}, bf16[128,1024]{1,0:T(8,128)(2,1)S(1)}, u32[]{:S(2)}, u32[]{:S(2)}) %collective-permute-start.3) | collective-permute-done | bytes 262176 | tf_op jit(solution)/shard_map/ppermute | solution.py:324
  72.6 3.9 %collective-permute-done.2.low = bf16[128,1024]{1,0:T(8,128)(2,1)S(1)} collective-permute-done((bf16[128,1024]{1,0:T(8,128)(2,1)S(1)}, bf16[128,1024]{1,0:T(8,128)(2,1)S(1)}, u32[]{:S(2)}, u32[]{:S(2)}) %collective-permute-start.2) | collective-permute-done | bytes 262176 | tf_op jit(solution)/shard_map/ppermute | solution.py:324
  76.5 0.0 collective-permute-done.1.after
  76.5 0.0 collective-permute-done.before
  76.6 0.0 copy-start.11
  76.6 0.0 copy-done.9
  76.6 0.0 copy-done.12
  76.6 0.7 copy-done.13
  77.3 0.2 copy-done.10
  77.4 0.2 copy-done.11
  77.6 6.8 %shard_map.112 = (bf16[4,272,256]{2,1,0:T(8,128)(2,1)}, bf16[2,272,256]{2,1,0:T(8,128)(2,1)}, bf16[2,272,256]{2,1,0:T(8,128)(2,1)}, bf16[256,3328]{1,0:T(8,128)(2,1)}, bf16[256,2048]{1,0:T(8,128)(2,1)}) custom-call(s32[1]{0:T(128)} %bitcast.me_ref, s32[1]{0:T(128)} %bitcast.4.data_ref, bf16[256,1024]{1,0:T(8,128)(2,1)} %bitcast.29, ...), custom_call_target="tpu_custom_call" | custom-call | flops 2013265920 | bytes 11534336 | tf_op jit(solution)/shard_map/pallas_call | solution.py:185
  84.5 2.1 %collective-permute-start.6 = (bf16[256,3328]{1,0:T(8,128)(2,1)}, bf16[256,3328]{1,0:T(8,128)(2,1)S(1)}, u32[]{:S(2)}, u32[]{:S(2)}) collective-permute-start(bf16[256,3328]{1,0:T(8,128)(2,1)} %get-tuple-element.22.acts_ref), channel_id=1, source_target_pairs={{0,1},{1,0},{2,3},{3,2},{4,5},{5,4},{6,7},{7,6},{8,9},{9,8},{10,11... | collective-permute-start | bytes 5111816 | tf_op jit(solution)/shard_map/ppermute | solution.py:328
  86.5 4.8 %collective-permute-start.4 = (bf16[2,272,256]{2,1,0:T(8,128)(2,1)}, bf16[2,272,256]{2,1,0:T(8,128)(2,1)S(1)}, u32[]{:S(2)}, u32[]{:S(2)}) collective-permute-start(bf16[2,272,256]{2,1,0:T(8,128)(2,1)} %get-tuple-element.19), channel_id=1, source_target_pairs={{0,4},{4,8},{8,12},{12,16},{16,20},{20,24},{24,28},{28,0},{1,5},{5... | collective-permute-start | bytes 835592 | tf_op jit(solution)/shard_map/ppermute | solution.py:324
  91.3 2.3 %collective-permute-start.5 = (bf16[2,272,256]{2,1,0:T(8,128)(2,1)}, bf16[2,272,256]{2,1,0:T(8,128)(2,1)S(1)}, u32[]{:S(2)}, u32[]{:S(2)}) collective-permute-start(bf16[2,272,256]{2,1,0:T(8,128)(2,1)} %get-tuple-element.20), channel_id=1, source_target_pairs={{0,28},{4,0},{8,4},{12,8},{16,12},{20,16},{24,20},{28,24},{1,29},{... | collective-permute-start | bytes 835592 | tf_op jit(solution)/shard_map/ppermute | solution.py:324
  93.6 5.3 %collective-permute-done.4.first_ref = bf16[2,272,256]{2,1,0:T(8,128)(2,1)S(1)} collective-permute-done((bf16[2,272,256]{2,1,0:T(8,128)(2,1)}, bf16[2,272,256]{2,1,0:T(8,128)(2,1)S(1)}, u32[]{:S(2)}, u32[]{:S(2)}) %collective-permute-start.4) | collective-permute-done | bytes 278560 | tf_op jit(solution)/shard_map/ppermute | solution.py:324
  98.9 3.3 %collective-permute-done.5.second_ref = bf16[2,272,256]{2,1,0:T(8,128)(2,1)S(1)} collective-permute-done((bf16[2,272,256]{2,1,0:T(8,128)(2,1)}, bf16[2,272,256]{2,1,0:T(8,128)(2,1)S(1)}, u32[]{:S(2)}, u32[]{:S(2)}) %collective-permute-start.5) | collective-permute-done | bytes 278560 | tf_op jit(solution)/shard_map/ppermute | solution.py:324
  102.2 1.1 copy-done.4
  103.2 0.1 shard_map.113
  103.4 0.8 copy-done.3
  104.2 4.1 %all-to-all-start.1 = ((bf16[4,272,256]{2,1,0:T(8,128)(2,1)}), bf16[4,272,256]{2,1,0:T(8,128)(2,1)}, u32[]{:S(2)}, u32[]{:S(2)}) async-start(bf16[4,272,256]{2,1,0:T(8,128)(2,1)} %copy-done.3), calls=%async_computation.1 | async-start | bytes 1114112 | tf_op jit(solution)/shard_map/all_to_all | solution.py:357
  108.3 0.0 collective-permute-done.6.other_ref
  108.4 0.0 copy-start.1
  108.4 1.2 copy-done.1
  109.6 1.8 %shard_map.115 = (bf16[512,640]{1,0:T(8,128)(2,1)}, bf16[640,512]{1,0:T(8,128)(2,1)}) custom-call(bf16[256,2048]{1,0:T(8,128)(2,1)S(1)} %copy-done.1, bf16[256,3328]{1,0:T(8,128)(2,1)S(1)} %copy-done, bf16[256,3328]{1,0:T(8,128)(2,1)S(1)} %collective-permute-done.6.other_ref), custom_call_target="tpu_custom_call" | custom-call | flops 671088640 | bytes 3670016 | tf_op jit(solution)/shard_map/pallas_call | solution.py:310
  111.4 3.4 %collective-permute-start.7 = (bf16[512,640]{1,0:T(8,128)(2,1)}, bf16[512,640]{1,0:T(8,128)(2,1)}, u32[]{:S(2)}, u32[]{:S(2)}) collective-permute-start(bf16[512,640]{1,0:T(8,128)(2,1)} %get-tuple-element.23), channel_id=1, source_target_pairs={{0,2},{1,3},{2,0},{3,1},{4,6},{5,7},{6,4},{7,5},{8,10},{9,11},{10,... | collective-permute-start | bytes 1966088 | tf_op jit(solution)/shard_map/ppermute | solution.py:328
  114.8 2.5 %collective-permute-start.8 = (bf16[640,512]{1,0:T(8,128)(2,1)}, bf16[640,512]{1,0:T(8,128)(2,1)}, u32[]{:S(2)}, u32[]{:S(2)}) collective-permute-start(bf16[640,512]{1,0:T(8,128)(2,1)} %get-tuple-element.24), channel_id=1, source_target_pairs={{0,2},{1,3},{2,0},{3,1},{4,6},{5,7},{6,4},{7,5},{8,10},{9,11},{10,... | collective-permute-start | bytes 1966088 | tf_op jit(solution)/shard_map/ppermute | solution.py:328
  117.3 6.9 %all-to-all-done.1.terms_ref = bf16[4,272,256]{2,1,0:T(8,128)(2,1)} async-done(((bf16[4,272,256]{2,1,0:T(8,128)(2,1)}), bf16[4,272,256]{2,1,0:T(8,128)(2,1)}, u32[]{:S(2)}, u32[]{:S(2)}) %all-to-all-start.1) | async-done | bytes 557088 | tf_op jit(solution)/shard_map/all_to_all | solution.py:357
  124.2 1.4 shard_map.114
  125.5 25.7 %all_to_all.16 = bf16[32,8,384]{2,1,0:T(8,128)(2,1)S(1)} all-to-all(bf16[32,8,384]{2,1,0:T(8,128)(2,1)S(1)} %bitcast.19), channel_id=1, replica_groups=mesh['expert'=32,'mp'=8,'dp'=4] {'expert'}, dimensions={0} | all-to-all | bytes 393216 | tf_op jit(solution)/shard_map/all_to_all | solution.py:340
  151.3 0.0 collective-permute-done.7.refs_0_
  151.3 0.0 collective-permute-done.8.refs_1_
  151.3 18.0 %all_gather.3.refs_0_ = bf16[1024,256]{1,0:T(8,128)(2,1)S(1)} all-gather(bf16[256,256]{1,0:T(8,128)(2,1)S(1)} %slice.25), channel_id=1, replica_groups={{0,8,16,24},{4,12,20,28},{1,9,17,25},{5,13,21,29},{2,10,18,26},{6,14,22..., dimensions={0}, use_global_device_ids=true | all-gather | bytes 655360 | tf_op jit(solution)/shard_map/all_gather | solution.py:332
  169.3 3.0 %collective-permute-start.10 = (bf16[512,256]{1,0:T(8,128)(2,1)S(1)}, bf16[512,256]{1,0:T(8,128)(2,1)S(1)}, u32[]{:S(2)}, u32[]{:S(2)}) collective-permute-start(bf16[512,256]{1,0:T(8,128)(2,1)S(1)} %get-tuple-element.32), channel_id=1, source_target_pairs={{0,28},{4,0},{8,4},{12,8},{16,12},{20,16},{24,20},{28,24},{1,29},{... | collective-permute-start | bytes 786440 | tf_op jit(solution)/shard_map/ppermute | solution.py:324
  172.3 0.0 copy-start.5
  172.3 0.0 copy-start.6
  172.3 0.0 copy-start.7
  172.3 0.0 copy-start.8
  172.3 3.0 %collective-permute-start.9 = (bf16[512,256]{1,0:T(8,128)(2,1)S(1)}, bf16[512,256]{1,0:T(8,128)(2,1)S(1)}, u32[]{:S(2)}, u32[]{:S(2)}) collective-permute-start(bf16[512,256]{1,0:T(8,128)(2,1)S(1)} %get-tuple-element.33), channel_id=1, source_target_pairs={{0,4},{4,8},{8,12},{12,16},{16,20},{20,24},{24,28},{28,0},{1,5},{5... | collective-permute-start | bytes 786440 | tf_op jit(solution)/shard_map/ppermute | solution.py:324
  175.3 3.1 %shard_map.117 = (bf16[512,640]{1,0:T(8,128)(2,1)}, bf16[640,512]{1,0:T(8,128)(2,1)}) custom-call(bf16[256,2048]{1,0:T(8,128)(2,1)S(1)} %copy-done.2, bf16[256,3328]{1,0:T(8,128)(2,1)S(1)} %copy-done, bf16[256,3328]{1,0:T(8,128)(2,1)S(1)} %collective-permute-done.6.other_ref, bf16[512,640]{1,0:T(8,128)(2,1)} %collective-permute-done.7.refs_0_, ...), custom_call_target="tpu_custom_call" | custom-call | flops 671088640 | bytes 3670016 | tf_op jit(solution)/shard_map/pallas_call | solution.py:310
  178.4 0.0 collective-permute-done.10.refs_2_
  178.4 3.5 %collective-permute-done.9.refs_1_ = bf16[512,256]{1,0:T(8,128)(2,1)S(1)} collective-permute-done((bf16[512,256]{1,0:T(8,128)(2,1)S(1)}, bf16[512,256]{1,0:T(8,128)(2,1)S(1)}, u32[]{:S(2)}, u32[]{:S(2)}) %collective-permute-start.9) | collective-permute-done | bytes 262176 | tf_op jit(solution)/shard_map/ppermute | solution.py:324
  181.9 1.5 shard_map.116
  (17 shorter events, 0.1 us)
Async XLA Ops:
  34.9 41.6 %copy-start.9 = (bf16[32,8,1024]{2,1,0:T(8,128)(2,1)}, bf16[32,8,1024]{2,1,0:T(8,128)(2,1)S(1)}, u32[]{:S(2)}) copy-start(bf16[32,8,1024]{2,1,0:T(8,128)(2,1)S(1)} %all_to_all.15) | copy-start | bytes 1572868
  34.9 41.6 %collective-permute-start.1 = (bf16[256,1024]{1,0:T(8,128)(2,1)S(1)}, bf16[256,1024]{1,0:T(8,128)(2,1)S(1)}, u32[]{:S(2)}, u32[]{:S(2)}) collective-permute-start(bf16[256,1024]{1,0:T(8,128)(2,1)S(1)} %bitcast.27), channel_id=1, source_target_pairs={{0,28},{4,0},{8,4},{12,8},{16,12},{20,16},{24,20},{28,24},{1,29},{... | collective-permute-start | bytes 1572872 | tf_op jit(solution)/shard_map/ppermute | solution.py:324
  52.2 24.4 %collective-permute-start = (bf16[256,1024]{1,0:T(8,128)(2,1)S(1)}, bf16[256,1024]{1,0:T(8,128)(2,1)S(1)}, u32[]{:S(2)}, u32[]{:S(2)}) collective-permute-start(bf16[256,1024]{1,0:T(8,128)(2,1)S(1)} %bitcast.28), channel_id=1, source_target_pairs={{0,4},{4,8},{8,12},{12,16},{16,20},{20,24},{24,28},{28,0},{1,5},{5... | collective-permute-start | bytes 1572872 | tf_op jit(solution)/shard_map/ppermute | solution.py:324
  54.2 18.4 %collective-permute-start.3 = (bf16[128,1024]{1,0:T(8,128)(2,1)S(1)}, bf16[128,1024]{1,0:T(8,128)(2,1)S(1)}, u32[]{:S(2)}, u32[]{:S(2)}) collective-permute-start(bf16[128,1024]{1,0:T(8,128)(2,1)S(1)} %get-tuple-element.34), channel_id=1, source_target_pairs={{0,24},{4,28},{8,0},{12,4},{16,8},{20,12},{24,16},{28,20},{1,25},{... | collective-permute-start | bytes 786440 | tf_op jit(solution)/shard_map/ppermute | solution.py:324
  57.5 19.0 %collective-permute-start.2 = (bf16[128,1024]{1,0:T(8,128)(2,1)S(1)}, bf16[128,1024]{1,0:T(8,128)(2,1)S(1)}, u32[]{:S(2)}, u32[]{:S(2)}) collective-permute-start(bf16[128,1024]{1,0:T(8,128)(2,1)S(1)} %get-tuple-element.35), channel_id=1, source_target_pairs={{0,8},{4,12},{8,16},{12,20},{16,24},{20,28},{24,0},{28,4},{1,9},{5... | collective-permute-start | bytes 786440 | tf_op jit(solution)/shard_map/ppermute | solution.py:324
  72.6 4.0 %copy-start.12 = (bf16[128,1024]{1,0:T(8,128)(2,1)}, bf16[128,1024]{1,0:T(8,128)(2,1)S(1)}, u32[]{:S(2)}) copy-start(bf16[128,1024]{1,0:T(8,128)(2,1)S(1)} %collective-permute-done.3.high) | copy-start | bytes 786436
  76.5 0.7 copy-start.13
  76.5 0.9 copy-start.10
  76.6 1.1 copy-start.11
  84.5 23.9 %copy-start = (bf16[256,3328]{1,0:T(8,128)(2,1)S(1)}, bf16[256,3328]{1,0:T(8,128)(2,1)}, u32[]{:S(2)}) copy-start(bf16[256,3328]{1,0:T(8,128)(2,1)} %get-tuple-element.22.acts_ref) | copy-start | bytes 5111812
  84.5 23.9 %collective-permute-start.6 = (bf16[256,3328]{1,0:T(8,128)(2,1)}, bf16[256,3328]{1,0:T(8,128)(2,1)S(1)}, u32[]{:S(2)}, u32[]{:S(2)}) collective-permute-start(bf16[256,3328]{1,0:T(8,128)(2,1)} %get-tuple-element.22.acts_ref), channel_id=1, source_target_pairs={{0,1},{1,0},{2,3},{3,2},{4,5},{5,4},{6,7},{7,6},{8,9},{9,8},{10,11... | collective-permute-start | bytes 5111816 | tf_op jit(solution)/shard_map/ppermute | solution.py:328
  86.5 12.4 %collective-permute-start.4 = (bf16[2,272,256]{2,1,0:T(8,128)(2,1)}, bf16[2,272,256]{2,1,0:T(8,128)(2,1)S(1)}, u32[]{:S(2)}, u32[]{:S(2)}) collective-permute-start(bf16[2,272,256]{2,1,0:T(8,128)(2,1)} %get-tuple-element.19), channel_id=1, source_target_pairs={{0,4},{4,8},{8,12},{12,16},{16,20},{20,24},{24,28},{28,0},{1,5},{5... | collective-permute-start | bytes 835592 | tf_op jit(solution)/shard_map/ppermute | solution.py:324
  91.3 10.9 %collective-permute-start.5 = (bf16[2,272,256]{2,1,0:T(8,128)(2,1)}, bf16[2,272,256]{2,1,0:T(8,128)(2,1)S(1)}, u32[]{:S(2)}, u32[]{:S(2)}) collective-permute-start(bf16[2,272,256]{2,1,0:T(8,128)(2,1)} %get-tuple-element.20), channel_id=1, source_target_pairs={{0,28},{4,0},{8,4},{12,8},{16,12},{20,16},{24,20},{28,24},{1,29},{... | collective-permute-start | bytes 835592 | tf_op jit(solution)/shard_map/ppermute | solution.py:324
  102.2 1.1 copy-start.4
  103.4 0.8 copy-start.3
  104.2 20.0 %all-to-all-start.1 = ((bf16[4,272,256]{2,1,0:T(8,128)(2,1)}), bf16[4,272,256]{2,1,0:T(8,128)(2,1)}, u32[]{:S(2)}, u32[]{:S(2)}) async-start(bf16[4,272,256]{2,1,0:T(8,128)(2,1)} %copy-done.3), calls=%async_computation.1 | async-start | bytes 1114112 | tf_op jit(solution)/shard_map/all_to_all | solution.py:357
  108.4 1.2 copy-start.1
  111.4 39.8 %collective-permute-start.7 = (bf16[512,640]{1,0:T(8,128)(2,1)}, bf16[512,640]{1,0:T(8,128)(2,1)}, u32[]{:S(2)}, u32[]{:S(2)}) collective-permute-start(bf16[512,640]{1,0:T(8,128)(2,1)} %get-tuple-element.23), channel_id=1, source_target_pairs={{0,2},{1,3},{2,0},{3,1},{4,6},{5,7},{6,4},{7,5},{8,10},{9,11},{10,... | collective-permute-start | bytes 1966088 | tf_op jit(solution)/shard_map/ppermute | solution.py:328
  114.8 36.4 %collective-permute-start.8 = (bf16[640,512]{1,0:T(8,128)(2,1)}, bf16[640,512]{1,0:T(8,128)(2,1)}, u32[]{:S(2)}, u32[]{:S(2)}) collective-permute-start(bf16[640,512]{1,0:T(8,128)(2,1)} %get-tuple-element.24), channel_id=1, source_target_pairs={{0,2},{1,3},{2,0},{3,1},{4,6},{5,7},{6,4},{7,5},{8,10},{9,11},{10,... | collective-permute-start | bytes 1966088 | tf_op jit(solution)/shard_map/ppermute | solution.py:328
  124.1 51.2 %copy-start.2 = (bf16[256,2048]{1,0:T(8,128)(2,1)S(1)}, bf16[256,2048]{1,0:T(8,128)(2,1)}, u32[]{:S(2)}) copy-start(bf16[256,2048]{1,0:T(8,128)(2,1)} %get-tuple-element.21.mine_ref) | copy-start | bytes 3145732
  169.3 9.1 %collective-permute-start.10 = (bf16[512,256]{1,0:T(8,128)(2,1)S(1)}, bf16[512,256]{1,0:T(8,128)(2,1)S(1)}, u32[]{:S(2)}, u32[]{:S(2)}) collective-permute-start(bf16[512,256]{1,0:T(8,128)(2,1)S(1)} %get-tuple-element.32), channel_id=1, source_target_pairs={{0,28},{4,0},{8,4},{12,8},{16,12},{20,16},{24,20},{28,24},{1,29},{... | collective-permute-start | bytes 786440 | tf_op jit(solution)/shard_map/ppermute | solution.py:324
  172.3 9.7 %copy-start.5 = (s32[256]{0:T(256)S(1)}, s32[256]{0:T(256)}, u32[]{:S(2)}) copy-start(s32[256]{0:T(256)} %param.11) | copy-start | bytes 3076
  172.3 9.6 %copy-start.6 = (s32[256]{0:T(256)S(1)}, s32[256]{0:T(256)}, u32[]{:S(2)}) copy-start(s32[256]{0:T(256)} %param.12) | copy-start | bytes 3076
  172.3 9.6 %copy-start.7 = (s32[256]{0:T(256)S(1)}, s32[256]{0:T(256)}, u32[]{:S(2)}) copy-start(s32[256]{0:T(256)} %param.13) | copy-start | bytes 3076
  172.3 9.6 %copy-start.8 = (bf16[256]{0:T(256)(128)(2,1)S(1)}, bf16[256]{0:T(256)(128)(2,1)}, u32[]{:S(2)}) copy-start(bf16[256]{0:T(256)(128)(2,1)} %gate_ref.3) | copy-start | bytes 1540
  172.3 9.6 %collective-permute-start.9 = (bf16[512,256]{1,0:T(8,128)(2,1)S(1)}, bf16[512,256]{1,0:T(8,128)(2,1)S(1)}, u32[]{:S(2)}, u32[]{:S(2)}) collective-permute-start(bf16[512,256]{1,0:T(8,128)(2,1)S(1)} %get-tuple-element.33), channel_id=1, source_target_pairs={{0,4},{4,8},{8,12},{12,16},{16,20},{20,24},{24,28},{28,0},{1,5},{5... | collective-permute-start | bytes 786440 | tf_op jit(solution)/shard_map/ppermute | solution.py:324

commit v5 on v4

--- a/solution.py
+++ b/solution.py
@@ -15,7 +15,6 @@
 ANY = pl.BlockSpec(memory_space=pl.ANY)
 SMEM = pl.BlockSpec(memory_space=pltpu.SMEM)
 BF16 = jnp.bfloat16
-PARITIES = [[0, 2, 4, 6], [1, 3, 5, 7]]
 F32 = jnp.float32
 
 root_two_pi = math.sqrt(2.0 / math.pi)
@@ -52,6 +51,9 @@
 def slot_hits(expert_ref, slot_ref, kept_ref, slots):
     position = jnp.where(kept_ref[...] == 1, expert_ref[...] * CAP + slot_ref[...], -1)
     return iota((slots, position.shape[1]), 0) == position
+
+
+CARRIED = (0, 5, 2)
 
 
 def dispatch_kernel(me_ref, expert_ref, slot_ref, kept_ref, gate_ref, tokens, grad_out, send_ref, x_ref, dy_ref, sems):
@@ -63,29 +65,29 @@
     for load in loads:
         load.start()
     position = jnp.where(kept_ref[...] == 1, expert_ref[...] * CAP + slot_ref[...], -1)
-    shape = (rows, position.shape[1])
-    row = iota(shape, 0)
-    hits = (row & ~7) + (me_ref[0] & 3) + 4 * (row & 1) == position
-    quarter = (row >> 1) & 3
+    run = half // len(CARRIED)
+    row = iota((rows, position.shape[1]), 0)
+    hits = [(row & ~7) + ((me_ref[0] + offset) & 7) == position for offset in CARRIED]
     gate_row = gate_ref[...].astype(F32).reshape(1, -1)
-    total = None
-    for q, (ref, factor) in enumerate(
-        ((x_ref, 1.0), (x_ref, 1.0), (dy_ref, gate_row), (dy_ref, gate_row))
-    ):
-        pick = jnp.where(hits & (quarter == q), factor, 0.0).astype(BF16)
-        if q % 2 == 0:
-            loads[q // 2].wait()
-        low = (q % 2) * half
-        term = dot(pick, ref[:, low : low + half], 1, 0)
-        total = term if total is None else total + term
-    send_ref[...] = total.astype(BF16)
+    totals = [None] * len(CARRIED)
+    for r in range(8):
+        ref, factor = ((x_ref, 1.0), (dy_ref, gate_row))[r // 4]
+        if r % 4 == 0:
+            loads[r // 4].wait()
+        piece = ref[:, (r % 4) * run : (r % 4 + 1) * run]
+        for k, hit in enumerate(hits):
+            pick = jnp.where(hit & ((row & 7) == r), factor, 0.0).astype(BF16)
+            term = dot(pick, piece, 1, 0)
+            totals[k] = term if r == 0 else totals[k] + term
+    for k, total in enumerate(totals):
+        send_ref[:, k * run : (k + 1) * run] = total.astype(BF16)
 
 
 def dispatch(me, slots, index_rows, gate, tokens, grad_out):
     count, width = tokens.shape
     return pl.pallas_call(
         dispatch_kernel,
-        out_shape=jax.ShapeDtypeStruct((slots, width // 2), BF16),
+        out_shape=jax.ShapeDtypeStruct((slots, width // 4 * len(CARRIED)), BF16),
         in_specs=[SMEM] + [VMEM] * 4 + [ANY] * 2,
         out_specs=VMEM,
         scratch_shapes=[
@@ -99,38 +101,40 @@
 
 
 def expert_kernel(
-    me_ref, data_ref, own, before, after, low, high, w_in, w_out, same, first, second, acts, mine,
-    packed, x_ref, s_ref, in_ref, out_ref, rows_ref, acts_ref, mine_ref, sems,
+    me_ref, data_ref, own, before, after, w_in, w_out, rows, acts, mine,
+    own_ref, before_ref, after_ref, x_ref, s_ref, in_ref, out_ref, rows_ref, acts_ref, mine_ref, sems,
 ):
     slots, width = x_ref.shape
     hidden_width = in_ref.shape[1]
-    quarter, half, part_rows = width // 4, slots // 2, slots // 4
+    quarter, part_rows = width // 4, slots // 8
     parts = rows_ref.shape[0]
     loads = [
-        pltpu.make_async_copy(own, packed.at[0], sems.at[0]),
-        pltpu.make_async_copy(before, packed.at[1], sems.at[1]),
-        pltpu.make_async_copy(after, packed.at[2], sems.at[2]),
-        pltpu.make_async_copy(low, packed.at[3, :half], sems.at[3]),
-        pltpu.make_async_copy(high, packed.at[3, half:], sems.at[4]),
-        pltpu.make_async_copy(w_in, in_ref, sems.at[5]),
-        pltpu.make_async_copy(w_out, out_ref, sems.at[6]),
+        pltpu.make_async_copy(own, own_ref, sems.at[0]),
+        pltpu.make_async_copy(before, before_ref, sems.at[1]),
+        pltpu.make_async_copy(after, after_ref, sems.at[2]),
+        pltpu.make_async_copy(w_in, in_ref, sems.at[3]),
+        pltpu.make_async_copy(w_out, out_ref, sems.at[4]),
     ]
     for load in loads:
         load.start()
     square = (slots, slots)
     to, at = iota(square, 0), iota(square, 1)
-    inner = to % part_rows
-    unpack = jnp.where(at == (inner >> 1) * 8 + (to // part_rows) * 2 + (inner & 1), 1.0, 0.0).astype(BF16)
-    for k, offset in enumerate((0, 3, 1, 2)):
+    unpack = jnp.where(at == (to % part_rows) * 8 + to // part_rows, 1.0, 0.0).astype(BF16)
+    middle = quarter // 2
+    for k, (ref, offset, skip) in enumerate(((own_ref, 0, 0), (before_ref, 7, 0), (after_ref, 1, middle))):
         loads[k].wait()
-        if k == 3:
-            loads[4].wait()
-        plain = dot(unpack, packed[k], 1, 0).astype(BF16)
-        group = (me_ref[0] + offset) & 3
-        place = pl.ds(pl.multiple_of(group * part_rows, part_rows), part_rows)
-        for q, ref in enumerate((x_ref, x_ref, s_ref, s_ref)):
-            start = (q % 2) * (width // 2)
-            ref[place, start : start + width // 2] = plain[q * part_rows : (q + 1) * part_rows]
+        plain = dot(unpack, ref[...], 1, 0).astype(BF16)
+        for carried, slot_offset in enumerate(CARRIED):
+            start = max(carried * quarter, skip)
+            end = min((carried + 1) * quarter, skip + ref.shape[1])
+            slot = (me_ref[0] + offset + slot_offset) & 7
+            place = pl.ds(pl.multiple_of(slot * part_rows, part_rows), part_rows)
+            for r in range(8):
+                target = (x_ref, s_ref)[r // 4]
+                first = (r % 4) * quarter + start - carried * quarter
+                target[place, first : first + end - start] = plain[
+                    r * part_rows : (r + 1) * part_rows, start - skip : end - skip
+                ]
     for k, ref in enumerate((x_ref, x_ref, s_ref, s_ref)):
         for target, mask in ((mine_ref, (0, 2)[k % 2]), (acts_ref, (1, 3)[k % 2])):
             place = pl.ds(pl.multiple_of((data_ref[0] ^ mask) * quarter, quarter), quarter)
@@ -140,12 +144,12 @@
         pltpu.make_async_copy(acts_ref, acts, sems.at[8 + parts]),
     ]
     stores[0].start()
-    loads[5].wait()
+    loads[3].wait()
     pre = dot(x_ref[...], in_ref[...], 1, 0)
     value, slope = gelu_pair(pre)
     hidden = value.astype(BF16)
     acts_ref[:, width + hidden_width :] = hidden
-    loads[6].wait()
+    loads[4].wait()
     back = dot(s_ref[...], out_ref[...], 1, 1)
     grad_pre = (back * slope).astype(BF16)
     acts_ref[:, width : width + hidden_width] = grad_pre
@@ -154,18 +158,11 @@
     gate_row = jnp.sum(jnp.where(to == at, gate, 0.0), axis=0, keepdims=True)
     gate_rows = jnp.broadcast_to(gate_row, (16, slots)).astype(BF16)
     block = width // parts
-    odd = me_ref[0] & 1
-    half_parts = parts // 2
     for part in range(parts):
-        index = 2 * (part % half_parts) + (odd if part >= half_parts else 1 - odd)
-        place = pl.ds(pl.multiple_of(index * block, block), block)
-        rows_ref[part, :slots, :] = dot(grad_pre, in_ref[place, :], 1, 1).astype(BF16)
+        term = dot(grad_pre, in_ref[part * block : (part + 1) * block, :], 1, 1)
+        rows_ref[part, :slots, :] = term.astype(BF16)
         rows_ref[part, slots:, :] = gate_rows
-        if part >= half_parts:
-            target = same.at[part - half_parts]
-        else:
-            target = (first, second)[part // 2].at[part % 2]
-        stores.append(pltpu.make_async_copy(rows_ref.at[part], target, sems.at[7 + part]))
+        stores.append(pltpu.make_async_copy(rows_ref.at[part], rows.at[part], sems.at[7 + part]))
         stores[-1].start()
     for store in stores:
         store.wait()
@@ -174,50 +171,30 @@
 def expert(me, data, packs, w_in, w_out, parts):
     slots = packs[0].shape[0]
     width, hidden_width = w_in.shape
-    rows = (slots + 16, width // parts)
     outs = (
-        (parts // 2,) + rows,
-        (2,) + rows,
-        (2,) + rows,
+        (parts, slots + 16, width // parts),
         (slots, width + 2 * hidden_width),
         (slots, width),
     )
     return pl.pallas_call(
         expert_kernel,
         out_shape=tuple(jax.ShapeDtypeStruct(shape, BF16) for shape in outs),
-        in_specs=[SMEM, SMEM] + [ANY] * 7,
-        out_specs=(ANY,) * 5,
+        in_specs=[SMEM, SMEM] + [ANY] * 5,
+        out_specs=(ANY, ANY, ANY),
         scratch_shapes=[
-            pltpu.VMEM((4, slots, width // 2), BF16),
+            *[pltpu.VMEM(pack.shape, BF16) for pack in packs],
             pltpu.VMEM((slots, width), BF16),
             pltpu.VMEM((slots, width), BF16),
             pltpu.VMEM(w_in.shape, BF16),
             pltpu.VMEM(w_out.shape, BF16),
         ]
-        + [pltpu.VMEM(shape, BF16) for shape in ((parts,) + rows,) + outs[3:]]
+        + [pltpu.VMEM(shape, BF16) for shape in outs]
         + [pltpu.SemaphoreType.DMA((9 + parts,))],
         compiler_params=params(59),
         cost_estimate=cost(
             6 * slots * width * hidden_width, 4 * width * (slots + hidden_width) + 8 * slots * width
         ),
     )(me, data, *packs, w_in, w_out)
-
-
-def add_kernel(same_ref, first_ref, second_ref, out_ref):
-    for k in range(4):
-        other = (first_ref, second_ref)[k // 2]
-        out_ref[k] = (same_ref[k].astype(F32) + other[k % 2].astype(F32)).astype(BF16)
-
-
-def add_terms(same, first, second):
-    return pl.pallas_call(
-        add_kernel,
-        out_shape=jax.ShapeDtypeStruct(same.shape, BF16),
-        in_specs=[VMEM] * 3,
-        out_specs=VMEM,
-        compiler_params=params(24),
-        cost_estimate=cost(same.size, 6 * same.size),
-    )(same, first, second)
 
 
 def sum_kernel(terms_ref, out_ref):
@@ -227,7 +204,7 @@
     for part in range(1, terms_ref.shape[0]):
         total = total + terms_ref[part].astype(F32)
     to, at = iota((slots, slots), 0), iota((slots, slots), 1)
-    from_row = (to & 3) * (slots // 4) + (to >> 3) * 2 + ((to >> 2) & 1)
+    from_row = (to & 7) * (slots // 8) + (to >> 3)
     order = jnp.where(at == from_row, 1.0, 0.0)
     gate = jnp.sum(order * total[slots : slots + 1], axis=1, keepdims=True)
     sums = dot(order.astype(BF16), total[:slots].astype(BF16), 1, 0)
@@ -330,7 +307,7 @@
 
 def gather_pieces(piece):
     same = lax.all_gather(
-        piece, "mp", axis=0, tiled=True, axis_index_groups=PARITIES
+        piece, "mp", axis=0, tiled=True, axis_index_groups=[[0, 2, 4, 6], [1, 3, 5, 7]]
     )
     half = same.shape[0] // 2
     return same, shift(same[:half], 1), shift(same[half:], -1)
@@ -350,11 +327,11 @@
     data = lax.axis_index("dp").astype(jnp.int32).reshape(1)
 
     send = dispatch(me, slots, index_rows, gate, tokens, grad_out)
-    came = scatter(send.reshape(experts, CAP, width // 2), "expert").reshape(send.shape)
-    packs = (came, shift(came, 1), shift(came, -1), shift(came[: slots // 2], 2), shift(came[slots // 2 :], -2))
-    same, first, second, acts, mine = expert(me, data, packs, w_in[0], w_out[0], parts)
-    pairs = add_terms(same, shift(first, 1), shift(second, -1))
-    terms = lax.all_to_all(pairs, "mp", 0, 0, axis_index_groups=PARITIES, tiled=True)
+    came = scatter(send.reshape(experts, CAP, send.shape[1]), "expert").reshape(send.shape)
+    middle = width // 8
+    packs = (came, shift(came[:, : came.shape[1] - middle], 1), shift(came[:, middle:], -1))
+    rows, acts, mine = expert(me, data, packs, w_in[0], w_out[0], parts)
+    terms = scatter(rows, "mp")
 
     other = swap(acts, 1)
     added = [swap(value, 2) for value in weight_terms(1, mine, acts, other)]

time: 184 us -> 174 us (0.946)
  the two profiles are of different devices: /device:TPU:16 before, /device:TPU:2 now
where the time goes in v5:
time: 174 us
  blocking collectives  74.5 us (43%)
  waiting for transfers between devices  39.6 us (23%)
  starting transfers between devices  36.8 us (21%)
  Pallas kernels  19.5 us (11%)
  local copies, waits for them, and re-layouts  2.22 us (1%)
    all_to_all x2, blocking collectives, scatter(): return lax.all_to_all(value, axis, split_axis=0, concat_axis=0, tiled=True)  59 us
    ppermute x4, starting transfers between devices, shift(): return lax.ppermute(value, 'mp', [(i, (i + step) % 8) for i in range(8)])  24.7 us
    all_to_all x1, waiting for transfers between devices, scatter(): return lax.all_to_all(value, axis, split_axis=0, concat_axis=0, tiled=True)  22.2 us
    ppermute x4, waiting for transfers between devices, shift(): return lax.ppermute(value, 'mp', [(i, (i + step) % 8) for i in range(8)])  17.4 us
    all_gather x1, blocking collectives, gather_pieces(): lax.all_gather(piece, 'mp', axis=0, tiled=True, axis_index_groups=[[0, 2,...  15.5 us
    ppermute x3, starting transfers between devices, swap(): return lax.ppermute(value, 'dp', [(i, i ^ bit) for i in range(4)])  7.89 us
    pallas_call x1, Pallas kernels, expert(): pl.pallas_call(expert_kernel, out_shape=tuple((jax.ShapeDtypeStruct(shape...  6.83 us
    pallas_call x2, Pallas kernels, weight_terms(): pl.pallas_call(functools.partial(weight_kernel, turn), in_specs=[VMEM] *...  4.91 us
  transfers between devices with their start and end apart: 8, of which 4 were waited for; matrix products, arithmetic and copies ran while one was open for 0% of the time, Pallas kernels for 4%

profile of v5, /device:TPU:2, one launch (start us, length us, event | category | flops | bytes accessed | tf_op | source)
XLA Modules:
  0.0 173.5 jit_solution(1727015231157578382)
XLA Ops:
  0.6 4.7 %shard_map.111 = bf16[256,1536]{1,0:T(8,128)(2,1)} custom-call(s32[1]{0:T(128)} %bitcast.me_ref, s32[1,256]{1,0:T(1,128)} %bitcast.16, s32[1,256]{1,0:T(1,128)} %bitcast.18, s32[1,256]{1,0:T(1,128)} %bitcast.20, bf16[256]{0:T(256)(128)(2,1)} %gate_ref.3, bf16[256,2048]{1,0:T(8,128)(2,1)} %tokens.1, bf16[256,2048]{1,0:T(8,128)(2,1)} %grad_out.1), custom_call_target="tpu_custom_call" | custom-call | flops 536870912 | bytes 2621440 | tf_op jit(solution)/shard_map/pallas_call | solution.py:88
  5.3 38.1 %all_to_all.15 = bf16[32,8,1536]{2,1,0:T(8,128)(2,1)S(1)} all-to-all(bf16[32,8,1536]{2,1,0:T(8,128)(2,1)} %bitcast.24), channel_id=1, replica_groups=mesh['expert'=32,'mp'=8,'dp'=4] {'expert'}, dimensions={0} | all-to-all | bytes 1572864 | tf_op jit(solution)/shard_map/all_to_all | solution.py:317
  43.4 0.0 copy-start.7
  43.4 0.1 fusion
  43.5 16.8 %collective-permute-start.1 = (bf16[256,1280]{1,0:T(8,128)(2,1)S(1)}, bf16[256,1280]{1,0:T(8,128)(2,1)S(1)}, u32[]{:S(2)}, u32[]{:S(2)}) collective-permute-start(bf16[256,1280]{1,0:T(8,128)(2,1)S(1)} %get-tuple-element.28), channel_id=1, source_target_pairs={{0,28},{4,0},{8,4},{12,8},{16,12},{20,16},{24,20},{28,24},{1,29},{... | collective-permute-start | bytes 1966088 | tf_op jit(solution)/shard_map/ppermute | solution.py:301
  60.3 1.9 %collective-permute-start = (bf16[256,1280]{1,0:T(8,128)(2,1)S(1)}, bf16[256,1280]{1,0:T(8,128)(2,1)S(1)}, u32[]{:S(2)}, u32[]{:S(2)}) collective-permute-start(bf16[256,1280]{1,0:T(8,128)(2,1)S(1)} %get-tuple-element.29), channel_id=1, source_target_pairs={{0,4},{4,8},{8,12},{12,16},{16,20},{20,24},{24,28},{28,0},{1,5},{5... | collective-permute-start | bytes 1966088 | tf_op jit(solution)/shard_map/ppermute | solution.py:301
  62.2 9.6 %collective-permute-done.1.after = bf16[256,1280]{1,0:T(8,128)(2,1)S(1)} collective-permute-done((bf16[256,1280]{1,0:T(8,128)(2,1)S(1)}, bf16[256,1280]{1,0:T(8,128)(2,1)S(1)}, u32[]{:S(2)}, u32[]{:S(2)}) %collective-permute-start.1) | collective-permute-done | bytes 655392 | tf_op jit(solution)/shard_map/ppermute | solution.py:301
  71.9 0.0 copy-start.8
  71.9 5.3 %collective-permute-done.before = bf16[256,1280]{1,0:T(8,128)(2,1)S(1)} collective-permute-done((bf16[256,1280]{1,0:T(8,128)(2,1)S(1)}, bf16[256,1280]{1,0:T(8,128)(2,1)S(1)}, u32[]{:S(2)}, u32[]{:S(2)}) %collective-permute-start) | collective-permute-done | bytes 655392 | tf_op jit(solution)/shard_map/ppermute | solution.py:301
  77.2 0.0 copy-start.9
  77.2 0.0 copy-done.7
  77.2 0.0 copy-done.8
  77.2 0.8 copy-done.9
  78.0 6.8 %shard_map.112 = (bf16[8,272,256]{2,1,0:T(8,128)(2,1)}, bf16[256,3328]{1,0:T(8,128)(2,1)}, bf16[256,2048]{1,0:T(8,128)(2,1)}) custom-call(s32[1]{0:T(128)} %bitcast.me_ref, s32[1]{0:T(128)} %bitcast.4.data_ref, bf16[256,1536]{1,0:T(8,128)(2,1)} %bitcast.23, bf16[256,1280]{1,0:T(8,128)(2,1)} %copy-done.9, bf16[256,1280]{1,0:T(8,128)(2,1)} %copy-done.8, ...), custom_call_target="tpu_custom_call" | custom-call | flops 2013265920 | bytes 11534336 | tf_op jit(solution)/shard_map/pallas_call | solution.py:179
  84.9 0.0 copy-start
  84.9 2.1 %collective-permute-start.2 = (bf16[256,3328]{1,0:T(8,128)(2,1)}, bf16[256,3328]{1,0:T(8,128)(2,1)S(1)}, u32[]{:S(2)}, u32[]{:S(2)}) collective-permute-start(bf16[256,3328]{1,0:T(8,128)(2,1)} %get-tuple-element.18.acts_ref), channel_id=1, source_target_pairs={{0,1},{1,0},{2,3},{3,2},{4,5},{5,4},{6,7},{7,6},{8,9},{9,8},{10,11... | collective-permute-start | bytes 5111816 | tf_op jit(solution)/shard_map/ppermute | solution.py:305
  86.9 4.3 %all-to-all-start.1 = ((bf16[8,272,256]{2,1,0:T(8,128)(2,1)}), bf16[8,272,256]{2,1,0:T(8,128)(2,1)}, u32[]{:S(2)}, u32[]{:S(2)}) async-start(bf16[8,272,256]{2,1,0:T(8,128)(2,1)} %get-tuple-element.16), calls=%async_computation.1 | async-start | bytes 2228224 | tf_op jit(solution)/shard_map/all_to_all | solution.py:317
  91.2 0.0 collective-permute-done.2.other_ref
  91.2 0.0 copy-done
  91.2 0.0 copy-start.1
  91.2 1.2 copy-done.1
  92.4 1.8 %shard_map.114 = (bf16[512,640]{1,0:T(8,128)(2,1)}, bf16[640,512]{1,0:T(8,128)(2,1)}) custom-call(bf16[256,2048]{1,0:T(8,128)(2,1)S(1)} %copy-done.1, bf16[256,3328]{1,0:T(8,128)(2,1)S(1)} %copy-done, bf16[256,3328]{1,0:T(8,128)(2,1)S(1)} %collective-permute-done.2.other_ref), custom_call_target="tpu_custom_call" | custom-call | flops 671088640 | bytes 3670016 | tf_op jit(solution)/shard_map/pallas_call | solution.py:287
  94.3 2.9 %collective-permute-start.3 = (bf16[512,640]{1,0:T(8,128)(2,1)}, bf16[512,640]{1,0:T(8,128)(2,1)}, u32[]{:S(2)}, u32[]{:S(2)}) collective-permute-start(bf16[512,640]{1,0:T(8,128)(2,1)} %get-tuple-element.19), channel_id=1, source_target_pairs={{0,2},{1,3},{2,0},{3,1},{4,6},{5,7},{6,4},{7,5},{8,10},{9,11},{10,... | collective-permute-start | bytes 1966088 | tf_op jit(solution)/shard_map/ppermute | solution.py:305
  97.2 3.0 %collective-permute-start.4 = (bf16[640,512]{1,0:T(8,128)(2,1)}, bf16[640,512]{1,0:T(8,128)(2,1)}, u32[]{:S(2)}, u32[]{:S(2)}) collective-permute-start(bf16[640,512]{1,0:T(8,128)(2,1)} %get-tuple-element.20), channel_id=1, source_target_pairs={{0,2},{1,3},{2,0},{3,1},{4,6},{5,7},{6,4},{7,5},{8,10},{9,11},{10,... | collective-permute-start | bytes 1966088 | tf_op jit(solution)/shard_map/ppermute | solution.py:305
  100.1 22.2 %all-to-all-done.1.terms_ref = bf16[8,272,256]{2,1,0:T(8,128)(2,1)} async-done(((bf16[8,272,256]{2,1,0:T(8,128)(2,1)}), bf16[8,272,256]{2,1,0:T(8,128)(2,1)}, u32[]{:S(2)}, u32[]{:S(2)}) %all-to-all-start.1) | async-done | bytes 1114144 | tf_op jit(solution)/shard_map/all_to_all | solution.py:317
  122.3 0.0 copy-start.2
  122.3 1.6 shard_map.113
  124.0 20.9 %all_to_all.16 = bf16[32,8,384]{2,1,0:T(8,128)(2,1)S(1)} all-to-all(bf16[32,8,384]{2,1,0:T(8,128)(2,1)S(1)} %bitcast.15), channel_id=1, replica_groups=mesh['expert'=32,'mp'=8,'dp'=4] {'expert'}, dimensions={0} | all-to-all | bytes 393216 | tf_op jit(solution)/shard_map/all_to_all | solution.py:317
  144.9 0.0 collective-permute-done.3.refs_0_
  144.9 0.0 collective-permute-done.4.refs_1_
  144.9 15.5 %all_gather.3.refs_0_ = bf16[1024,256]{1,0:T(8,128)(2,1)S(1)} all-gather(bf16[256,256]{1,0:T(8,128)(2,1)S(1)} %slice.17), channel_id=1, replica_groups={{0,8,16,24},{4,12,20,28},{1,9,17,25},{5,13,21,29},{2,10,18,26},{6,14,22..., dimensions={0}, use_global_device_ids=true | all-gather | bytes 655360 | tf_op jit(solution)/shard_map/all_gather | solution.py:309
  160.5 1.9 %collective-permute-start.6 = (bf16[512,256]{1,0:T(8,128)(2,1)S(1)}, bf16[512,256]{1,0:T(8,128)(2,1)S(1)}, u32[]{:S(2)}, u32[]{:S(2)}) collective-permute-start(bf16[512,256]{1,0:T(8,128)(2,1)S(1)} %get-tuple-element.30), channel_id=1, source_target_pairs={{0,28},{4,0},{8,4},{12,8},{16,12},{20,16},{24,20},{28,24},{1,29},{... | collective-permute-start | bytes 786440 | tf_op jit(solution)/shard_map/ppermute | solution.py:301
  162.4 0.0 copy-start.3
  162.4 0.0 copy-start.4
  162.4 0.0 copy-start.5
  162.4 0.0 copy-start.6
  162.5 4.1 %collective-permute-start.5 = (bf16[512,256]{1,0:T(8,128)(2,1)S(1)}, bf16[512,256]{1,0:T(8,128)(2,1)S(1)}, u32[]{:S(2)}, u32[]{:S(2)}) collective-permute-start(bf16[512,256]{1,0:T(8,128)(2,1)S(1)} %get-tuple-element.31), channel_id=1, source_target_pairs={{0,4},{4,8},{8,12},{12,16},{16,20},{20,24},{24,28},{28,0},{1,5},{5... | collective-permute-start | bytes 786440 | tf_op jit(solution)/shard_map/ppermute | solution.py:301
  166.5 0.0 copy-done.2
  166.5 3.1 %shard_map.116 = (bf16[512,640]{1,0:T(8,128)(2,1)}, bf16[640,512]{1,0:T(8,128)(2,1)}) custom-call(bf16[256,2048]{1,0:T(8,128)(2,1)S(1)} %copy-done.2, bf16[256,3328]{1,0:T(8,128)(2,1)S(1)} %copy-done, bf16[256,3328]{1,0:T(8,128)(2,1)S(1)} %collective-permute-done.2.other_ref, bf16[512,640]{1,0:T(8,128)(2,1)} %collective-permute-done.3.refs_0_, ...), custom_call_target="tpu_custom_call" | custom-call | flops 671088640 | bytes 3670016 | tf_op jit(solution)/shard_map/pallas_call | solution.py:287
  169.6 0.0 collective-permute-done.6.refs_2_
  169.6 2.5 %collective-permute-done.5.refs_1_ = bf16[512,256]{1,0:T(8,128)(2,1)S(1)} collective-permute-done((bf16[512,256]{1,0:T(8,128)(2,1)S(1)}, bf16[512,256]{1,0:T(8,128)(2,1)S(1)}, u32[]{:S(2)}, u32[]{:S(2)}) %collective-permute-start.5) | collective-permute-done | bytes 262176 | tf_op jit(solution)/shard_map/ppermute | solution.py:301
  172.1 0.0 copy-done.3
  172.1 0.0 copy-done.4
  172.1 0.0 copy-done.5
  172.1 0.0 copy-done.6
  172.1 1.5 shard_map.115
  (2 shorter events, 0.0 us)
Async XLA Ops:
  43.4 33.8 %copy-start.7 = (bf16[32,8,1536]{2,1,0:T(8,128)(2,1)}, bf16[32,8,1536]{2,1,0:T(8,128)(2,1)S(1)}, u32[]{:S(2)}) copy-start(bf16[32,8,1536]{2,1,0:T(8,128)(2,1)S(1)} %all_to_all.15) | copy-start | bytes 2359300
  43.5 28.3 %collective-permute-start.1 = (bf16[256,1280]{1,0:T(8,128)(2,1)S(1)}, bf16[256,1280]{1,0:T(8,128)(2,1)S(1)}, u32[]{:S(2)}, u32[]{:S(2)}) collective-permute-start(bf16[256,1280]{1,0:T(8,128)(2,1)S(1)} %get-tuple-element.28), channel_id=1, source_target_pairs={{0,28},{4,0},{8,4},{12,8},{16,12},{20,16},{24,20},{28,24},{1,29},{... | collective-permute-start | bytes 1966088 | tf_op jit(solution)/shard_map/ppermute | solution.py:301
  60.3 16.9 %collective-permute-start = (bf16[256,1280]{1,0:T(8,128)(2,1)S(1)}, bf16[256,1280]{1,0:T(8,128)(2,1)S(1)}, u32[]{:S(2)}, u32[]{:S(2)}) collective-permute-start(bf16[256,1280]{1,0:T(8,128)(2,1)S(1)} %get-tuple-element.29), channel_id=1, source_target_pairs={{0,4},{4,8},{8,12},{12,16},{16,20},{20,24},{24,28},{28,0},{1,5},{5... | collective-permute-start | bytes 1966088 | tf_op jit(solution)/shard_map/ppermute | solution.py:301
  71.9 5.3 %copy-start.8 = (bf16[256,1280]{1,0:T(8,128)(2,1)}, bf16[256,1280]{1,0:T(8,128)(2,1)S(1)}, u32[]{:S(2)}) copy-start(bf16[256,1280]{1,0:T(8,128)(2,1)S(1)} %collective-permute-done.1.after) | copy-start | bytes 1966084
  77.2 0.8 copy-start.9
  84.9 6.3 %copy-start = (bf16[256,3328]{1,0:T(8,128)(2,1)S(1)}, bf16[256,3328]{1,0:T(8,128)(2,1)}, u32[]{:S(2)}) copy-start(bf16[256,3328]{1,0:T(8,128)(2,1)} %get-tuple-element.18.acts_ref) | copy-start | bytes 5111812
  84.9 6.3 %collective-permute-start.2 = (bf16[256,3328]{1,0:T(8,128)(2,1)}, bf16[256,3328]{1,0:T(8,128)(2,1)S(1)}, u32[]{:S(2)}, u32[]{:S(2)}) collective-permute-start(bf16[256,3328]{1,0:T(8,128)(2,1)} %get-tuple-element.18.acts_ref), channel_id=1, source_target_pairs={{0,1},{1,0},{2,3},{3,2},{4,5},{5,4},{6,7},{7,6},{8,9},{9,8},{10,11... | collective-permute-start | bytes 5111816 | tf_op jit(solution)/shard_map/ppermute | solution.py:305
  86.9 35.4 %all-to-all-start.1 = ((bf16[8,272,256]{2,1,0:T(8,128)(2,1)}), bf16[8,272,256]{2,1,0:T(8,128)(2,1)}, u32[]{:S(2)}, u32[]{:S(2)}) async-start(bf16[8,272,256]{2,1,0:T(8,128)(2,1)} %get-tuple-element.16), calls=%async_computation.1 | async-start | bytes 2228224 | tf_op jit(solution)/shard_map/all_to_all | solution.py:317
  91.2 1.2 copy-start.1
  94.3 50.6 %collective-permute-start.3 = (bf16[512,640]{1,0:T(8,128)(2,1)}, bf16[512,640]{1,0:T(8,128)(2,1)}, u32[]{:S(2)}, u32[]{:S(2)}) collective-permute-start(bf16[512,640]{1,0:T(8,128)(2,1)} %get-tuple-element.19), channel_id=1, source_target_pairs={{0,2},{1,3},{2,0},{3,1},{4,6},{5,7},{6,4},{7,5},{8,10},{9,11},{10,... | collective-permute-start | bytes 1966088 | tf_op jit(solution)/shard_map/ppermute | solution.py:305
  97.2 47.7 %collective-permute-start.4 = (bf16[640,512]{1,0:T(8,128)(2,1)}, bf16[640,512]{1,0:T(8,128)(2,1)}, u32[]{:S(2)}, u32[]{:S(2)}) collective-permute-start(bf16[640,512]{1,0:T(8,128)(2,1)} %get-tuple-element.20), channel_id=1, source_target_pairs={{0,2},{1,3},{2,0},{3,1},{4,6},{5,7},{6,4},{7,5},{8,10},{9,11},{10,... | collective-permute-start | bytes 1966088 | tf_op jit(solution)/shard_map/ppermute | solution.py:305
  122.3 44.2 %copy-start.2 = (bf16[256,2048]{1,0:T(8,128)(2,1)S(1)}, bf16[256,2048]{1,0:T(8,128)(2,1)}, u32[]{:S(2)}) copy-start(bf16[256,2048]{1,0:T(8,128)(2,1)} %get-tuple-element.17.mine_ref) | copy-start | bytes 3145732
  160.5 9.1 %collective-permute-start.6 = (bf16[512,256]{1,0:T(8,128)(2,1)S(1)}, bf16[512,256]{1,0:T(8,128)(2,1)S(1)}, u32[]{:S(2)}, u32[]{:S(2)}) collective-permute-start(bf16[512,256]{1,0:T(8,128)(2,1)S(1)} %get-tuple-element.30), channel_id=1, source_target_pairs={{0,28},{4,0},{8,4},{12,8},{16,12},{20,16},{24,20},{28,24},{1,29},{... | collective-permute-start | bytes 786440 | tf_op jit(solution)/shard_map/ppermute | solution.py:301
  162.4 9.7 %copy-start.3 = (s32[256]{0:T(256)S(1)}, s32[256]{0:T(256)}, u32[]{:S(2)}) copy-start(s32[256]{0:T(256)} %param.11) | copy-start | bytes 3076
  162.4 9.6 %copy-start.4 = (s32[256]{0:T(256)S(1)}, s32[256]{0:T(256)}, u32[]{:S(2)}) copy-start(s32[256]{0:T(256)} %param.12) | copy-start | bytes 3076
  162.4 9.6 %copy-start.5 = (s32[256]{0:T(256)S(1)}, s32[256]{0:T(256)}, u32[]{:S(2)}) copy-start(s32[256]{0:T(256)} %param.13) | copy-start | bytes 3076
  162.4 9.6 %copy-start.6 = (bf16[256]{0:T(256)(128)(2,1)S(1)}, bf16[256]{0:T(256)(128)(2,1)}, u32[]{:S(2)}) copy-start(bf16[256]{0:T(256)(128)(2,1)} %gate_ref.3) | copy-start | bytes 1540
  162.5 9.6 %collective-permute-start.5 = (bf16[512,256]{1,0:T(8,128)(2,1)S(1)}, bf16[512,256]{1,0:T(8,128)(2,1)S(1)}, u32[]{:S(2)}, u32[]{:S(2)}) collective-permute-start(bf16[512,256]{1,0:T(8,128)(2,1)S(1)} %get-tuple-element.31), channel_id=1, source_target_pairs={{0,4},{4,8},{8,12},{12,16},{16,20},{20,24},{24,28},{28,0},{1,5},{5... | collective-permute-start | bytes 786440 | tf_op jit(solution)/shard_map/ppermute | solution.py:301

commit v6 on v5

--- a/solution.py
+++ b/solution.py
@@ -56,7 +56,7 @@
 CARRIED = (0, 5, 2)
 
 
-def dispatch_kernel(me_ref, expert_ref, slot_ref, kept_ref, gate_ref, tokens, grad_out, send_ref, x_ref, dy_ref, sems):
+def dispatch_kernel(me_ref, expert_ref, slot_ref, kept_ref, gate_ref, tokens, grad_out, send_ref, x_ref, dy_ref, spread_ref, sems):
     rows, half = send_ref.shape
     loads = [
         pltpu.make_async_copy(tokens, x_ref, sems.at[0]),
@@ -66,25 +66,31 @@
         load.start()
     position = jnp.where(kept_ref[...] == 1, expert_ref[...] * CAP + slot_ref[...], -1)
     run = half // len(CARRIED)
-    row = iota((rows, position.shape[1]), 0)
-    hits = [(row & ~7) + ((me_ref[0] + offset) & 7) == position for offset in CARRIED]
+    experts = rows // 8
+    tile = spread_ref.shape[2]
+    tiles = run // tile
     gate_row = gate_ref[...].astype(F32).reshape(1, -1)
-    totals = [None] * len(CARRIED)
-    for r in range(8):
-        ref, factor = ((x_ref, 1.0), (dy_ref, gate_row))[r // 4]
-        if r % 4 == 0:
-            loads[r // 4].wait()
-        piece = ref[:, (r % 4) * run : (r % 4 + 1) * run]
-        for k, hit in enumerate(hits):
-            pick = jnp.where(hit & ((row & 7) == r), factor, 0.0).astype(BF16)
-            term = dot(pick, piece, 1, 0)
-            totals[k] = term if r == 0 else totals[k] + term
-    for k, total in enumerate(totals):
-        send_ref[:, k * run : (k + 1) * run] = total.astype(BF16)
+    row = iota((len(CARRIED) * experts, position.shape[1]), 0)
+    carried = row // experts
+    offset = jnp.where(carried == 0, CARRIED[0], jnp.where(carried == 1, CARRIED[1], CARRIED[2]))
+    hits = (row - carried * experts) * CAP + ((me_ref[0] + offset) & 7) == position
+    for side, (ref, factor) in enumerate(((x_ref, 1.0), (dy_ref, gate_row))):
+        pick = jnp.where(hits, factor, 0.0).astype(BF16)
+        loads[side].wait()
+        for part in range(4):
+            r = 4 * side + part
+            found = dot(pick, ref[:, part * run : (part + 1) * run], 1, 0)
+            for k in range(len(CARRIED)):
+                for j in range(tiles):
+                    term = found[k * experts : (k + 1) * experts, j * tile : (j + 1) * tile]
+                    spread_ref[k * tiles + j, pl.ds(r, experts, stride=8), :] = term
+    for j in range(spread_ref.shape[0]):
+        send_ref[:, j * tile : (j + 1) * tile] = spread_ref[j].astype(BF16)
 
 
 def dispatch(me, slots, index_rows, gate, tokens, grad_out):
     count, width = tokens.shape
+    tile = min(LANES, width // 4)
     return pl.pallas_call(
         dispatch_kernel,
         out_shape=jax.ShapeDtypeStruct((slots, width // 4 * len(CARRIED)), BF16),
@@ -93,6 +99,7 @@
         scratch_shapes=[
             pltpu.VMEM((count, width), BF16),
             pltpu.VMEM((count, width), BF16),
+            pltpu.VMEM((width // 4 * len(CARRIED) // tile, slots, tile), F32),
             pltpu.SemaphoreType.DMA((2,)),
         ],
         compiler_params=params(58),
@@ -146,11 +153,11 @@
     stores[0].start()
     loads[3].wait()
     pre = dot(x_ref[...], in_ref[...], 1, 0)
+    loads[4].wait()
+    back = dot(s_ref[...], out_ref[...], 1, 1)
     value, slope = gelu_pair(pre)
     hidden = value.astype(BF16)
     acts_ref[:, width + hidden_width :] = hidden
-    loads[4].wait()
-    back = dot(s_ref[...], out_ref[...], 1, 1)
     grad_pre = (back * slope).astype(BF16)
     acts_ref[:, width : width + hidden_width] = grad_pre
     stores[1].start()
@@ -190,7 +197,7 @@
         ]
         + [pltpu.VMEM(shape, BF16) for shape in outs]
         + [pltpu.SemaphoreType.DMA((9 + parts,))],
-        compiler_params=params(59),
+        compiler_params=params(52),
         cost_estimate=cost(
             6 * slots * width * hidden_width, 4 * width * (slots + hidden_width) + 8 * slots * width
         ),

time: 174 us -> 172 us (0.989)
  no operation moved by 1% of the time
where the time goes in v6:
time: 172 us
  blocking collectives  74.5 us (43%)
  waiting for transfers between devices  39.6 us (23%)
  starting transfers between devices  36.8 us (21%)
  Pallas kernels  18.5 us (11%)
    all_to_all x2, blocking collectives, scatter(): return lax.all_to_all(value, axis, split_axis=0, concat_axis=0, tiled=True)  59 us
    ppermute x4, starting transfers between devices, shift(): return lax.ppermute(value, 'mp', [(i, (i + step) % 8) for i in range(8)])  24.7 us
    all_to_all x1, waiting for transfers between devices, scatter(): return lax.all_to_all(value, axis, split_axis=0, concat_axis=0, tiled=True)  22.2 us
    ppermute x4, waiting for transfers between devices, shift(): return lax.ppermute(value, 'mp', [(i, (i + step) % 8) for i in range(8)])  17.4 us
    all_gather x1, blocking collectives, gather_pieces(): lax.all_gather(piece, 'mp', axis=0, tiled=True, axis_index_groups=[[0, 2,...  15.5 us
    ppermute x3, starting transfers between devices, swap(): return lax.ppermute(value, 'dp', [(i, i ^ bit) for i in range(4)])  7.89 us
    pallas_call x1, Pallas kernels, expert(): pl.pallas_call(expert_kernel, out_shape=tuple((jax.ShapeDtypeStruct(shape...  6.72 us
    pallas_call x2, Pallas kernels, weight_terms(): pl.pallas_call(functools.partial(weight_kernel, turn), in_specs=[VMEM] *...  4.91 us
  transfers between devices with their start and end apart: 8, of which 4 were waited for; matrix products, arithmetic and copies ran while one was open for 0% of the time, Pallas kernels for 4%

profile of v6, /device:TPU:2, one launch (start us, length us, event | category | flops | bytes accessed | tf_op | source)
XLA Modules:
  0.0 171.6 jit_solution(14436159086103161900)
XLA Ops:
  0.6 3.7 %shard_map.111 = bf16[256,1536]{1,0:T(8,128)(2,1)} custom-call(s32[1]{0:T(128)} %bitcast.me_ref, s32[1,256]{1,0:T(1,128)} %bitcast.16, s32[1,256]{1,0:T(1,128)} %bitcast.18, s32[1,256]{1,0:T(1,128)} %bitcast.20, bf16[256]{0:T(256)(128)(2,1)} %gate_ref.3, bf16[256,2048]{1,0:T(8,128)(2,1)} %tokens.1, bf16[256,2048]{1,0:T(8,128)(2,1)} %grad_out.1), custom_call_target="tpu_custom_call" | custom-call | flops 536870912 | bytes 2621440 | tf_op jit(solution)/shard_map/pallas_call | solution.py:94
  4.4 38.1 %all_to_all.15 = bf16[32,8,1536]{2,1,0:T(8,128)(2,1)S(1)} all-to-all(bf16[32,8,1536]{2,1,0:T(8,128)(2,1)} %bitcast.24), channel_id=1, replica_groups=mesh['expert'=32,'mp'=8,'dp'=4] {'expert'}, dimensions={0} | all-to-all | bytes 1572864 | tf_op jit(solution)/shard_map/all_to_all | solution.py:324
  42.5 0.0 copy-start.7
  42.5 0.1 fusion
  42.6 16.8 %collective-permute-start.1 = (bf16[256,1280]{1,0:T(8,128)(2,1)S(1)}, bf16[256,1280]{1,0:T(8,128)(2,1)S(1)}, u32[]{:S(2)}, u32[]{:S(2)}) collective-permute-start(bf16[256,1280]{1,0:T(8,128)(2,1)S(1)} %get-tuple-element.28), channel_id=1, source_target_pairs={{0,28},{4,0},{8,4},{12,8},{16,12},{20,16},{24,20},{28,24},{1,29},{... | collective-permute-start | bytes 1966088 | tf_op jit(solution)/shard_map/ppermute | solution.py:308
  59.3 1.9 %collective-permute-start = (bf16[256,1280]{1,0:T(8,128)(2,1)S(1)}, bf16[256,1280]{1,0:T(8,128)(2,1)S(1)}, u32[]{:S(2)}, u32[]{:S(2)}) collective-permute-start(bf16[256,1280]{1,0:T(8,128)(2,1)S(1)} %get-tuple-element.29), channel_id=1, source_target_pairs={{0,4},{4,8},{8,12},{12,16},{16,20},{20,24},{24,28},{28,0},{1,5},{5... | collective-permute-start | bytes 1966088 | tf_op jit(solution)/shard_map/ppermute | solution.py:308
  61.3 9.6 %collective-permute-done.1.after = bf16[256,1280]{1,0:T(8,128)(2,1)S(1)} collective-permute-done((bf16[256,1280]{1,0:T(8,128)(2,1)S(1)}, bf16[256,1280]{1,0:T(8,128)(2,1)S(1)}, u32[]{:S(2)}, u32[]{:S(2)}) %collective-permute-start.1) | collective-permute-done | bytes 655392 | tf_op jit(solution)/shard_map/ppermute | solution.py:308
  70.9 5.3 %collective-permute-done.before = bf16[256,1280]{1,0:T(8,128)(2,1)S(1)} collective-permute-done((bf16[256,1280]{1,0:T(8,128)(2,1)S(1)}, bf16[256,1280]{1,0:T(8,128)(2,1)S(1)}, u32[]{:S(2)}, u32[]{:S(2)}) %collective-permute-start) | collective-permute-done | bytes 655392 | tf_op jit(solution)/shard_map/ppermute | solution.py:308
  76.2 0.0 copy-done.7
  76.2 6.7 %shard_map.112 = (bf16[8,272,256]{2,1,0:T(8,128)(2,1)}, bf16[256,3328]{1,0:T(8,128)(2,1)}, bf16[256,2048]{1,0:T(8,128)(2,1)}) custom-call(s32[1]{0:T(128)} %bitcast.me_ref, s32[1]{0:T(128)} %bitcast.4.data_ref, bf16[256,1536]{1,0:T(8,128)(2,1)} %bitcast.23, bf16[256,1280]{1,0:T(8,128)(2,1)S(1)} %collective-permute-done.before, ...), custom_call_target="tpu_custom_call" | custom-call | flops 2013265920 | bytes 11534336 | tf_op jit(solution)/shard_map/pallas_call | solution.py:186
  83.0 0.0 copy-start
  83.0 2.1 %collective-permute-start.2 = (bf16[256,3328]{1,0:T(8,128)(2,1)}, bf16[256,3328]{1,0:T(8,128)(2,1)S(1)}, u32[]{:S(2)}, u32[]{:S(2)}) collective-permute-start(bf16[256,3328]{1,0:T(8,128)(2,1)} %get-tuple-element.18.acts_ref), channel_id=1, source_target_pairs={{0,1},{1,0},{2,3},{3,2},{4,5},{5,4},{6,7},{7,6},{8,9},{9,8},{10,11... | collective-permute-start | bytes 5111816 | tf_op jit(solution)/shard_map/ppermute | solution.py:312
  85.0 4.3 %all-to-all-start.1 = ((bf16[8,272,256]{2,1,0:T(8,128)(2,1)}), bf16[8,272,256]{2,1,0:T(8,128)(2,1)}, u32[]{:S(2)}, u32[]{:S(2)}) async-start(bf16[8,272,256]{2,1,0:T(8,128)(2,1)} %get-tuple-element.16), calls=%async_computation.1 | async-start | bytes 2228224 | tf_op jit(solution)/shard_map/all_to_all | solution.py:324
  89.3 0.0 collective-permute-done.2.other_ref
  89.3 0.0 copy-done
  89.3 0.0 copy-start.1
  89.3 1.2 copy-done.1
  90.5 1.8 %shard_map.114 = (bf16[512,640]{1,0:T(8,128)(2,1)}, bf16[640,512]{1,0:T(8,128)(2,1)}) custom-call(bf16[256,2048]{1,0:T(8,128)(2,1)S(1)} %copy-done.1, bf16[256,3328]{1,0:T(8,128)(2,1)S(1)} %copy-done, bf16[256,3328]{1,0:T(8,128)(2,1)S(1)} %collective-permute-done.2.other_ref), custom_call_target="tpu_custom_call" | custom-call | flops 671088640 | bytes 3670016 | tf_op jit(solution)/shard_map/pallas_call | solution.py:294
  92.4 2.9 %collective-permute-start.3 = (bf16[512,640]{1,0:T(8,128)(2,1)}, bf16[512,640]{1,0:T(8,128)(2,1)}, u32[]{:S(2)}, u32[]{:S(2)}) collective-permute-start(bf16[512,640]{1,0:T(8,128)(2,1)} %get-tuple-element.19), channel_id=1, source_target_pairs={{0,2},{1,3},{2,0},{3,1},{4,6},{5,7},{6,4},{7,5},{8,10},{9,11},{10,... | collective-permute-start | bytes 1966088 | tf_op jit(solution)/shard_map/ppermute | solution.py:312
  95.2 3.0 %collective-permute-start.4 = (bf16[640,512]{1,0:T(8,128)(2,1)}, bf16[640,512]{1,0:T(8,128)(2,1)}, u32[]{:S(2)}, u32[]{:S(2)}) collective-permute-start(bf16[640,512]{1,0:T(8,128)(2,1)} %get-tuple-element.20), channel_id=1, source_target_pairs={{0,2},{1,3},{2,0},{3,1},{4,6},{5,7},{6,4},{7,5},{8,10},{9,11},{10,... | collective-permute-start | bytes 1966088 | tf_op jit(solution)/shard_map/ppermute | solution.py:312
  98.2 22.2 %all-to-all-done.1.terms_ref = bf16[8,272,256]{2,1,0:T(8,128)(2,1)} async-done(((bf16[8,272,256]{2,1,0:T(8,128)(2,1)}), bf16[8,272,256]{2,1,0:T(8,128)(2,1)}, u32[]{:S(2)}, u32[]{:S(2)}) %all-to-all-start.1) | async-done | bytes 1114144 | tf_op jit(solution)/shard_map/all_to_all | solution.py:324
  120.4 0.0 copy-start.2
  120.4 1.6 shard_map.113
  122.0 20.9 %all_to_all.16 = bf16[32,8,384]{2,1,0:T(8,128)(2,1)S(1)} all-to-all(bf16[32,8,384]{2,1,0:T(8,128)(2,1)S(1)} %bitcast.15), channel_id=1, replica_groups=mesh['expert'=32,'mp'=8,'dp'=4] {'expert'}, dimensions={0} | all-to-all | bytes 393216 | tf_op jit(solution)/shard_map/all_to_all | solution.py:324
  143.0 0.0 collective-permute-done.3.refs_0_
  143.0 0.0 collective-permute-done.4.refs_1_
  143.0 15.5 %all_gather.3.refs_0_ = bf16[1024,256]{1,0:T(8,128)(2,1)S(1)} all-gather(bf16[256,256]{1,0:T(8,128)(2,1)S(1)} %slice.17), channel_id=1, replica_groups={{0,8,16,24},{4,12,20,28},{1,9,17,25},{5,13,21,29},{2,10,18,26},{6,14,22..., dimensions={0}, use_global_device_ids=true | all-gather | bytes 655360 | tf_op jit(solution)/shard_map/all_gather | solution.py:316
  158.6 1.9 %collective-permute-start.6 = (bf16[512,256]{1,0:T(8,128)(2,1)S(1)}, bf16[512,256]{1,0:T(8,128)(2,1)S(1)}, u32[]{:S(2)}, u32[]{:S(2)}) collective-permute-start(bf16[512,256]{1,0:T(8,128)(2,1)S(1)} %get-tuple-element.30), channel_id=1, source_target_pairs={{0,28},{4,0},{8,4},{12,8},{16,12},{20,16},{24,20},{28,24},{1,29},{... | collective-permute-start | bytes 786440 | tf_op jit(solution)/shard_map/ppermute | solution.py:308
  160.5 0.0 copy-start.3
  160.5 0.0 copy-start.4
  160.5 0.0 copy-start.5
  160.5 0.0 copy-start.6
  160.5 4.1 %collective-permute-start.5 = (bf16[512,256]{1,0:T(8,128)(2,1)S(1)}, bf16[512,256]{1,0:T(8,128)(2,1)S(1)}, u32[]{:S(2)}, u32[]{:S(2)}) collective-permute-start(bf16[512,256]{1,0:T(8,128)(2,1)S(1)} %get-tuple-element.31), channel_id=1, source_target_pairs={{0,4},{4,8},{8,12},{12,16},{16,20},{20,24},{24,28},{28,0},{1,5},{5... | collective-permute-start | bytes 786440 | tf_op jit(solution)/shard_map/ppermute | solution.py:308
  164.6 0.0 copy-done.2
  164.6 3.1 %shard_map.116 = (bf16[512,640]{1,0:T(8,128)(2,1)}, bf16[640,512]{1,0:T(8,128)(2,1)}) custom-call(bf16[256,2048]{1,0:T(8,128)(2,1)S(1)} %copy-done.2, bf16[256,3328]{1,0:T(8,128)(2,1)S(1)} %copy-done, bf16[256,3328]{1,0:T(8,128)(2,1)S(1)} %collective-permute-done.2.other_ref, bf16[512,640]{1,0:T(8,128)(2,1)} %collective-permute-done.3.refs_0_, ...), custom_call_target="tpu_custom_call" | custom-call | flops 671088640 | bytes 3670016 | tf_op jit(solution)/shard_map/pallas_call | solution.py:294
  167.7 0.0 collective-permute-done.6.refs_2_
  167.7 2.5 %collective-permute-done.5.refs_1_ = bf16[512,256]{1,0:T(8,128)(2,1)S(1)} collective-permute-done((bf16[512,256]{1,0:T(8,128)(2,1)S(1)}, bf16[512,256]{1,0:T(8,128)(2,1)S(1)}, u32[]{:S(2)}, u32[]{:S(2)}) %collective-permute-start.5) | collective-permute-done | bytes 262176 | tf_op jit(solution)/shard_map/ppermute | solution.py:308
  170.2 0.0 copy-done.3
  170.2 0.0 copy-done.4
  170.2 0.0 copy-done.5
  170.2 0.0 copy-done.6
  170.2 1.5 shard_map.115
  (2 shorter events, 0.0 us)
Async XLA Ops:
  42.5 33.8 %copy-start.7 = (bf16[32,8,1536]{2,1,0:T(8,128)(2,1)}, bf16[32,8,1536]{2,1,0:T(8,128)(2,1)S(1)}, u32[]{:S(2)}) copy-start(bf16[32,8,1536]{2,1,0:T(8,128)(2,1)S(1)} %all_to_all.15) | copy-start | bytes 2359300
  42.6 28.3 %collective-permute-start.1 = (bf16[256,1280]{1,0:T(8,128)(2,1)S(1)}, bf16[256,1280]{1,0:T(8,128)(2,1)S(1)}, u32[]{:S(2)}, u32[]{:S(2)}) collective-permute-start(bf16[256,1280]{1,0:T(8,128)(2,1)S(1)} %get-tuple-element.28), channel_id=1, source_target_pairs={{0,28},{4,0},{8,4},{12,8},{16,12},{20,16},{24,20},{28,24},{1,29},{... | collective-permute-start | bytes 1966088 | tf_op jit(solution)/shard_map/ppermute | solution.py:308
  59.3 16.9 %collective-permute-start = (bf16[256,1280]{1,0:T(8,128)(2,1)S(1)}, bf16[256,1280]{1,0:T(8,128)(2,1)S(1)}, u32[]{:S(2)}, u32[]{:S(2)}) collective-permute-start(bf16[256,1280]{1,0:T(8,128)(2,1)S(1)} %get-tuple-element.29), channel_id=1, source_target_pairs={{0,4},{4,8},{8,12},{12,16},{16,20},{20,24},{24,28},{28,0},{1,5},{5... | collective-permute-start | bytes 1966088 | tf_op jit(solution)/shard_map/ppermute | solution.py:308
  83.0 6.3 %copy-start = (bf16[256,3328]{1,0:T(8,128)(2,1)S(1)}, bf16[256,3328]{1,0:T(8,128)(2,1)}, u32[]{:S(2)}) copy-start(bf16[256,3328]{1,0:T(8,128)(2,1)} %get-tuple-element.18.acts_ref) | copy-start | bytes 5111812
  83.0 6.3 %collective-permute-start.2 = (bf16[256,3328]{1,0:T(8,128)(2,1)}, bf16[256,3328]{1,0:T(8,128)(2,1)S(1)}, u32[]{:S(2)}, u32[]{:S(2)}) collective-permute-start(bf16[256,3328]{1,0:T(8,128)(2,1)} %get-tuple-element.18.acts_ref), channel_id=1, source_target_pairs={{0,1},{1,0},{2,3},{3,2},{4,5},{5,4},{6,7},{7,6},{8,9},{9,8},{10,11... | collective-permute-start | bytes 5111816 | tf_op jit(solution)/shard_map/ppermute | solution.py:312
  85.0 35.4 %all-to-all-start.1 = ((bf16[8,272,256]{2,1,0:T(8,128)(2,1)}), bf16[8,272,256]{2,1,0:T(8,128)(2,1)}, u32[]{:S(2)}, u32[]{:S(2)}) async-start(bf16[8,272,256]{2,1,0:T(8,128)(2,1)} %get-tuple-element.16), calls=%async_computation.1 | async-start | bytes 2228224 | tf_op jit(solution)/shard_map/all_to_all | solution.py:324
  89.3 1.2 copy-start.1
  92.4 50.6 %collective-permute-start.3 = (bf16[512,640]{1,0:T(8,128)(2,1)}, bf16[512,640]{1,0:T(8,128)(2,1)}, u32[]{:S(2)}, u32[]{:S(2)}) collective-permute-start(bf16[512,640]{1,0:T(8,128)(2,1)} %get-tuple-element.19), channel_id=1, source_target_pairs={{0,2},{1,3},{2,0},{3,1},{4,6},{5,7},{6,4},{7,5},{8,10},{9,11},{10,... | collective-permute-start | bytes 1966088 | tf_op jit(solution)/shard_map/ppermute | solution.py:312
  95.2 47.8 %collective-permute-start.4 = (bf16[640,512]{1,0:T(8,128)(2,1)}, bf16[640,512]{1,0:T(8,128)(2,1)}, u32[]{:S(2)}, u32[]{:S(2)}) collective-permute-start(bf16[640,512]{1,0:T(8,128)(2,1)} %get-tuple-element.20), channel_id=1, source_target_pairs={{0,2},{1,3},{2,0},{3,1},{4,6},{5,7},{6,4},{7,5},{8,10},{9,11},{10,... | collective-permute-start | bytes 1966088 | tf_op jit(solution)/shard_map/ppermute | solution.py:312
  120.4 44.2 %copy-start.2 = (bf16[256,2048]{1,0:T(8,128)(2,1)S(1)}, bf16[256,2048]{1,0:T(8,128)(2,1)}, u32[]{:S(2)}) copy-start(bf16[256,2048]{1,0:T(8,128)(2,1)} %get-tuple-element.17.mine_ref) | copy-start | bytes 3145732
  158.6 9.1 %collective-permute-start.6 = (bf16[512,256]{1,0:T(8,128)(2,1)S(1)}, bf16[512,256]{1,0:T(8,128)(2,1)S(1)}, u32[]{:S(2)}, u32[]{:S(2)}) collective-permute-start(bf16[512,256]{1,0:T(8,128)(2,1)S(1)} %get-tuple-element.30), channel_id=1, source_target_pairs={{0,28},{4,0},{8,4},{12,8},{16,12},{20,16},{24,20},{28,24},{1,29},{... | collective-permute-start | bytes 786440 | tf_op jit(solution)/shard_map/ppermute | solution.py:308
  160.5 9.7 %copy-start.3 = (s32[256]{0:T(256)S(1)}, s32[256]{0:T(256)}, u32[]{:S(2)}) copy-start(s32[256]{0:T(256)} %param.11) | copy-start | bytes 3076
  160.5 9.6 %copy-start.4 = (s32[256]{0:T(256)S(1)}, s32[256]{0:T(256)}, u32[]{:S(2)}) copy-start(s32[256]{0:T(256)} %param.12) | copy-start | bytes 3076
  160.5 9.6 %copy-start.5 = (s32[256]{0:T(256)S(1)}, s32[256]{0:T(256)}, u32[]{:S(2)}) copy-start(s32[256]{0:T(256)} %param.13) | copy-start | bytes 3076
  160.5 9.6 %copy-start.6 = (bf16[256]{0:T(256)(128)(2,1)S(1)}, bf16[256]{0:T(256)(128)(2,1)}, u32[]{:S(2)}) copy-start(bf16[256]{0:T(256)(128)(2,1)} %gate_ref.3) | copy-start | bytes 1540
  160.5 9.6 %collective-permute-start.5 = (bf16[512,256]{1,0:T(8,128)(2,1)S(1)}, bf16[512,256]{1,0:T(8,128)(2,1)S(1)}, u32[]{:S(2)}, u32[]{:S(2)}) collective-permute-start(bf16[512,256]{1,0:T(8,128)(2,1)S(1)} %get-tuple-element.31), channel_id=1, source_target_pairs={{0,4},{4,8},{8,12},{12,16},{16,20},{20,24},{24,28},{28,0},{1,5},{5... | collective-permute-start | bytes 786440 | tf_op jit(solution)/shard_map/ppermute | solution.py:308

commit v7 on v6

--- a/solution.py
+++ b/solution.py
@@ -268,40 +268,49 @@
     )(me, *index_rows, gate, home, *pieces)
 
 
-def weight_kernel(turn, mine_ref, acts_ref, other_ref, *refs):
-    added, (in_ref, out_ref) = refs[:-2], refs[-2:]
+def term(left, mine_ref, acts_ref, other_ref, turn, first, activations):
+    quarter = mine_ref.shape[1] // 4
+    cols = slice((turn + first) * quarter, (turn + first + 1) * quarter)
+    total = None
+    for rows_ref, from_ref in ((mine_ref, acts_ref), (other_ref, other_ref)):
+        pair = rows_ref[:, cols], from_ref[:, activations]
+        product = dot(*(pair if left else pair[::-1]), 0, 0)
+        total = product if total is None else total + product
+    return total
+
+
+def pass_kernel(mine_ref, acts_ref, other_ref, out_ref):
+    quarter, width = mine_ref.shape[1] // 4, out_ref.shape[1]
+    grads = slice(4 * quarter, 4 * quarter + width)
+    hiddens = slice(4 * quarter + width, 4 * quarter + 2 * width)
+    out_ref[:quarter] = term(True, mine_ref, acts_ref, other_ref, 1, 0, grads).astype(BF16)
+    out_ref[quarter:] = term(True, mine_ref, acts_ref, other_ref, 1, 2, hiddens).astype(BF16)
+
+
+def keep_kernel(mine_ref, acts_ref, other_ref, added_ref, in_ref, out_ref):
     quarter, width = in_ref.shape
     grads = slice(4 * quarter, 4 * quarter + width)
     hiddens = slice(4 * quarter + width, 4 * quarter + 2 * width)
-    x_cols = slice(turn * quarter, (turn + 1) * quarter)
-    s_cols = slice((turn + 2) * quarter, (turn + 3) * quarter)
-    first = dot(mine_ref[:, x_cols], acts_ref[:, grads], 0, 0)
-    first = first + dot(other_ref[:, x_cols], other_ref[:, grads], 0, 0)
-    if added:
-        first = first + added[0][...].astype(F32)
-    in_ref[...] = first.astype(BF16)
-    second = dot(acts_ref[:, hiddens], mine_ref[:, s_cols], 0, 0)
-    second = second + dot(other_ref[:, hiddens], other_ref[:, s_cols], 0, 0)
-    if added:
-        second = second + added[1][...].astype(F32)
-    out_ref[...] = second.astype(BF16)
-
-
-def weight_terms(turn, mine, acts, other, added=()):
+    first = term(True, mine_ref, acts_ref, other_ref, 0, 0, grads)
+    in_ref[...] = (first + added_ref[:quarter].astype(F32)).astype(BF16)
+    second = term(False, mine_ref, acts_ref, other_ref, 0, 2, hiddens)
+    out_ref[...] = (second + added_ref[quarter:].astype(F32).T).astype(BF16)
+
+
+def weight_terms(mine, acts, other, added=None):
     slots = mine.shape[0]
     quarter = mine.shape[1] // 4
     width = (acts.shape[1] - 4 * quarter) // 2
-    return pl.pallas_call(
-        functools.partial(weight_kernel, turn),
-        in_specs=[VMEM] * (3 + len(added)),
-        out_specs=(VMEM, VMEM),
-        out_shape=(
-            jax.ShapeDtypeStruct((quarter, width), BF16),
-            jax.ShapeDtypeStruct((width, quarter), BF16),
-        ),
-        compiler_params=params(24),
+    shapes = ((2 * quarter, width),) if added is None else ((quarter, width), (width, quarter))
+    args = (mine, acts, other) if added is None else (mine, acts, other, added)
+    return pl.pallas_call(
+        pass_kernel if added is None else keep_kernel,
+        in_specs=[VMEM] * len(args),
+        out_specs=(VMEM,) * len(shapes),
+        out_shape=tuple(jax.ShapeDtypeStruct(shape, BF16) for shape in shapes),
+        compiler_params=params(24 if added is None else 24),
         cost_estimate=cost(8 * slots * quarter * width, 8 * slots * (quarter + width) + 4 * quarter * width),
-    )(mine, acts, other, *added)
+    )(*args)
 
 
 def shift(value, step):
@@ -341,12 +350,12 @@
     terms = scatter(rows, "mp")
 
     other = swap(acts, 1)
-    added = [swap(value, 2) for value in weight_terms(1, mine, acts, other)]
+    added = swap(weight_terms(mine, acts, other)[0], 2)
 
     total = sum_terms(terms, slots)
     home = scatter(total.reshape(experts, CAP, total.shape[1]), "expert").reshape(total.shape)
     home, added = lax.optimization_barrier((home, added))
-    grad_w_in, grad_w_out = weight_terms(0, mine, acts, other, added)
+    grad_w_in, grad_w_out = weight_terms(mine, acts, other, added)
     pieces = gather_pieces(home[:, : width // parts])
     grad_tokens, grad_gate = finish(me, index_rows, gate, home, pieces, width)
     return (grad_tokens, grad_gate, grad_w_in[None], grad_w_out[None])

time: 172 us -> 172 us (level)
  starting transfers between devices: 36.8 us -> 33.8 us
  waiting for transfers between devices: 39.6 us -> 42.3 us
    ppermute x3 -> x2, starting transfers between devices: 7.89 us -> 4.9 us  [swap(): return lax.ppermute(value, 'dp', [(i, i ^ bit) for i in range(4)])]
    all_to_all x1, waiting for transfers between devices: 22.2 us -> 24.9 us  [scatter(): return lax.all_to_all(value, axis, split_axis=0, concat_axis=0, tiled=True)]
  transfers between devices with their start and end apart: 8 -> 7, of which waited for: 4 -> 4; matrix products, arithmetic and copies ran while one was open for 0% -> 0% of each run, Pallas kernels for 4% -> 4%
where the time goes in v7:
time: 172 us
  blocking collectives  74.5 us (43%)
  waiting for transfers between devices  42.3 us (25%)
  starting transfers between devices  33.8 us (20%)
  Pallas kernels  18.7 us (11%)
    all_to_all x2, blocking collectives, scatter(): return lax.all_to_all(value, axis, split_axis=0, concat_axis=0, tiled=True)  59 us
    all_to_all x1, waiting for transfers between devices, scatter(): return lax.all_to_all(value, axis, split_axis=0, concat_axis=0, tiled=True)  24.9 us
    ppermute x4, starting transfers between devices, shift(): return lax.ppermute(value, 'mp', [(i, (i + step) % 8) for i in range(8)])  24.7 us
    ppermute x4, waiting for transfers between devices, shift(): return lax.ppermute(value, 'mp', [(i, (i + step) % 8) for i in range(8)])  17.4 us
    all_gather x1, blocking collectives, gather_pieces(): lax.all_gather(piece, 'mp', axis=0, tiled=True, axis_index_groups=[[0, 2,...  15.5 us
    pallas_call x1, Pallas kernels, expert(): pl.pallas_call(expert_kernel, out_shape=tuple((jax.ShapeDtypeStruct(shape...  6.69 us
    pallas_call x2, Pallas kernels, weight_terms(): pl.pallas_call(pass_kernel if added is None else keep_kernel, in_specs=[V...  5.19 us
    ppermute x2, starting transfers between devices, swap(): return lax.ppermute(value, 'dp', [(i, i ^ bit) for i in range(4)])  4.9 us
  transfers between devices with their start and end apart: 7, of which 4 were waited for; matrix products, arithmetic and copies ran while one was open for 0% of the time, Pallas kernels for 4%

profile of v7, /device:TPU:2, one launch (start us, length us, event | category | flops | bytes accessed | tf_op | source)
XLA Modules:
  0.0 171.6 jit_solution(3469227008500775915)
XLA Ops:
  0.6 3.7 %shard_map.111 = bf16[256,1536]{1,0:T(8,128)(2,1)} custom-call(s32[1]{0:T(128)} %bitcast.me_ref, s32[1,256]{1,0:T(1,128)} %bitcast.16, s32[1,256]{1,0:T(1,128)} %bitcast.18, s32[1,256]{1,0:T(1,128)} %bitcast.20, bf16[256]{0:T(256)(128)(2,1)} %gate_ref.3, bf16[256,2048]{1,0:T(8,128)(2,1)} %tokens.1, bf16[256,2048]{1,0:T(8,128)(2,1)} %grad_out.1), custom_call_target="tpu_custom_call" | custom-call | flops 536870912 | bytes 2621440 | tf_op jit(solution)/shard_map/pallas_call | solution.py:94
  4.4 38.1 %all_to_all.15 = bf16[32,8,1536]{2,1,0:T(8,128)(2,1)S(1)} all-to-all(bf16[32,8,1536]{2,1,0:T(8,128)(2,1)} %bitcast.24), channel_id=1, replica_groups=mesh['expert'=32,'mp'=8,'dp'=4] {'expert'}, dimensions={0} | all-to-all | bytes 1572864 | tf_op jit(solution)/shard_map/all_to_all | solution.py:333
  42.5 0.0 copy-start.7
  42.5 0.1 fusion
  42.6 16.8 %collective-permute-start.1 = (bf16[256,1280]{1,0:T(8,128)(2,1)S(1)}, bf16[256,1280]{1,0:T(8,128)(2,1)S(1)}, u32[]{:S(2)}, u32[]{:S(2)}) collective-permute-start(bf16[256,1280]{1,0:T(8,128)(2,1)S(1)} %get-tuple-element.22), channel_id=1, source_target_pairs={{0,28},{4,0},{8,4},{12,8},{16,12},{20,16},{24,20},{28,24},{1,29},{... | collective-permute-start | bytes 1966088 | tf_op jit(solution)/shard_map/ppermute | solution.py:317
  59.3 1.9 %collective-permute-start = (bf16[256,1280]{1,0:T(8,128)(2,1)S(1)}, bf16[256,1280]{1,0:T(8,128)(2,1)S(1)}, u32[]{:S(2)}, u32[]{:S(2)}) collective-permute-start(bf16[256,1280]{1,0:T(8,128)(2,1)S(1)} %get-tuple-element.23), channel_id=1, source_target_pairs={{0,4},{4,8},{8,12},{12,16},{16,20},{20,24},{24,28},{28,0},{1,5},{5... | collective-permute-start | bytes 1966088 | tf_op jit(solution)/shard_map/ppermute | solution.py:317
  61.3 9.6 %collective-permute-done.1.after = bf16[256,1280]{1,0:T(8,128)(2,1)S(1)} collective-permute-done((bf16[256,1280]{1,0:T(8,128)(2,1)S(1)}, bf16[256,1280]{1,0:T(8,128)(2,1)S(1)}, u32[]{:S(2)}, u32[]{:S(2)}) %collective-permute-start.1) | collective-permute-done | bytes 655392 | tf_op jit(solution)/shard_map/ppermute | solution.py:317
  70.9 5.3 %collective-permute-done.before = bf16[256,1280]{1,0:T(8,128)(2,1)S(1)} collective-permute-done((bf16[256,1280]{1,0:T(8,128)(2,1)S(1)}, bf16[256,1280]{1,0:T(8,128)(2,1)S(1)}, u32[]{:S(2)}, u32[]{:S(2)}) %collective-permute-start) | collective-permute-done | bytes 655392 | tf_op jit(solution)/shard_map/ppermute | solution.py:317
  76.2 0.0 copy-done.7
  76.2 6.7 %shard_map.112 = (bf16[8,272,256]{2,1,0:T(8,128)(2,1)}, bf16[256,3328]{1,0:T(8,128)(2,1)}, bf16[256,2048]{1,0:T(8,128)(2,1)}) custom-call(s32[1]{0:T(128)} %bitcast.me_ref, s32[1]{0:T(128)} %bitcast.4.data_ref, bf16[256,1536]{1,0:T(8,128)(2,1)} %bitcast.23, bf16[256,1280]{1,0:T(8,128)(2,1)S(1)} %collective-permute-done.before, ...), custom_call_target="tpu_custom_call" | custom-call | flops 2013265920 | bytes 11534336 | tf_op jit(solution)/shard_map/pallas_call | solution.py:186
  82.9 0.0 copy-start
  82.9 2.1 %collective-permute-start.2 = (bf16[256,3328]{1,0:T(8,128)(2,1)}, bf16[256,3328]{1,0:T(8,128)(2,1)S(1)}, u32[]{:S(2)}, u32[]{:S(2)}) collective-permute-start(bf16[256,3328]{1,0:T(8,128)(2,1)} %get-tuple-element.15.acts_ref), channel_id=1, source_target_pairs={{0,1},{1,0},{2,3},{3,2},{4,5},{5,4},{6,7},{7,6},{8,9},{9,8},{10,11... | collective-permute-start | bytes 5111816 | tf_op jit(solution)/shard_map/ppermute | solution.py:321
  85.0 4.3 %all-to-all-start.1 = ((bf16[8,272,256]{2,1,0:T(8,128)(2,1)}), bf16[8,272,256]{2,1,0:T(8,128)(2,1)}, u32[]{:S(2)}, u32[]{:S(2)}) async-start(bf16[8,272,256]{2,1,0:T(8,128)(2,1)} %get-tuple-element.13), calls=%async_computation.1 | async-start | bytes 2228224 | tf_op jit(solution)/shard_map/all_to_all | solution.py:333
  89.3 0.0 collective-permute-done.2.other_ref
  89.3 0.0 copy-done
  89.3 0.0 copy-start.1
  89.3 1.2 copy-done.1
  90.5 2.1 %shard_map.114 = bf16[1024,640]{1,0:T(8,128)(2,1)} custom-call(bf16[256,2048]{1,0:T(8,128)(2,1)S(1)} %copy-done.1, bf16[256,3328]{1,0:T(8,128)(2,1)S(1)} %copy-done, bf16[256,3328]{1,0:T(8,128)(2,1)S(1)} %collective-permute-done.2.other_ref), custom_call_target="tpu_custom_call" | custom-call | flops 671088640 | bytes 3670016 | tf_op jit(solution)/shard_map/pallas_call | solution.py:306
  92.6 2.9 %collective-permute-start.3 = (bf16[1024,640]{1,0:T(8,128)(2,1)}, bf16[1024,640]{1,0:T(8,128)(2,1)}, u32[]{:S(2)}, u32[]{:S(2)}) collective-permute-start(bf16[1024,640]{1,0:T(8,128)(2,1)} %shard_map.114), channel_id=1, source_target_pairs={{0,2},{1,3},{2,0},{3,1},{4,6},{5,7},{6,4},{7,5},{8,10},{9,11},{10,... | collective-permute-start | bytes 3932168 | tf_op jit(solution)/shard_map/ppermute | solution.py:321
  95.5 24.9 %all-to-all-done.1.terms_ref = bf16[8,272,256]{2,1,0:T(8,128)(2,1)} async-done(((bf16[8,272,256]{2,1,0:T(8,128)(2,1)}), bf16[8,272,256]{2,1,0:T(8,128)(2,1)}, u32[]{:S(2)}, u32[]{:S(2)}) %all-to-all-start.1) | async-done | bytes 1114144 | tf_op jit(solution)/shard_map/all_to_all | solution.py:333
  120.4 0.0 copy-start.2
  120.4 1.6 shard_map.113
  122.0 20.9 %all_to_all.16 = bf16[32,8,384]{2,1,0:T(8,128)(2,1)S(1)} all-to-all(bf16[32,8,384]{2,1,0:T(8,128)(2,1)S(1)} %bitcast.15), channel_id=1, replica_groups=mesh['expert'=32,'mp'=8,'dp'=4] {'expert'}, dimensions={0} | all-to-all | bytes 393216 | tf_op jit(solution)/shard_map/all_to_all | solution.py:333
  143.0 0.0 collective-permute-done.3.added_ref
  143.0 15.5 %all_gather.3.refs_0_ = bf16[1024,256]{1,0:T(8,128)(2,1)S(1)} all-gather(bf16[256,256]{1,0:T(8,128)(2,1)S(1)} %slice.17), channel_id=1, replica_groups={{0,8,16,24},{4,12,20,28},{1,9,17,25},{5,13,21,29},{2,10,18,26},{6,14,22..., dimensions={0}, use_global_device_ids=true | all-gather | bytes 655360 | tf_op jit(solution)/shard_map/all_gather | solution.py:325
  158.5 1.9 %collective-permute-start.5 = (bf16[512,256]{1,0:T(8,128)(2,1)S(1)}, bf16[512,256]{1,0:T(8,128)(2,1)S(1)}, u32[]{:S(2)}, u32[]{:S(2)}) collective-permute-start(bf16[512,256]{1,0:T(8,128)(2,1)S(1)} %get-tuple-element.24), channel_id=1, source_target_pairs={{0,28},{4,0},{8,4},{12,8},{16,12},{20,16},{24,20},{28,24},{1,29},{... | collective-permute-start | bytes 786440 | tf_op jit(solution)/shard_map/ppermute | solution.py:317
  160.5 0.0 copy-start.3
  160.5 0.0 copy-start.4
  160.5 0.0 copy-start.5
  160.5 0.0 copy-start.6
  160.5 4.1 %collective-permute-start.4 = (bf16[512,256]{1,0:T(8,128)(2,1)S(1)}, bf16[512,256]{1,0:T(8,128)(2,1)S(1)}, u32[]{:S(2)}, u32[]{:S(2)}) collective-permute-start(bf16[512,256]{1,0:T(8,128)(2,1)S(1)} %get-tuple-element.25), channel_id=1, source_target_pairs={{0,4},{4,8},{8,12},{12,16},{16,20},{20,24},{24,28},{28,0},{1,5},{5... | collective-permute-start | bytes 786440 | tf_op jit(solution)/shard_map/ppermute | solution.py:317
  164.6 0.0 copy-done.2
  164.6 3.1 %shard_map.116 = (bf16[512,640]{1,0:T(8,128)(2,1)}, bf16[640,512]{1,0:T(8,128)(2,1)}) custom-call(bf16[256,2048]{1,0:T(8,128)(2,1)S(1)} %copy-done.2, bf16[256,3328]{1,0:T(8,128)(2,1)S(1)} %copy-done, bf16[256,3328]{1,0:T(8,128)(2,1)S(1)} %collective-permute-done.2.other_ref, bf16[1024,640]{1,0:T(8,128)(2,1)} %collective-permute-done.3.added_ref), custom_call_target="tpu_custom_call" | custom-call | flops 671088640 | bytes 3670016 | tf_op jit(solution)/shard_map/pallas_call | solution.py:306
  167.7 0.0 collective-permute-done.5.refs_2_
  167.7 2.4 %collective-permute-done.4.refs_1_ = bf16[512,256]{1,0:T(8,128)(2,1)S(1)} collective-permute-done((bf16[512,256]{1,0:T(8,128)(2,1)S(1)}, bf16[512,256]{1,0:T(8,128)(2,1)S(1)}, u32[]{:S(2)}, u32[]{:S(2)}) %collective-permute-start.4) | collective-permute-done | bytes 262176 | tf_op jit(solution)/shard_map/ppermute | solution.py:317
  170.1 0.0 copy-done.3
  170.1 0.0 copy-done.4
  170.1 0.0 copy-done.5
  170.1 0.0 copy-done.6
  170.1 1.5 shard_map.115
  (2 shorter events, 0.0 us)
Async XLA Ops:
  42.5 33.8 %copy-start.7 = (bf16[32,8,1536]{2,1,0:T(8,128)(2,1)}, bf16[32,8,1536]{2,1,0:T(8,128)(2,1)S(1)}, u32[]{:S(2)}) copy-start(bf16[32,8,1536]{2,1,0:T(8,128)(2,1)S(1)} %all_to_all.15) | copy-start | bytes 2359300
  42.6 28.3 %collective-permute-start.1 = (bf16[256,1280]{1,0:T(8,128)(2,1)S(1)}, bf16[256,1280]{1,0:T(8,128)(2,1)S(1)}, u32[]{:S(2)}, u32[]{:S(2)}) collective-permute-start(bf16[256,1280]{1,0:T(8,128)(2,1)S(1)} %get-tuple-element.22), channel_id=1, source_target_pairs={{0,28},{4,0},{8,4},{12,8},{16,12},{20,16},{24,20},{28,24},{1,29},{... | collective-permute-start | bytes 1966088 | tf_op jit(solution)/shard_map/ppermute | solution.py:317
  59.3 16.9 %collective-permute-start = (bf16[256,1280]{1,0:T(8,128)(2,1)S(1)}, bf16[256,1280]{1,0:T(8,128)(2,1)S(1)}, u32[]{:S(2)}, u32[]{:S(2)}) collective-permute-start(bf16[256,1280]{1,0:T(8,128)(2,1)S(1)} %get-tuple-element.23), channel_id=1, source_target_pairs={{0,4},{4,8},{8,12},{12,16},{16,20},{20,24},{24,28},{28,0},{1,5},{5... | collective-permute-start | bytes 1966088 | tf_op jit(solution)/shard_map/ppermute | solution.py:317
  82.9 6.3 %copy-start = (bf16[256,3328]{1,0:T(8,128)(2,1)S(1)}, bf16[256,3328]{1,0:T(8,128)(2,1)}, u32[]{:S(2)}) copy-start(bf16[256,3328]{1,0:T(8,128)(2,1)} %get-tuple-element.15.acts_ref) | copy-start | bytes 5111812
  82.9 6.3 %collective-permute-start.2 = (bf16[256,3328]{1,0:T(8,128)(2,1)}, bf16[256,3328]{1,0:T(8,128)(2,1)S(1)}, u32[]{:S(2)}, u32[]{:S(2)}) collective-permute-start(bf16[256,3328]{1,0:T(8,128)(2,1)} %get-tuple-element.15.acts_ref), channel_id=1, source_target_pairs={{0,1},{1,0},{2,3},{3,2},{4,5},{5,4},{6,7},{7,6},{8,9},{9,8},{10,11... | collective-permute-start | bytes 5111816 | tf_op jit(solution)/shard_map/ppermute | solution.py:321
  85.0 35.4 %all-to-all-start.1 = ((bf16[8,272,256]{2,1,0:T(8,128)(2,1)}), bf16[8,272,256]{2,1,0:T(8,128)(2,1)}, u32[]{:S(2)}, u32[]{:S(2)}) async-start(bf16[8,272,256]{2,1,0:T(8,128)(2,1)} %get-tuple-element.13), calls=%async_computation.1 | async-start | bytes 2228224 | tf_op jit(solution)/shard_map/all_to_all | solution.py:333
  89.3 1.2 copy-start.1
  92.6 50.4 %collective-permute-start.3 = (bf16[1024,640]{1,0:T(8,128)(2,1)}, bf16[1024,640]{1,0:T(8,128)(2,1)}, u32[]{:S(2)}, u32[]{:S(2)}) collective-permute-start(bf16[1024,640]{1,0:T(8,128)(2,1)} %shard_map.114), channel_id=1, source_target_pairs={{0,2},{1,3},{2,0},{3,1},{4,6},{5,7},{6,4},{7,5},{8,10},{9,11},{10,... | collective-permute-start | bytes 3932168 | tf_op jit(solution)/shard_map/ppermute | solution.py:321
  120.4 44.2 %copy-start.2 = (bf16[256,2048]{1,0:T(8,128)(2,1)S(1)}, bf16[256,2048]{1,0:T(8,128)(2,1)}, u32[]{:S(2)}) copy-start(bf16[256,2048]{1,0:T(8,128)(2,1)} %get-tuple-element.14.mine_ref) | copy-start | bytes 3145732
  158.5 9.2 %collective-permute-start.5 = (bf16[512,256]{1,0:T(8,128)(2,1)S(1)}, bf16[512,256]{1,0:T(8,128)(2,1)S(1)}, u32[]{:S(2)}, u32[]{:S(2)}) collective-permute-start(bf16[512,256]{1,0:T(8,128)(2,1)S(1)} %get-tuple-element.24), channel_id=1, source_target_pairs={{0,28},{4,0},{8,4},{12,8},{16,12},{20,16},{24,20},{28,24},{1,29},{... | collective-permute-start | bytes 786440 | tf_op jit(solution)/shard_map/ppermute | solution.py:317
  160.5 9.7 %copy-start.3 = (s32[256]{0:T(256)S(1)}, s32[256]{0:T(256)}, u32[]{:S(2)}) copy-start(s32[256]{0:T(256)} %param.11) | copy-start | bytes 3076
  160.5 9.6 %copy-start.4 = (s32[256]{0:T(256)S(1)}, s32[256]{0:T(256)}, u32[]{:S(2)}) copy-start(s32[256]{0:T(256)} %param.12) | copy-start | bytes 3076
  160.5 9.6 %copy-start.5 = (s32[256]{0:T(256)S(1)}, s32[256]{0:T(256)}, u32[]{:S(2)}) copy-start(s32[256]{0:T(256)} %param.13) | copy-start | bytes 3076
  160.5 9.6 %copy-start.6 = (bf16[256]{0:T(256)(128)(2,1)S(1)}, bf16[256]{0:T(256)(128)(2,1)}, u32[]{:S(2)}) copy-start(bf16[256]{0:T(256)(128)(2,1)} %gate_ref.3) | copy-start | bytes 1540
  160.5 9.6 %collective-permute-start.4 = (bf16[512,256]{1,0:T(8,128)(2,1)S(1)}, bf16[512,256]{1,0:T(8,128)(2,1)S(1)}, u32[]{:S(2)}, u32[]{:S(2)}) collective-permute-start(bf16[512,256]{1,0:T(8,128)(2,1)S(1)} %get-tuple-element.25), channel_id=1, source_target_pairs={{0,4},{4,8},{8,12},{12,16},{16,20},{20,24},{24,28},{28,0},{1,5},{5... | collective-permute-start | bytes 786440 | tf_op jit(solution)/shard_map/ppermute | solution.py:317

commit v8 on v7

--- a/solution.py
+++ b/solution.py
@@ -232,25 +232,28 @@
 
 
 def finish_kernel(me_ref, expert_ref, slot_ref, kept_ref, gate_ref, home_ref, *refs):
-    same_ref, low_ref, high_ref, tokens_ref, gates_ref = refs
-    slots, block = home_ref.shape[0], same_ref.shape[1]
+    own_ref, fifth_ref, second_ref, before_ref, after_ref, tokens_ref, gates_ref = refs
+    slots, block = own_ref.shape
     hits = slot_hits(expert_ref, slot_ref, kept_ref, slots)
     column = home_ref[:, block : block + 1].astype(F32)
     picked = jnp.sum(jnp.where(hits, column, 0.0), axis=0, keepdims=True)
     gate_row = gate_ref[...].astype(F32).reshape(1, -1)
     gates_ref[...] = (picked / gate_row).astype(BF16).reshape(-1)
     choose = jnp.where(hits, 1.0, 0.0).T.astype(BF16)
-    odd = me_ref[0] & 1
-
-    def store(index, piece):
-        place = pl.multiple_of(index * block, block)
-        tokens_ref[:, pl.ds(place, block)] = dot(choose, piece, 1, 0).astype(BF16)
-
-    for k in range(4):
-        store(2 * k + odd, same_ref[k * slots : (k + 1) * slots, :])
-    for k in range(2):
-        store(2 * k + 1 - odd, low_ref[k * slots : (k + 1) * slots, :])
-        store(2 * k + 5 - odd, high_ref[k * slots : (k + 1) * slots, :])
+    half = slots // 2
+
+    def store(offset, value):
+        place = pl.multiple_of(((me_ref[0] + offset) & 7) * block, block)
+        tokens_ref[:, pl.ds(place, block)] = value.astype(BF16)
+
+    whole_pieces = (
+        (0, own_ref, 0), (5, fifth_ref, 0), (2, second_ref, 0),
+        (7, before_ref, 0), (4, before_ref, slots), (6, after_ref, half), (3, after_ref, slots + half),
+    )
+    for offset, ref, start in whole_pieces:
+        store(offset, dot(choose, ref[start : start + slots, :], 1, 0))
+    low = dot(choose[:, :half], before_ref[2 * slots :, :], 1, 0)
+    store(1, low + dot(choose[:, half:], after_ref[:half, :], 1, 0))
 
 
 def finish(me, index_rows, gate, home, pieces, width):
@@ -322,11 +325,11 @@
 
 
 def gather_pieces(piece):
-    same = lax.all_gather(
-        piece, "mp", axis=0, tiled=True, axis_index_groups=[[0, 2, 4, 6], [1, 3, 5, 7]]
-    )
-    half = same.shape[0] // 2
-    return same, shift(same[:half], 1), shift(same[half:], -1)
+    held = piece, shift(piece, 3), shift(piece, -2)
+    half = piece.shape[0] // 2
+    before = jnp.concatenate([held[0], held[1], held[2][:half]])
+    after = jnp.concatenate([held[0][half:], held[1], held[2]])
+    return held + (shift(before, 1), shift(after, -1))
 
 
 def scatter(value, axis):

time: 172 us -> 174 us (1.012)
  blocking collectives: 74.5 us -> 59 us
  waiting for transfers between devices: 42.3 us -> 53.5 us
  starting transfers between devices: 33.8 us -> 40.2 us
    all_gather x1 -> x0, blocking collectives: 15.5 us -> none  [gather_pieces(): lax.all_gather(piece, 'mp', axis=0, tiled=True, axis_index_groups=[[0, 2,...]
    ppermute x4 -> x6, waiting for transfers between devices: 17.4 us -> 28.6 us  [shift(): return lax.ppermute(value, 'mp', [(i, (i + step) % 8) for i in range(8)])]
    ppermute x4 -> x6, starting transfers between devices: 24.7 us -> 31 us  [shift(): return lax.ppermute(value, 'mp', [(i, (i + step) % 8) for i in range(8)])]
  transfers between devices with their start and end apart: 7 -> 9, of which waited for: 4 -> 7; matrix products, arithmetic and copies ran while one was open for 0% -> 0% of each run, Pallas kernels for 4% -> 4%
where the time goes in v8:
time: 174 us
  blocking collectives  59 us (34%)
  waiting for transfers between devices  53.5 us (31%)
  starting transfers between devices  40.2 us (23%)
  Pallas kernels  18.8 us (11%)
    all_to_all x2, blocking collectives, scatter(): return lax.all_to_all(value, axis, split_axis=0, concat_axis=0, tiled=True)  59 us
    ppermute x6, starting transfers between devices, shift(): return lax.ppermute(value, 'mp', [(i, (i + step) % 8) for i in range(8)])  31 us
    ppermute x6, waiting for transfers between devices, shift(): return lax.ppermute(value, 'mp', [(i, (i + step) % 8) for i in range(8)])  28.6 us
    all_to_all x1, waiting for transfers between devices, scatter(): return lax.all_to_all(value, axis, split_axis=0, concat_axis=0, tiled=True)  24.9 us
    pallas_call x1, Pallas kernels, expert(): pl.pallas_call(expert_kernel, out_shape=tuple((jax.ShapeDtypeStruct(shape...  6.72 us
    pallas_call x2, Pallas kernels, weight_terms(): pl.pallas_call(pass_kernel if added is None else keep_kernel, in_specs=[V...  5.18 us
    ppermute x2, starting transfers between devices, swap(): return lax.ppermute(value, 'dp', [(i, i ^ bit) for i in range(4)])  4.91 us
    all_to_all x1, starting transfers between devices, scatter(): return lax.all_to_all(value, axis, split_axis=0, concat_axis=0, tiled=True)  4.26 us
  transfers between devices with their start and end apart: 9, of which 7 were waited for; matrix products, arithmetic and copies ran while one was open for 0% of the time, Pallas kernels for 4%

profile of v8, /device:TPU:2, one launch (start us, length us, event | category | flops | bytes accessed | tf_op | source)
XLA Modules:
  0.0 173.8 jit_solution(13300512394235310063)
XLA Ops:
  0.6 3.7 %shard_map.111 = bf16[256,1536]{1,0:T(8,128)(2,1)} custom-call(s32[1]{0:T(128)} %bitcast.me_ref, s32[1,256]{1,0:T(1,128)} %bitcast.17, s32[1,256]{1,0:T(1,128)} %bitcast.19, s32[1,256]{1,0:T(1,128)} %bitcast.21, bf16[256]{0:T(256)(128)(2,1)} %gate_ref.3, bf16[256,2048]{1,0:T(8,128)(2,1)} %tokens.1, bf16[256,2048]{1,0:T(8,128)(2,1)} %grad_out.1), custom_call_target="tpu_custom_call" | custom-call | flops 536870912 | bytes 2621440 | tf_op jit(solution)/shard_map/pallas_call | solution.py:94
  4.4 38.1 %all_to_all.15 = bf16[32,8,1536]{2,1,0:T(8,128)(2,1)S(1)} all-to-all(bf16[32,8,1536]{2,1,0:T(8,128)(2,1)} %bitcast.25), channel_id=1, replica_groups=mesh['expert'=32,'mp'=8,'dp'=4] {'expert'}, dimensions={0} | all-to-all | bytes 1572864 | tf_op jit(solution)/shard_map/all_to_all | solution.py:336
  42.5 0.0 copy-start.7
  42.5 0.1 fusion
  42.6 16.8 %collective-permute-start.1 = (bf16[256,1280]{1,0:T(8,128)(2,1)S(1)}, bf16[256,1280]{1,0:T(8,128)(2,1)S(1)}, u32[]{:S(2)}, u32[]{:S(2)}) collective-permute-start(bf16[256,1280]{1,0:T(8,128)(2,1)S(1)} %get-tuple-element.22), channel_id=1, source_target_pairs={{0,28},{4,0},{8,4},{12,8},{16,12},{20,16},{24,20},{28,24},{1,29},{... | collective-permute-start | bytes 1966088 | tf_op jit(solution)/shard_map/ppermute | solution.py:320
  59.3 1.9 %collective-permute-start = (bf16[256,1280]{1,0:T(8,128)(2,1)S(1)}, bf16[256,1280]{1,0:T(8,128)(2,1)S(1)}, u32[]{:S(2)}, u32[]{:S(2)}) collective-permute-start(bf16[256,1280]{1,0:T(8,128)(2,1)S(1)} %get-tuple-element.23), channel_id=1, source_target_pairs={{0,4},{4,8},{8,12},{12,16},{16,20},{20,24},{24,28},{28,0},{1,5},{5... | collective-permute-start | bytes 1966088 | tf_op jit(solution)/shard_map/ppermute | solution.py:320
  61.3 9.6 %collective-permute-done.1.after = bf16[256,1280]{1,0:T(8,128)(2,1)S(1)} collective-permute-done((bf16[256,1280]{1,0:T(8,128)(2,1)S(1)}, bf16[256,1280]{1,0:T(8,128)(2,1)S(1)}, u32[]{:S(2)}, u32[]{:S(2)}) %collective-permute-start.1) | collective-permute-done | bytes 655392 | tf_op jit(solution)/shard_map/ppermute | solution.py:320
  70.9 5.3 %collective-permute-done.before = bf16[256,1280]{1,0:T(8,128)(2,1)S(1)} collective-permute-done((bf16[256,1280]{1,0:T(8,128)(2,1)S(1)}, bf16[256,1280]{1,0:T(8,128)(2,1)S(1)}, u32[]{:S(2)}, u32[]{:S(2)}) %collective-permute-start) | collective-permute-done | bytes 655392 | tf_op jit(solution)/shard_map/ppermute | solution.py:320
  76.2 0.0 copy-done.7
  76.2 6.7 %shard_map.112 = (bf16[8,272,256]{2,1,0:T(8,128)(2,1)}, bf16[256,3328]{1,0:T(8,128)(2,1)}, bf16[256,2048]{1,0:T(8,128)(2,1)}) custom-call(s32[1]{0:T(128)} %bitcast.me_ref, s32[1]{0:T(128)} %bitcast.4.data_ref, bf16[256,1536]{1,0:T(8,128)(2,1)} %bitcast.24, bf16[256,1280]{1,0:T(8,128)(2,1)S(1)} %collective-permute-done.before, ...), custom_call_target="tpu_custom_call" | custom-call | flops 2013265920 | bytes 11534336 | tf_op jit(solution)/shard_map/pallas_call | solution.py:186
  82.9 0.0 copy-start
  83.0 2.1 %collective-permute-start.2 = (bf16[256,3328]{1,0:T(8,128)(2,1)}, bf16[256,3328]{1,0:T(8,128)(2,1)S(1)}, u32[]{:S(2)}, u32[]{:S(2)}) collective-permute-start(bf16[256,3328]{1,0:T(8,128)(2,1)} %get-tuple-element.15.acts_ref), channel_id=1, source_target_pairs={{0,1},{1,0},{2,3},{3,2},{4,5},{5,4},{6,7},{7,6},{8,9},{9,8},{10,11... | collective-permute-start | bytes 5111816 | tf_op jit(solution)/shard_map/ppermute | solution.py:324
  85.0 4.3 %all-to-all-start.1 = ((bf16[8,272,256]{2,1,0:T(8,128)(2,1)}), bf16[8,272,256]{2,1,0:T(8,128)(2,1)}, u32[]{:S(2)}, u32[]{:S(2)}) async-start(bf16[8,272,256]{2,1,0:T(8,128)(2,1)} %get-tuple-element.13), calls=%async_computation.1 | async-start | bytes 2228224 | tf_op jit(solution)/shard_map/all_to_all | solution.py:336
  89.3 0.0 collective-permute-done.2.other_ref
  89.3 0.0 copy-done
  89.3 0.0 copy-start.1
  89.3 1.2 copy-done.1
  90.5 2.1 %shard_map.114 = bf16[1024,640]{1,0:T(8,128)(2,1)} custom-call(bf16[256,2048]{1,0:T(8,128)(2,1)S(1)} %copy-done.1, bf16[256,3328]{1,0:T(8,128)(2,1)S(1)} %copy-done, bf16[256,3328]{1,0:T(8,128)(2,1)S(1)} %collective-permute-done.2.other_ref), custom_call_target="tpu_custom_call" | custom-call | flops 671088640 | bytes 3670016 | tf_op jit(solution)/shard_map/pallas_call | solution.py:309
  92.6 2.9 %collective-permute-start.3 = (bf16[1024,640]{1,0:T(8,128)(2,1)}, bf16[1024,640]{1,0:T(8,128)(2,1)}, u32[]{:S(2)}, u32[]{:S(2)}) collective-permute-start(bf16[1024,640]{1,0:T(8,128)(2,1)} %shard_map.114), channel_id=1, source_target_pairs={{0,2},{1,3},{2,0},{3,1},{4,6},{5,7},{6,4},{7,5},{8,10},{9,11},{10,... | collective-permute-start | bytes 3932168 | tf_op jit(solution)/shard_map/ppermute | solution.py:324
  95.5 24.9 %all-to-all-done.1.terms_ref = bf16[8,272,256]{2,1,0:T(8,128)(2,1)} async-done(((bf16[8,272,256]{2,1,0:T(8,128)(2,1)}), bf16[8,272,256]{2,1,0:T(8,128)(2,1)}, u32[]{:S(2)}, u32[]{:S(2)}) %all-to-all-start.1) | async-done | bytes 1114144 | tf_op jit(solution)/shard_map/all_to_all | solution.py:336
  120.4 0.0 copy-start.2
  120.4 1.6 shard_map.113
  122.1 20.9 %all_to_all.16 = bf16[32,8,384]{2,1,0:T(8,128)(2,1)S(1)} all-to-all(bf16[32,8,384]{2,1,0:T(8,128)(2,1)S(1)} %bitcast.16), channel_id=1, replica_groups=mesh['expert'=32,'mp'=8,'dp'=4] {'expert'}, dimensions={0} | all-to-all | bytes 393216 | tf_op jit(solution)/shard_map/all_to_all | solution.py:336
  143.0 0.0 collective-permute-done.3.added_ref
  143.0 2.2 %collective-permute-start.5 = (bf16[256,256]{1,0:T(8,128)(2,1)S(1)}, bf16[256,256]{1,0:T(8,128)(2,1)S(1)}, u32[]{:S(2)}, u32[]{:S(2)}) collective-permute-start(bf16[256,256]{1,0:T(8,128)(2,1)S(1)} %slice.18.refs_0_), channel_id=1, source_target_pairs={{0,24},{4,28},{8,0},{12,4},{16,8},{20,12},{24,16},{28,20},{1,25},{... | collective-permute-start | bytes 393224 | tf_op jit(solution)/shard_map/ppermute | solution.py:320
  145.3 4.1 %collective-permute-start.4 = (bf16[256,256]{1,0:T(8,128)(2,1)S(1)}, bf16[256,256]{1,0:T(8,128)(2,1)S(1)}, u32[]{:S(2)}, u32[]{:S(2)}) collective-permute-start(bf16[256,256]{1,0:T(8,128)(2,1)S(1)} %slice.18.refs_0_), channel_id=1, source_target_pairs={{0,12},{4,16},{8,20},{12,24},{16,28},{20,0},{24,4},{28,8},{1,13},{... | collective-permute-start | bytes 393224 | tf_op jit(solution)/shard_map/ppermute | solution.py:320
  149.4 2.7 %collective-permute-done.5.refs_2_ = bf16[256,256]{1,0:T(8,128)(2,1)S(1)} collective-permute-done((bf16[256,256]{1,0:T(8,128)(2,1)S(1)}, bf16[256,256]{1,0:T(8,128)(2,1)S(1)}, u32[]{:S(2)}, u32[]{:S(2)}) %collective-permute-start.5) | collective-permute-done | bytes 131104 | tf_op jit(solution)/shard_map/ppermute | solution.py:320
  152.1 5.5 %collective-permute-done.4.refs_1_ = bf16[256,256]{1,0:T(8,128)(2,1)S(1)} collective-permute-done((bf16[256,256]{1,0:T(8,128)(2,1)S(1)}, bf16[256,256]{1,0:T(8,128)(2,1)S(1)}, u32[]{:S(2)}, u32[]{:S(2)}) %collective-permute-start.4) | collective-permute-done | bytes 131104 | tf_op jit(solution)/shard_map/ppermute | solution.py:320
  157.6 2.5 %collective-permute-start.7 = (bf16[640,256]{1,0:T(8,128)(2,1)S(1)}, bf16[640,256]{1,0:T(8,128)(2,1)S(1)}, u32[]{:S(2)}, u32[]{:S(2)}) collective-permute-start(bf16[640,256]{1,0:T(8,128)(2,1)S(1)} %get-tuple-element.24), channel_id=1, source_target_pairs={{0,28},{4,0},{8,4},{12,8},{16,12},{20,16},{24,20},{28,24},{1,29},{... | collective-permute-start | bytes 983048 | tf_op jit(solution)/shard_map/ppermute | solution.py:320
  160.1 0.0 copy-start.3
  160.1 0.0 copy-start.4
  160.1 0.0 copy-start.5
  160.2 0.0 copy-start.6
  160.2 3.5 %collective-permute-start.6 = (bf16[640,256]{1,0:T(8,128)(2,1)S(1)}, bf16[640,256]{1,0:T(8,128)(2,1)S(1)}, u32[]{:S(2)}, u32[]{:S(2)}) collective-permute-start(bf16[640,256]{1,0:T(8,128)(2,1)S(1)} %get-tuple-element.25), channel_id=1, source_target_pairs={{0,4},{4,8},{8,12},{12,16},{16,20},{20,24},{24,28},{28,0},{1,5},{5... | collective-permute-start | bytes 983048 | tf_op jit(solution)/shard_map/ppermute | solution.py:320
  163.7 0.0 copy-done.2
  163.7 3.1 %shard_map.116 = (bf16[512,640]{1,0:T(8,128)(2,1)}, bf16[640,512]{1,0:T(8,128)(2,1)}) custom-call(bf16[256,2048]{1,0:T(8,128)(2,1)S(1)} %copy-done.2, bf16[256,3328]{1,0:T(8,128)(2,1)S(1)} %copy-done, bf16[256,3328]{1,0:T(8,128)(2,1)S(1)} %collective-permute-done.2.other_ref, bf16[1024,640]{1,0:T(8,128)(2,1)} %collective-permute-done.3.added_ref), custom_call_target="tpu_custom_call" | custom-call | flops 671088640 | bytes 3670016 | tf_op jit(solution)/shard_map/pallas_call | solution.py:309
  166.8 1.1 collective-permute-done.7.refs_4_
  167.9 4.4 %collective-permute-done.6.refs_3_ = bf16[640,256]{1,0:T(8,128)(2,1)S(1)} collective-permute-done((bf16[640,256]{1,0:T(8,128)(2,1)S(1)}, bf16[640,256]{1,0:T(8,128)(2,1)S(1)}, u32[]{:S(2)}, u32[]{:S(2)}) %collective-permute-start.6) | collective-permute-done | bytes 327712 | tf_op jit(solution)/shard_map/ppermute | solution.py:320
  172.2 0.0 copy-done.3
  172.2 0.0 copy-done.4
  172.2 0.0 copy-done.5
  172.3 0.0 copy-done.6
  172.3 1.5 shard_map.115
  (4 shorter events, 0.1 us)
Async XLA Ops:
  42.5 33.8 %copy-start.7 = (bf16[32,8,1536]{2,1,0:T(8,128)(2,1)}, bf16[32,8,1536]{2,1,0:T(8,128)(2,1)S(1)}, u32[]{:S(2)}) copy-start(bf16[32,8,1536]{2,1,0:T(8,128)(2,1)S(1)} %all_to_all.15) | copy-start | bytes 2359300
  42.6 28.3 %collective-permute-start.1 = (bf16[256,1280]{1,0:T(8,128)(2,1)S(1)}, bf16[256,1280]{1,0:T(8,128)(2,1)S(1)}, u32[]{:S(2)}, u32[]{:S(2)}) collective-permute-start(bf16[256,1280]{1,0:T(8,128)(2,1)S(1)} %get-tuple-element.22), channel_id=1, source_target_pairs={{0,28},{4,0},{8,4},{12,8},{16,12},{20,16},{24,20},{28,24},{1,29},{... | collective-permute-start | bytes 1966088 | tf_op jit(solution)/shard_map/ppermute | solution.py:320
  59.3 16.9 %collective-permute-start = (bf16[256,1280]{1,0:T(8,128)(2,1)S(1)}, bf16[256,1280]{1,0:T(8,128)(2,1)S(1)}, u32[]{:S(2)}, u32[]{:S(2)}) collective-permute-start(bf16[256,1280]{1,0:T(8,128)(2,1)S(1)} %get-tuple-element.23), channel_id=1, source_target_pairs={{0,4},{4,8},{8,12},{12,16},{16,20},{20,24},{24,28},{28,0},{1,5},{5... | collective-permute-start | bytes 1966088 | tf_op jit(solution)/shard_map/ppermute | solution.py:320
  82.9 6.4 %copy-start = (bf16[256,3328]{1,0:T(8,128)(2,1)S(1)}, bf16[256,3328]{1,0:T(8,128)(2,1)}, u32[]{:S(2)}) copy-start(bf16[256,3328]{1,0:T(8,128)(2,1)} %get-tuple-element.15.acts_ref) | copy-start | bytes 5111812
  83.0 6.3 %collective-permute-start.2 = (bf16[256,3328]{1,0:T(8,128)(2,1)}, bf16[256,3328]{1,0:T(8,128)(2,1)S(1)}, u32[]{:S(2)}, u32[]{:S(2)}) collective-permute-start(bf16[256,3328]{1,0:T(8,128)(2,1)} %get-tuple-element.15.acts_ref), channel_id=1, source_target_pairs={{0,1},{1,0},{2,3},{3,2},{4,5},{5,4},{6,7},{7,6},{8,9},{9,8},{10,11... | collective-permute-start | bytes 5111816 | tf_op jit(solution)/shard_map/ppermute | solution.py:324
  85.0 35.4 %all-to-all-start.1 = ((bf16[8,272,256]{2,1,0:T(8,128)(2,1)}), bf16[8,272,256]{2,1,0:T(8,128)(2,1)}, u32[]{:S(2)}, u32[]{:S(2)}) async-start(bf16[8,272,256]{2,1,0:T(8,128)(2,1)} %get-tuple-element.13), calls=%async_computation.1 | async-start | bytes 2228224 | tf_op jit(solution)/shard_map/all_to_all | solution.py:336
  89.3 1.2 copy-start.1
  92.6 50.4 %collective-permute-start.3 = (bf16[1024,640]{1,0:T(8,128)(2,1)}, bf16[1024,640]{1,0:T(8,128)(2,1)}, u32[]{:S(2)}, u32[]{:S(2)}) collective-permute-start(bf16[1024,640]{1,0:T(8,128)(2,1)} %shard_map.114), channel_id=1, source_target_pairs={{0,2},{1,3},{2,0},{3,1},{4,6},{5,7},{6,4},{7,5},{8,10},{9,11},{10,... | collective-permute-start | bytes 3932168 | tf_op jit(solution)/shard_map/ppermute | solution.py:324
  120.4 43.3 %copy-start.2 = (bf16[256,2048]{1,0:T(8,128)(2,1)S(1)}, bf16[256,2048]{1,0:T(8,128)(2,1)}, u32[]{:S(2)}) copy-start(bf16[256,2048]{1,0:T(8,128)(2,1)} %get-tuple-element.14.mine_ref) | copy-start | bytes 3145732
  143.0 9.1 %collective-permute-start.5 = (bf16[256,256]{1,0:T(8,128)(2,1)S(1)}, bf16[256,256]{1,0:T(8,128)(2,1)S(1)}, u32[]{:S(2)}, u32[]{:S(2)}) collective-permute-start(bf16[256,256]{1,0:T(8,128)(2,1)S(1)} %slice.18.refs_0_), channel_id=1, source_target_pairs={{0,24},{4,28},{8,0},{12,4},{16,8},{20,12},{24,16},{28,20},{1,25},{... | collective-permute-start | bytes 393224 | tf_op jit(solution)/shard_map/ppermute | solution.py:320
  145.3 12.3 %collective-permute-start.4 = (bf16[256,256]{1,0:T(8,128)(2,1)S(1)}, bf16[256,256]{1,0:T(8,128)(2,1)S(1)}, u32[]{:S(2)}, u32[]{:S(2)}) collective-permute-start(bf16[256,256]{1,0:T(8,128)(2,1)S(1)} %slice.18.refs_0_), channel_id=1, source_target_pairs={{0,12},{4,16},{8,20},{12,24},{16,28},{20,0},{24,4},{28,8},{1,13},{... | collective-permute-start | bytes 393224 | tf_op jit(solution)/shard_map/ppermute | solution.py:320
  157.6 10.2 %collective-permute-start.7 = (bf16[640,256]{1,0:T(8,128)(2,1)S(1)}, bf16[640,256]{1,0:T(8,128)(2,1)S(1)}, u32[]{:S(2)}, u32[]{:S(2)}) collective-permute-start(bf16[640,256]{1,0:T(8,128)(2,1)S(1)} %get-tuple-element.24), channel_id=1, source_target_pairs={{0,28},{4,0},{8,4},{12,8},{16,12},{20,16},{24,20},{28,24},{1,29},{... | collective-permute-start | bytes 983048 | tf_op jit(solution)/shard_map/ppermute | solution.py:320
  160.1 12.1 %copy-start.3 = (s32[256]{0:T(256)S(1)}, s32[256]{0:T(256)}, u32[]{:S(2)}) copy-start(s32[256]{0:T(256)} %param.11) | copy-start | bytes 3076
  160.1 12.1 %copy-start.4 = (s32[256]{0:T(256)S(1)}, s32[256]{0:T(256)}, u32[]{:S(2)}) copy-start(s32[256]{0:T(256)} %param.12) | copy-start | bytes 3076
  160.1 12.1 %copy-start.5 = (s32[256]{0:T(256)S(1)}, s32[256]{0:T(256)}, u32[]{:S(2)}) copy-start(s32[256]{0:T(256)} %param.13) | copy-start | bytes 3076
  160.2 12.1 %copy-start.6 = (bf16[256]{0:T(256)(128)(2,1)S(1)}, bf16[256]{0:T(256)(128)(2,1)}, u32[]{:S(2)}) copy-start(bf16[256]{0:T(256)(128)(2,1)} %gate_ref.3) | copy-start | bytes 1540
  160.2 12.1 %collective-permute-start.6 = (bf16[640,256]{1,0:T(8,128)(2,1)S(1)}, bf16[640,256]{1,0:T(8,128)(2,1)S(1)}, u32[]{:S(2)}, u32[]{:S(2)}) collective-permute-start(bf16[640,256]{1,0:T(8,128)(2,1)S(1)} %get-tuple-element.25), channel_id=1, source_target_pairs={{0,4},{4,8},{8,12},{12,16},{16,20},{20,24},{24,28},{28,0},{1,5},{5... | collective-permute-start | bytes 983048 | tf_op jit(solution)/shard_map/ppermute | solution.py:320
